TPU v7x, 512 devices: a whole 4x4x16 slice. The times are simulated.
512 devices in a mesh: ctx: 16 (over z), beam: 32 (over y, x, core).
Axes of the slice: x: 4, y: 4, z: 16, core: 2. Of those that a mesh axis runs over, the one named last changes fastest.
Arguments:
- queries: bfloat16 [512, 64, 128], P('beam', 'ctx'), may hold values from -20 to 20
- prompt_kv: bfloat16 [2, 16384, 8, 128], P(None, 'ctx'), may hold values from -16 to 16
- suffix_kv: bfloat16 [2, 512, 64, 8, 128], P(None, 'beam', 'ctx'), may hold values from -9 to 9
- new_kv: bfloat16 [2, 512, 8, 128], P(None, 'beam'), may hold values from -11 to 11
- parents: int32 [512], P('beam'), may hold values from 0 to 511, as said below
- lengths: int32 [512], P('beam'), may hold values from 1 to 64, as said below
- token_ids: int32 [512], P('beam'), may hold values from 0 to 128255
- group_ids: int32 [512], P('beam'), may hold values from 0 to 7
Outputs:
- attended: bfloat16 [512, 64, 128], P('beam', 'ctx')
- penalty: float32 [512], P('beam')
Inputs may be any that keep to these rules, and one draw needn't show every extreme that they name: parents[b] lies in the same aligned block of 64 beams as b. `lengths`: some beam has exactly 64 live suffix positions and some exactly 1.
All inputs are finite; a program needn't handle non-finite values.
Results may differ from a plain program's by a relative error of at most 0.014.
Values may be sent and summed in bfloat16 or wider, within the bound.
No kernel may reach another device: no remote copies, remote signals or barrier semaphores. Data moves between devices by JAX's collectives and lax.ppermute only.
A program may use at most 64 MiB of HBM per device.

v0:
```python
import jax
import jax.numpy as jnp
from jax import lax
from jax.sharding import PartitionSpec as P

HEADS = 64
KVH = 8


PENALTY_WEIGHT = 0.5
FAR_BELOW = -1e30


def swapped(block, axis, stride):
    count = lax.axis_size(axis)
    route = []
    for low in range(count):
        high = low | 1 << stride
        if high != low and high < count:
            route += [(low, high), (high, low)]
    return lax.ppermute(block, axis, route)


def from_behind(block, axis, distance):
    devices = range(lax.axis_size(axis))
    route = [((i - distance) % len(devices), i) for i in devices]
    return lax.ppermute(block, axis, route)


def attend_partially(query_group, prompt_part, suffix_part, live_mask, score_scale):
    prompt_scores = (
        jnp.einsum(
            "bkgd,pkd->bkgp", query_group, prompt_part[0], preferred_element_type=jnp.float32
        )
        * score_scale
    )
    suffix_scores = (
        jnp.einsum(
            "bkgd,bskd->bkgs", query_group, suffix_part[0], preferred_element_type=jnp.float32
        )
        * score_scale
    )
    suffix_scores = jnp.where(live_mask[:, None, None, :], suffix_scores, -jnp.inf)
    highest = jnp.maximum(jnp.max(prompt_scores, axis=3), jnp.max(suffix_scores, axis=3))
    prompt_weights = jnp.exp(prompt_scores - highest[..., None])
    suffix_weights = jnp.exp(suffix_scores - highest[..., None])
    running_totals = jnp.sum(prompt_weights, axis=3) + jnp.sum(suffix_weights, axis=3)
    mixed = jnp.einsum(
        "bkgp,pkd->bkgd",
        prompt_weights.astype(jnp.bfloat16),
        prompt_part[1],
        preferred_element_type=jnp.float32,
    )
    mixed = mixed + jnp.einsum(
        "bkgs,bskd->bkgd",
        suffix_weights.astype(jnp.bfloat16),
        suffix_part[1],
        preferred_element_type=jnp.float32,
    )
    return (mixed, highest, running_totals)


def combine_parts(former, latter):
    ceiling = jnp.maximum(former[1], latter[1])
    old_factor = jnp.exp(former[1] - ceiling)
    new_factor = jnp.exp(latter[1] - ceiling)
    mixed = former[0] * old_factor[..., None] + latter[0] * new_factor[..., None]
    return (mixed, ceiling, former[2] * old_factor + latter[2] * new_factor)


def body(queries, prompt_kv, suffix_kv, new_kv, parents, lengths, token_ids, group_ids):
    beam_dev = queries.shape[0]
    heads_dev = queries.shape[1]
    head_dim = queries.shape[2]
    suffix_dev = suffix_kv.shape[2]
    group_size = HEADS // KVH
    kv_count = max(1, heads_dev // group_size)
    per_kv = heads_dev // kv_count
    score_scale = head_dim ** (-0.5)
    ctx_count = lax.axis_size("ctx")
    ctx_rank = lax.axis_index("ctx")
    beam_rank = lax.axis_index("beam")
    positions = ctx_rank * suffix_dev + jnp.arange(suffix_dev, dtype=jnp.int32)
    live_mask = positions[None, :] < lengths[:, None]
    reordered = None
    held = suffix_kv
    for bit_number in range(2):
        partner = swapped(held, "beam", bit_number)
        lower_half = beam_rank // 2**bit_number % 2 == 0
        held = jnp.where(
            lower_half,
            jnp.concatenate((held, partner), axis=1),
            jnp.concatenate((partner, held), axis=1),
        )
    numbers = beam_rank // 4 * 4 * beam_dev + jnp.arange(held.shape[1], dtype=jnp.int32)
    onehot = (parents[:, None] == numbers[None, :]).astype(jnp.bfloat16)
    picked = jnp.einsum("bj,cjskd->cbskd", onehot, held, preferred_element_type=jnp.float32)
    reordered = picked.astype(jnp.bfloat16)

    def cycle_turn(turn, carry):
        visitor = carry[0]
        reference_point = (ctx_rank - turn) % ctx_count
        kv_first = reference_point * heads_dev // group_size
        prompt_part = lax.dynamic_slice_in_dim(prompt_kv, kv_first, kv_count, 2)
        suffix_part = lax.dynamic_slice_in_dim(reordered, kv_first, kv_count, 3)
        query_group = visitor.astype(jnp.bfloat16).reshape(beam_dev, kv_count, per_kv, head_dim)
        fresh = attend_partially(query_group, prompt_part, suffix_part, live_mask, score_scale)
        merged = combine_parts(carry[1:], fresh)
        return from_behind((visitor, merged[0], merged[1], merged[2]), "ctx", 1)

    initial_carry = (
        queries.astype(jnp.float32),
        jnp.zeros((beam_dev, kv_count, per_kv, head_dim), jnp.float32),
        jnp.full((beam_dev, kv_count, per_kv), FAR_BELOW, jnp.float32),
        jnp.zeros((beam_dev, kv_count, per_kv), jnp.float32),
    )
    final_carry = lax.fori_loop(0, ctx_count, cycle_turn, initial_carry)
    mixed, highest, running_totals = (final_carry[1], final_carry[2], final_carry[3])
    kv_home = ctx_rank * heads_dev // group_size
    local_portion = lax.dynamic_slice_in_dim(new_kv, kv_home, kv_count, 2)
    resident_group = queries.reshape(beam_dev, kv_count, per_kv, head_dim)
    own_scores = (
        jnp.einsum(
            "whzu,whu->whz", resident_group, local_portion[0], preferred_element_type=jnp.float32
        )
        * score_scale
    )
    ceiling = jnp.maximum(highest, own_scores)
    old_factor = jnp.exp(highest - ceiling)
    own_weights = jnp.exp(own_scores - ceiling)
    mixed = mixed * old_factor[..., None] + jnp.einsum(
        "nco,ncm->ncom",
        own_weights.astype(jnp.bfloat16),
        local_portion[1],
        preferred_element_type=jnp.float32,
    )
    running_totals = running_totals * old_factor + own_weights
    attended = (
        (mixed / running_totals[..., None])
        .reshape(beam_dev, heads_dev, head_dim)
        .astype(jnp.bfloat16)
    )
    all_tokens, all_groups = (
        lax.all_gather(token_ids, "beam", axis=0, tiled=True),
        lax.all_gather(group_ids, "beam", axis=0, tiled=True),
    )
    earlier = (all_groups[None, :] < group_ids[:, None]) & (
        all_tokens[None, :] == token_ids[:, None]
    )
    penalty = PENALTY_WEIGHT * jnp.sum(earlier.astype(jnp.float32), axis=1)
    return (attended, penalty)


def solution(mesh):
    in_specs = (
        P("beam", "ctx", None),
        P(None, "ctx", None, None),
        P(None, "beam", "ctx", None, None),
        P(None, "beam", None, None),
        P("beam"),
        P("beam"),
        P("beam"),
        P("beam"),
    )
    out_specs = (P("beam", "ctx", None), P("beam"))
    return jax.shard_map(body, mesh=mesh, in_specs=in_specs, out_specs=out_specs, check_vma=False)
```

profile of v0, /device:TPU:2, one launch (start us, length us, event | category | flops | bytes accessed | tf_op | source)
XLA Modules:
  0.0 345.2 jit_solution(15509896668519599816)
XLA Ops:
  4.3 4.9 %copy.68 = bf16[2,1024,8,128]{3,1,2,0:T(8,128)(2,1)} copy(bf16[2,1024,8,128]{3,2,1,0:T(8,128)(2,1)} %param.11) | data formatting | bytes 8388608
  11.7 15.7 %all-reduce.2 = (s32[512]{0:T(512)S(1)}, s32[512]{0:T(512)S(1)}) all-reduce(s32[512]{0:T(512)S(1)} %dynamic-update-slice.1, s32[512]{0:T(512)S(1)} %dynamic-update-slice), channel_id=1, replica_groups=mesh['ctx'=16,'beam'=32] {'beam'}, use_global_device_ids=true, to_apply=%add.1 | all-reduce | flops 1024 | bytes 8192
  27.6 3.7 %collective-permute-start.5 = (bf16[2,32,4,8,128]{4,3,2,1,0:T(8,128)(2,1)S(1)}, bf16[2,32,4,8,128]{4,3,2,1,0:T(8,128)(2,1)S(1)}, u32[]{:S(2)}, u32[]{:S(2)}) collective-permute-start(bf16[2,32,4,8,128]{4,3,2,1,0:T(8,128)(2,1)S(1)} %maximum_select_fusion.1), channel_id=1, source_target_pairs={{0,2},{2,0},{1,3},{3,1},{4,6},{6,4},{5,7},{7,5},{8,10},{10,8},{9,1... | collective-permute-start | bytes 1572872 | tf_op jit(solution)/shard_map/ppermute | solution.py:21
  31.8 8.6 %collective-permute-done.5 = bf16[2,32,4,8,128]{4,3,2,1,0:T(8,128)(2,1)S(1)} collective-permute-done((bf16[2,32,4,8,128]{4,3,2,1,0:T(8,128)(2,1)S(1)}, bf16[2,32,4,8,128]{4,3,2,1,0:T(8,128)(2,1)S(1)}, u32[]{:S(2)}, u32[]{:S(2)}) %collective-permute-start.5) | collective-permute-done | bytes 524320 | tf_op jit(solution)/shard_map/ppermute | solution.py:21
  41.0 303.1 %while.22 = (s32[]{:T(128)}, bf16[16,4,128]{2,1,0:T(4,128)(2,1)S(1)}, f32[16,1,4,128]{3,0,2,1:T(8,128)S(1)}, f32[16,1,4]{0,2,1:T(4,128)S(1)}, f32[16,1,4]{0,2,1:...) while((s32[]{:T(128)}, ...), condition=%wide.region_5.6_spmd.clone, body=%wide.region_0.5_spmd.clone.sunk | while | flops 34113696 | bytes 1815682 | solution.py:117
  44.5 3.8 %collective-permute-start.1 = (f32[16,1,4,128]{3,0,2,1:T(8,128)S(1)}, f32[16,1,4,128]{3,0,2,1:T(8,128)S(1)}, u32[]{:S(2)}, u32[]{:S(2)}) collective-permute-start(f32[16,1,4,128]{3,0,2,1:T(8,128)S(1)} %fusion.63), channel_id=1, source_target_pairs={{480,0},{0,32},{32,64},{64,96},{96,128},{128,160},{160,192},{192,2... | collective-permute-start | bytes 98312 | tf_op jit(solution)/shard_map/while/body/eval_jaxpr/ppermute | solution.py:27
  48.4 3.8 %collective-permute-start = (bf16[16,4,128]{2,1,0:T(4,128)(2,1)S(1)}, bf16[16,4,128]{2,1,0:T(4,128)(2,1)S(1)}, u32[]{:S(2)}, u32[]{:S(2)}) collective-permute-start(bf16[16,4,128]{2,1,0:T(4,128)(2,1)S(1)} %copy.132), channel_id=1, source_target_pairs={{480,0},{0,32},{32,64},{64,96},{96,128},{128,160},{160,192},{192,2... | collective-permute-start | bytes 49160 | tf_op jit(solution)/shard_map/while/body/eval_jaxpr/ppermute | solution.py:27
  52.2 3.8 %collective-permute-start.2 = (f32[16,1,4]{0,2,1:T(4,128)S(1)}, f32[16,1,4]{0,2,1:T(4,128)S(1)}, u32[]{:S(2)}, u32[]{:S(2)}) collective-permute-start(f32[16,1,4]{0,2,1:T(4,128)S(1)} %get-tuple-element.423), channel_id=1, source_target_pairs={{480,0},{0,32},{32,64},{64,96},{96,128},{128,160},{160,192},{192,2... | collective-permute-start | bytes 776 | tf_op jit(solution)/shard_map/while/body/eval_jaxpr/ppermute | solution.py:27
  56.0 5.0 %collective-permute-start.3 = (f32[16,1,4]{0,2,1:T(4,128)S(1)}, f32[16,1,4]{0,2,1:T(4,128)S(1)}, u32[]{:S(2)}, u32[]{:S(2)}) collective-permute-start(f32[16,1,4]{0,2,1:T(4,128)S(1)} %get-tuple-element.424), channel_id=1, source_target_pairs={{480,0},{0,32},{32,64},{64,96},{96,128},{128,160},{160,192},{192,2... | collective-permute-start | bytes 776 | tf_op jit(solution)/shard_map/while/body/eval_jaxpr/ppermute | solution.py:27
  66.7 3.3 collective-permute-start.1
  70.0 3.8 %collective-permute-start = (bf16[16,4,128]{2,1,0:T(4,128)(2,1)S(1)}, bf16[16,4,128]{2,1,0:T(4,128)(2,1)S(1)}, u32[]{:S(2)}, u32[]{:S(2)}) collective-permute-start(bf16[16,4,128]{2,1,0:T(4,128)(2,1)S(1)} %copy.132), channel_id=1, source_target_pairs={{480,0},{0,32},{32,64},{64,96},{96,128},{128,160},{160,192},{192,2... | collective-permute-start | bytes 49160 | tf_op jit(solution)/shard_map/while/body/eval_jaxpr/ppermute | solution.py:27
  73.8 3.8 %collective-permute-start.2 = (f32[16,1,4]{0,2,1:T(4,128)S(1)}, f32[16,1,4]{0,2,1:T(4,128)S(1)}, u32[]{:S(2)}, u32[]{:S(2)}) collective-permute-start(f32[16,1,4]{0,2,1:T(4,128)S(1)} %get-tuple-element.423), channel_id=1, source_target_pairs={{480,0},{0,32},{32,64},{64,96},{96,128},{128,160},{160,192},{192,2... | collective-permute-start | bytes 776 | tf_op jit(solution)/shard_map/while/body/eval_jaxpr/ppermute | solution.py:27
  77.7 5.1 %collective-permute-start.3 = (f32[16,1,4]{0,2,1:T(4,128)S(1)}, f32[16,1,4]{0,2,1:T(4,128)S(1)}, u32[]{:S(2)}, u32[]{:S(2)}) collective-permute-start(f32[16,1,4]{0,2,1:T(4,128)S(1)} %get-tuple-element.424), channel_id=1, source_target_pairs={{480,0},{0,32},{32,64},{64,96},{96,128},{128,160},{160,192},{192,2... | collective-permute-start | bytes 776 | tf_op jit(solution)/shard_map/while/body/eval_jaxpr/ppermute | solution.py:27
  87.8 3.8 %collective-permute-start.1 = (f32[16,1,4,128]{3,0,2,1:T(8,128)S(1)}, f32[16,1,4,128]{3,0,2,1:T(8,128)S(1)}, u32[]{:S(2)}, u32[]{:S(2)}) collective-permute-start(f32[16,1,4,128]{3,0,2,1:T(8,128)S(1)} %fusion.63), channel_id=1, source_target_pairs={{480,0},{0,32},{32,64},{64,96},{96,128},{128,160},{160,192},{192,2... | collective-permute-start | bytes 98312 | tf_op jit(solution)/shard_map/while/body/eval_jaxpr/ppermute | solution.py:27
  91.7 3.8 %collective-permute-start = (bf16[16,4,128]{2,1,0:T(4,128)(2,1)S(1)}, bf16[16,4,128]{2,1,0:T(4,128)(2,1)S(1)}, u32[]{:S(2)}, u32[]{:S(2)}) collective-permute-start(bf16[16,4,128]{2,1,0:T(4,128)(2,1)S(1)} %copy.132), channel_id=1, source_target_pairs={{480,0},{0,32},{32,64},{64,96},{96,128},{128,160},{160,192},{192,2... | collective-permute-start | bytes 49160 | tf_op jit(solution)/shard_map/while/body/eval_jaxpr/ppermute | solution.py:27
  98.4 4.1 %collective-permute-start.3 = (f32[16,1,4]{0,2,1:T(4,128)S(1)}, f32[16,1,4]{0,2,1:T(4,128)S(1)}, u32[]{:S(2)}, u32[]{:S(2)}) collective-permute-start(f32[16,1,4]{0,2,1:T(4,128)S(1)} %get-tuple-element.424), channel_id=1, source_target_pairs={{480,0},{0,32},{32,64},{64,96},{96,128},{128,160},{160,192},{192,2... | collective-permute-start | bytes 776 | tf_op jit(solution)/shard_map/while/body/eval_jaxpr/ppermute | solution.py:27
  108.5 2.9 collective-permute-start.1
  111.5 2.9 collective-permute-start
  116.3 3.9 %collective-permute-start.3 = (f32[16,1,4]{0,2,1:T(4,128)S(1)}, f32[16,1,4]{0,2,1:T(4,128)S(1)}, u32[]{:S(2)}, u32[]{:S(2)}) collective-permute-start(f32[16,1,4]{0,2,1:T(4,128)S(1)} %get-tuple-element.424), channel_id=1, source_target_pairs={{480,0},{0,32},{32,64},{64,96},{96,128},{128,160},{160,192},{192,2... | collective-permute-start | bytes 776 | tf_op jit(solution)/shard_map/while/body/eval_jaxpr/ppermute | solution.py:27
  129.2 2.9 collective-permute-start
  132.1 2.9 collective-permute-start.2
  135.1 3.1 collective-permute-start.3
  138.8 2.9 collective-permute-done.3
  151.0 3.1 collective-permute-start.3
  165.1 3.8 %collective-permute-start.2 = (f32[16,1,4]{0,2,1:T(4,128)S(1)}, f32[16,1,4]{0,2,1:T(4,128)S(1)}, u32[]{:S(2)}, u32[]{:S(2)}) collective-permute-start(f32[16,1,4]{0,2,1:T(4,128)S(1)} %get-tuple-element.423), channel_id=1, source_target_pairs={{480,0},{0,32},{32,64},{64,96},{96,128},{128,160},{160,192},{192,2... | collective-permute-start | bytes 776 | tf_op jit(solution)/shard_map/while/body/eval_jaxpr/ppermute | solution.py:27
  169.0 5.0 %collective-permute-start.3 = (f32[16,1,4]{0,2,1:T(4,128)S(1)}, f32[16,1,4]{0,2,1:T(4,128)S(1)}, u32[]{:S(2)}, u32[]{:S(2)}) collective-permute-start(f32[16,1,4]{0,2,1:T(4,128)S(1)} %get-tuple-element.424), channel_id=1, source_target_pairs={{480,0},{0,32},{32,64},{64,96},{96,128},{128,160},{160,192},{192,2... | collective-permute-start | bytes 776 | tf_op jit(solution)/shard_map/while/body/eval_jaxpr/ppermute | solution.py:27
  179.1 3.8 %collective-permute-start.1 = (f32[16,1,4,128]{3,0,2,1:T(8,128)S(1)}, f32[16,1,4,128]{3,0,2,1:T(8,128)S(1)}, u32[]{:S(2)}, u32[]{:S(2)}) collective-permute-start(f32[16,1,4,128]{3,0,2,1:T(8,128)S(1)} %fusion.63), channel_id=1, source_target_pairs={{480,0},{0,32},{32,64},{64,96},{96,128},{128,160},{160,192},{192,2... | collective-permute-start | bytes 98312 | tf_op jit(solution)/shard_map/while/body/eval_jaxpr/ppermute | solution.py:27
  182.9 3.8 %collective-permute-start = (bf16[16,4,128]{2,1,0:T(4,128)(2,1)S(1)}, bf16[16,4,128]{2,1,0:T(4,128)(2,1)S(1)}, u32[]{:S(2)}, u32[]{:S(2)}) collective-permute-start(bf16[16,4,128]{2,1,0:T(4,128)(2,1)S(1)} %copy.132), channel_id=1, source_target_pairs={{480,0},{0,32},{32,64},{64,96},{96,128},{128,160},{160,192},{192,2... | collective-permute-start | bytes 49160 | tf_op jit(solution)/shard_map/while/body/eval_jaxpr/ppermute | solution.py:27
  186.8 3.8 %collective-permute-start.2 = (f32[16,1,4]{0,2,1:T(4,128)S(1)}, f32[16,1,4]{0,2,1:T(4,128)S(1)}, u32[]{:S(2)}, u32[]{:S(2)}) collective-permute-start(f32[16,1,4]{0,2,1:T(4,128)S(1)} %get-tuple-element.423), channel_id=1, source_target_pairs={{480,0},{0,32},{32,64},{64,96},{96,128},{128,160},{160,192},{192,2... | collective-permute-start | bytes 776 | tf_op jit(solution)/shard_map/while/body/eval_jaxpr/ppermute | solution.py:27
  190.6 4.1 %collective-permute-start.3 = (f32[16,1,4]{0,2,1:T(4,128)S(1)}, f32[16,1,4]{0,2,1:T(4,128)S(1)}, u32[]{:S(2)}, u32[]{:S(2)}) collective-permute-start(f32[16,1,4]{0,2,1:T(4,128)S(1)} %get-tuple-element.424), channel_id=1, source_target_pairs={{480,0},{0,32},{32,64},{64,96},{96,128},{128,160},{160,192},{192,2... | collective-permute-start | bytes 776 | tf_op jit(solution)/shard_map/while/body/eval_jaxpr/ppermute | solution.py:27
  203.7 2.9 collective-permute-start
  209.6 3.1 collective-permute-start.3
  213.3 2.9 collective-permute-done.3
  227.3 4.1 %collective-permute-start.3 = (f32[16,1,4]{0,2,1:T(4,128)S(1)}, f32[16,1,4]{0,2,1:T(4,128)S(1)}, u32[]{:S(2)}, u32[]{:S(2)}) collective-permute-start(f32[16,1,4]{0,2,1:T(4,128)S(1)} %get-tuple-element.424), channel_id=1, source_target_pairs={{480,0},{0,32},{32,64},{64,96},{96,128},{128,160},{160,192},{192,2... | collective-permute-start | bytes 776 | tf_op jit(solution)/shard_map/while/body/eval_jaxpr/ppermute | solution.py:27
  237.4 2.9 collective-permute-start.1
  244.2 3.1 collective-permute-start.3
  260.3 5.0 %collective-permute-start.3 = (f32[16,1,4]{0,2,1:T(4,128)S(1)}, f32[16,1,4]{0,2,1:T(4,128)S(1)}, u32[]{:S(2)}, u32[]{:S(2)}) collective-permute-start(f32[16,1,4]{0,2,1:T(4,128)S(1)} %get-tuple-element.424), channel_id=1, source_target_pairs={{480,0},{0,32},{32,64},{64,96},{96,128},{128,160},{160,192},{192,2... | collective-permute-start | bytes 776 | tf_op jit(solution)/shard_map/while/body/eval_jaxpr/ppermute | solution.py:27
  270.4 3.8 %collective-permute-start.1 = (f32[16,1,4,128]{3,0,2,1:T(8,128)S(1)}, f32[16,1,4,128]{3,0,2,1:T(8,128)S(1)}, u32[]{:S(2)}, u32[]{:S(2)}) collective-permute-start(f32[16,1,4,128]{3,0,2,1:T(8,128)S(1)} %fusion.63), channel_id=1, source_target_pairs={{480,0},{0,32},{32,64},{64,96},{96,128},{128,160},{160,192},{192,2... | collective-permute-start | bytes 98312 | tf_op jit(solution)/shard_map/while/body/eval_jaxpr/ppermute | solution.py:27
  274.3 3.8 %collective-permute-start = (bf16[16,4,128]{2,1,0:T(4,128)(2,1)S(1)}, bf16[16,4,128]{2,1,0:T(4,128)(2,1)S(1)}, u32[]{:S(2)}, u32[]{:S(2)}) collective-permute-start(bf16[16,4,128]{2,1,0:T(4,128)(2,1)S(1)} %copy.132), channel_id=1, source_target_pairs={{480,0},{0,32},{32,64},{64,96},{96,128},{128,160},{160,192},{192,2... | collective-permute-start | bytes 49160 | tf_op jit(solution)/shard_map/while/body/eval_jaxpr/ppermute | solution.py:27
  278.1 3.8 %collective-permute-start.2 = (f32[16,1,4]{0,2,1:T(4,128)S(1)}, f32[16,1,4]{0,2,1:T(4,128)S(1)}, u32[]{:S(2)}, u32[]{:S(2)}) collective-permute-start(f32[16,1,4]{0,2,1:T(4,128)S(1)} %get-tuple-element.423), channel_id=1, source_target_pairs={{480,0},{0,32},{32,64},{64,96},{96,128},{128,160},{160,192},{192,2... | collective-permute-start | bytes 776 | tf_op jit(solution)/shard_map/while/body/eval_jaxpr/ppermute | solution.py:27
  281.9 5.0 %collective-permute-start.3 = (f32[16,1,4]{0,2,1:T(4,128)S(1)}, f32[16,1,4]{0,2,1:T(4,128)S(1)}, u32[]{:S(2)}, u32[]{:S(2)}) collective-permute-start(f32[16,1,4]{0,2,1:T(4,128)S(1)} %get-tuple-element.424), channel_id=1, source_target_pairs={{480,0},{0,32},{32,64},{64,96},{96,128},{128,160},{160,192},{192,2... | collective-permute-start | bytes 776 | tf_op jit(solution)/shard_map/while/body/eval_jaxpr/ppermute | solution.py:27
  292.1 3.8 %collective-permute-start.1 = (f32[16,1,4,128]{3,0,2,1:T(8,128)S(1)}, f32[16,1,4,128]{3,0,2,1:T(8,128)S(1)}, u32[]{:S(2)}, u32[]{:S(2)}) collective-permute-start(f32[16,1,4,128]{3,0,2,1:T(8,128)S(1)} %fusion.63), channel_id=1, source_target_pairs={{480,0},{0,32},{32,64},{64,96},{96,128},{128,160},{160,192},{192,2... | collective-permute-start | bytes 98312 | tf_op jit(solution)/shard_map/while/body/eval_jaxpr/ppermute | solution.py:27
  295.9 2.9 collective-permute-start
  301.8 4.1 %collective-permute-start.3 = (f32[16,1,4]{0,2,1:T(4,128)S(1)}, f32[16,1,4]{0,2,1:T(4,128)S(1)}, u32[]{:S(2)}, u32[]{:S(2)}) collective-permute-start(f32[16,1,4]{0,2,1:T(4,128)S(1)} %get-tuple-element.424), channel_id=1, source_target_pairs={{480,0},{0,32},{32,64},{64,96},{96,128},{128,160},{160,192},{192,2... | collective-permute-start | bytes 776 | tf_op jit(solution)/shard_map/while/body/eval_jaxpr/ppermute | solution.py:27
  311.9 2.9 collective-permute-start.1
  319.5 4.1 %collective-permute-start.3 = (f32[16,1,4]{0,2,1:T(4,128)S(1)}, f32[16,1,4]{0,2,1:T(4,128)S(1)}, u32[]{:S(2)}, u32[]{:S(2)}) collective-permute-start(f32[16,1,4]{0,2,1:T(4,128)S(1)} %get-tuple-element.424), channel_id=1, source_target_pairs={{480,0},{0,32},{32,64},{64,96},{96,128},{128,160},{160,192},{192,2... | collective-permute-start | bytes 776 | tf_op jit(solution)/shard_map/while/body/eval_jaxpr/ppermute | solution.py:27
  332.6 3.0 collective-permute-start
  337.5 3.1 collective-permute-start.3
  (347 shorter events, 151.0 us)
Async XLA Ops:
  1.3 26.2 %collective-permute-start.4 = (bf16[2,16,4,8,128]{4,3,2,1,0:T(8,128)(2,1)}, bf16[2,16,4,8,128]{4,3,2,1,0:T(8,128)(2,1)S(1)}, u32[]{:S(2)}, u32[]{:S(2)}) collective-permute-start(bf16[2,16,4,8,128]{4,3,2,1,0:T(8,128)(2,1)} %param.12), channel_id=1, source_target_pairs={{0,1},{1,0},{2,3},{3,2},{4,5},{5,4},{6,7},{7,6},{8,9},{9,8},{10,11... | collective-permute-start | bytes 786440 | tf_op jit(solution)/shard_map/ppermute | solution.py:21
  27.6 12.8 %collective-permute-start.5 = (bf16[2,32,4,8,128]{4,3,2,1,0:T(8,128)(2,1)S(1)}, bf16[2,32,4,8,128]{4,3,2,1,0:T(8,128)(2,1)S(1)}, u32[]{:S(2)}, u32[]{:S(2)}) collective-permute-start(bf16[2,32,4,8,128]{4,3,2,1,0:T(8,128)(2,1)S(1)} %maximum_select_fusion.1), channel_id=1, source_target_pairs={{0,2},{2,0},{1,3},{3,1},{4,6},{6,4},{5,7},{7,5},{8,10},{10,8},{9,1... | collective-permute-start | bytes 1572872 | tf_op jit(solution)/shard_map/ppermute | solution.py:21
  44.5 18.8 %collective-permute-start.1 = (f32[16,1,4,128]{3,0,2,1:T(8,128)S(1)}, f32[16,1,4,128]{3,0,2,1:T(8,128)S(1)}, u32[]{:S(2)}, u32[]{:S(2)}) collective-permute-start(f32[16,1,4,128]{3,0,2,1:T(8,128)S(1)} %fusion.63), channel_id=1, source_target_pairs={{480,0},{0,32},{32,64},{64,96},{96,128},{128,160},{160,192},{192,2... | collective-permute-start | bytes 98312 | tf_op jit(solution)/shard_map/while/body/eval_jaxpr/ppermute | solution.py:27
  48.4 14.9 %collective-permute-start = (bf16[16,4,128]{2,1,0:T(4,128)(2,1)S(1)}, bf16[16,4,128]{2,1,0:T(4,128)(2,1)S(1)}, u32[]{:S(2)}, u32[]{:S(2)}) collective-permute-start(bf16[16,4,128]{2,1,0:T(4,128)(2,1)S(1)} %copy.132), channel_id=1, source_target_pairs={{480,0},{0,32},{32,64},{64,96},{96,128},{128,160},{160,192},{192,2... | collective-permute-start | bytes 49160 | tf_op jit(solution)/shard_map/while/body/eval_jaxpr/ppermute | solution.py:27
  52.2 9.1 %collective-permute-start.2 = (f32[16,1,4]{0,2,1:T(4,128)S(1)}, f32[16,1,4]{0,2,1:T(4,128)S(1)}, u32[]{:S(2)}, u32[]{:S(2)}) collective-permute-start(f32[16,1,4]{0,2,1:T(4,128)S(1)} %get-tuple-element.423), channel_id=1, source_target_pairs={{480,0},{0,32},{32,64},{64,96},{96,128},{128,160},{160,192},{192,2... | collective-permute-start | bytes 776 | tf_op jit(solution)/shard_map/while/body/eval_jaxpr/ppermute | solution.py:27
  56.0 7.2 %collective-permute-start.3 = (f32[16,1,4]{0,2,1:T(4,128)S(1)}, f32[16,1,4]{0,2,1:T(4,128)S(1)}, u32[]{:S(2)}, u32[]{:S(2)}) collective-permute-start(f32[16,1,4]{0,2,1:T(4,128)S(1)} %get-tuple-element.424), channel_id=1, source_target_pairs={{480,0},{0,32},{32,64},{64,96},{96,128},{128,160},{160,192},{192,2... | collective-permute-start | bytes 776 | tf_op jit(solution)/shard_map/while/body/eval_jaxpr/ppermute | solution.py:27
  66.7 17.6 %collective-permute-start.1 = (f32[16,1,4,128]{3,0,2,1:T(8,128)S(1)}, f32[16,1,4,128]{3,0,2,1:T(8,128)S(1)}, u32[]{:S(2)}, u32[]{:S(2)}) collective-permute-start(f32[16,1,4,128]{3,0,2,1:T(8,128)S(1)} %fusion.63), channel_id=1, source_target_pairs={{480,0},{0,32},{32,64},{64,96},{96,128},{128,160},{160,192},{192,2... | collective-permute-start | bytes 98312 | tf_op jit(solution)/shard_map/while/body/eval_jaxpr/ppermute | solution.py:27
  70.0 14.4 %collective-permute-start = (bf16[16,4,128]{2,1,0:T(4,128)(2,1)S(1)}, bf16[16,4,128]{2,1,0:T(4,128)(2,1)S(1)}, u32[]{:S(2)}, u32[]{:S(2)}) collective-permute-start(bf16[16,4,128]{2,1,0:T(4,128)(2,1)S(1)} %copy.132), channel_id=1, source_target_pairs={{480,0},{0,32},{32,64},{64,96},{96,128},{128,160},{160,192},{192,2... | collective-permute-start | bytes 49160 | tf_op jit(solution)/shard_map/while/body/eval_jaxpr/ppermute | solution.py:27
  73.8 8.9 %collective-permute-start.2 = (f32[16,1,4]{0,2,1:T(4,128)S(1)}, f32[16,1,4]{0,2,1:T(4,128)S(1)}, u32[]{:S(2)}, u32[]{:S(2)}) collective-permute-start(f32[16,1,4]{0,2,1:T(4,128)S(1)} %get-tuple-element.423), channel_id=1, source_target_pairs={{480,0},{0,32},{32,64},{64,96},{96,128},{128,160},{160,192},{192,2... | collective-permute-start | bytes 776 | tf_op jit(solution)/shard_map/while/body/eval_jaxpr/ppermute | solution.py:27
  77.7 6.7 %collective-permute-start.3 = (f32[16,1,4]{0,2,1:T(4,128)S(1)}, f32[16,1,4]{0,2,1:T(4,128)S(1)}, u32[]{:S(2)}, u32[]{:S(2)}) collective-permute-start(f32[16,1,4]{0,2,1:T(4,128)S(1)} %get-tuple-element.424), channel_id=1, source_target_pairs={{480,0},{0,32},{32,64},{64,96},{96,128},{128,160},{160,192},{192,2... | collective-permute-start | bytes 776 | tf_op jit(solution)/shard_map/while/body/eval_jaxpr/ppermute | solution.py:27
  87.8 17.3 %collective-permute-start.1 = (f32[16,1,4,128]{3,0,2,1:T(8,128)S(1)}, f32[16,1,4,128]{3,0,2,1:T(8,128)S(1)}, u32[]{:S(2)}, u32[]{:S(2)}) collective-permute-start(f32[16,1,4,128]{3,0,2,1:T(8,128)S(1)} %fusion.63), channel_id=1, source_target_pairs={{480,0},{0,32},{32,64},{64,96},{96,128},{128,160},{160,192},{192,2... | collective-permute-start | bytes 98312 | tf_op jit(solution)/shard_map/while/body/eval_jaxpr/ppermute | solution.py:27
  91.7 13.4 %collective-permute-start = (bf16[16,4,128]{2,1,0:T(4,128)(2,1)S(1)}, bf16[16,4,128]{2,1,0:T(4,128)(2,1)S(1)}, u32[]{:S(2)}, u32[]{:S(2)}) collective-permute-start(bf16[16,4,128]{2,1,0:T(4,128)(2,1)S(1)} %copy.132), channel_id=1, source_target_pairs={{480,0},{0,32},{32,64},{64,96},{96,128},{128,160},{160,192},{192,2... | collective-permute-start | bytes 49160 | tf_op jit(solution)/shard_map/while/body/eval_jaxpr/ppermute | solution.py:27
  95.5 7.1 %collective-permute-start.2 = (f32[16,1,4]{0,2,1:T(4,128)S(1)}, f32[16,1,4]{0,2,1:T(4,128)S(1)}, u32[]{:S(2)}, u32[]{:S(2)}) collective-permute-start(f32[16,1,4]{0,2,1:T(4,128)S(1)} %get-tuple-element.423), channel_id=1, source_target_pairs={{480,0},{0,32},{32,64},{64,96},{96,128},{128,160},{160,192},{192,2... | collective-permute-start | bytes 776 | tf_op jit(solution)/shard_map/while/body/eval_jaxpr/ppermute | solution.py:27
  108.5 14.5 %collective-permute-start.1 = (f32[16,1,4,128]{3,0,2,1:T(8,128)S(1)}, f32[16,1,4,128]{3,0,2,1:T(8,128)S(1)}, u32[]{:S(2)}, u32[]{:S(2)}) collective-permute-start(f32[16,1,4,128]{3,0,2,1:T(8,128)S(1)} %fusion.63), channel_id=1, source_target_pairs={{480,0},{0,32},{32,64},{64,96},{96,128},{128,160},{160,192},{192,2... | collective-permute-start | bytes 98312 | tf_op jit(solution)/shard_map/while/body/eval_jaxpr/ppermute | solution.py:27
  111.5 11.6 %collective-permute-start = (bf16[16,4,128]{2,1,0:T(4,128)(2,1)S(1)}, bf16[16,4,128]{2,1,0:T(4,128)(2,1)S(1)}, u32[]{:S(2)}, u32[]{:S(2)}) collective-permute-start(bf16[16,4,128]{2,1,0:T(4,128)(2,1)S(1)} %copy.132), channel_id=1, source_target_pairs={{480,0},{0,32},{32,64},{64,96},{96,128},{128,160},{160,192},{192,2... | collective-permute-start | bytes 49160 | tf_op jit(solution)/shard_map/while/body/eval_jaxpr/ppermute | solution.py:27
  114.4 6.7 %collective-permute-start.2 = (f32[16,1,4]{0,2,1:T(4,128)S(1)}, f32[16,1,4]{0,2,1:T(4,128)S(1)}, u32[]{:S(2)}, u32[]{:S(2)}) collective-permute-start(f32[16,1,4]{0,2,1:T(4,128)S(1)} %get-tuple-element.423), channel_id=1, source_target_pairs={{480,0},{0,32},{32,64},{64,96},{96,128},{128,160},{160,192},{192,2... | collective-permute-start | bytes 776 | tf_op jit(solution)/shard_map/while/body/eval_jaxpr/ppermute | solution.py:27
  126.5 15.3 %collective-permute-start.1 = (f32[16,1,4,128]{3,0,2,1:T(8,128)S(1)}, f32[16,1,4,128]{3,0,2,1:T(8,128)S(1)}, u32[]{:S(2)}, u32[]{:S(2)}) collective-permute-start(f32[16,1,4,128]{3,0,2,1:T(8,128)S(1)} %fusion.63), channel_id=1, source_target_pairs={{480,0},{0,32},{32,64},{64,96},{96,128},{128,160},{160,192},{192,2... | collective-permute-start | bytes 98312 | tf_op jit(solution)/shard_map/while/body/eval_jaxpr/ppermute | solution.py:27
  129.2 12.6 %collective-permute-start = (bf16[16,4,128]{2,1,0:T(4,128)(2,1)S(1)}, bf16[16,4,128]{2,1,0:T(4,128)(2,1)S(1)}, u32[]{:S(2)}, u32[]{:S(2)}) collective-permute-start(bf16[16,4,128]{2,1,0:T(4,128)(2,1)S(1)} %copy.132), channel_id=1, source_target_pairs={{480,0},{0,32},{32,64},{64,96},{96,128},{128,160},{160,192},{192,2... | collective-permute-start | bytes 49160 | tf_op jit(solution)/shard_map/while/body/eval_jaxpr/ppermute | solution.py:27
  145.2 12.5 %collective-permute-start.1 = (f32[16,1,4,128]{3,0,2,1:T(8,128)S(1)}, f32[16,1,4,128]{3,0,2,1:T(8,128)S(1)}, u32[]{:S(2)}, u32[]{:S(2)}) collective-permute-start(f32[16,1,4,128]{3,0,2,1:T(8,128)S(1)} %fusion.63), channel_id=1, source_target_pairs={{480,0},{0,32},{32,64},{64,96},{96,128},{128,160},{160,192},{192,2... | collective-permute-start | bytes 98312 | tf_op jit(solution)/shard_map/while/body/eval_jaxpr/ppermute | solution.py:27
  147.1 10.5 %collective-permute-start = (bf16[16,4,128]{2,1,0:T(4,128)(2,1)S(1)}, bf16[16,4,128]{2,1,0:T(4,128)(2,1)S(1)}, u32[]{:S(2)}, u32[]{:S(2)}) collective-permute-start(bf16[16,4,128]{2,1,0:T(4,128)(2,1)S(1)} %copy.132), channel_id=1, source_target_pairs={{480,0},{0,32},{32,64},{64,96},{96,128},{128,160},{160,192},{192,2... | collective-permute-start | bytes 49160 | tf_op jit(solution)/shard_map/while/body/eval_jaxpr/ppermute | solution.py:27
  161.1 14.5 %collective-permute-start.1 = (f32[16,1,4,128]{3,0,2,1:T(8,128)S(1)}, f32[16,1,4,128]{3,0,2,1:T(8,128)S(1)}, u32[]{:S(2)}, u32[]{:S(2)}) collective-permute-start(f32[16,1,4,128]{3,0,2,1:T(8,128)S(1)} %fusion.63), channel_id=1, source_target_pairs={{480,0},{0,32},{32,64},{64,96},{96,128},{128,160},{160,192},{192,2... | collective-permute-start | bytes 98312 | tf_op jit(solution)/shard_map/while/body/eval_jaxpr/ppermute | solution.py:27
  163.1 12.6 %collective-permute-start = (bf16[16,4,128]{2,1,0:T(4,128)(2,1)S(1)}, bf16[16,4,128]{2,1,0:T(4,128)(2,1)S(1)}, u32[]{:S(2)}, u32[]{:S(2)}) collective-permute-start(bf16[16,4,128]{2,1,0:T(4,128)(2,1)S(1)} %copy.132), channel_id=1, source_target_pairs={{480,0},{0,32},{32,64},{64,96},{96,128},{128,160},{160,192},{192,2... | collective-permute-start | bytes 49160 | tf_op jit(solution)/shard_map/while/body/eval_jaxpr/ppermute | solution.py:27
  165.1 8.9 %collective-permute-start.2 = (f32[16,1,4]{0,2,1:T(4,128)S(1)}, f32[16,1,4]{0,2,1:T(4,128)S(1)}, u32[]{:S(2)}, u32[]{:S(2)}) collective-permute-start(f32[16,1,4]{0,2,1:T(4,128)S(1)} %get-tuple-element.423), channel_id=1, source_target_pairs={{480,0},{0,32},{32,64},{64,96},{96,128},{128,160},{160,192},{192,2... | collective-permute-start | bytes 776 | tf_op jit(solution)/shard_map/while/body/eval_jaxpr/ppermute | solution.py:27
  179.1 18.2 %collective-permute-start.1 = (f32[16,1,4,128]{3,0,2,1:T(8,128)S(1)}, f32[16,1,4,128]{3,0,2,1:T(8,128)S(1)}, u32[]{:S(2)}, u32[]{:S(2)}) collective-permute-start(f32[16,1,4,128]{3,0,2,1:T(8,128)S(1)} %fusion.63), channel_id=1, source_target_pairs={{480,0},{0,32},{32,64},{64,96},{96,128},{128,160},{160,192},{192,2... | collective-permute-start | bytes 98312 | tf_op jit(solution)/shard_map/while/body/eval_jaxpr/ppermute | solution.py:27
  182.9 14.4 %collective-permute-start = (bf16[16,4,128]{2,1,0:T(4,128)(2,1)S(1)}, bf16[16,4,128]{2,1,0:T(4,128)(2,1)S(1)}, u32[]{:S(2)}, u32[]{:S(2)}) collective-permute-start(bf16[16,4,128]{2,1,0:T(4,128)(2,1)S(1)} %copy.132), channel_id=1, source_target_pairs={{480,0},{0,32},{32,64},{64,96},{96,128},{128,160},{160,192},{192,2... | collective-permute-start | bytes 49160 | tf_op jit(solution)/shard_map/while/body/eval_jaxpr/ppermute | solution.py:27
  186.8 8.0 %collective-permute-start.2 = (f32[16,1,4]{0,2,1:T(4,128)S(1)}, f32[16,1,4]{0,2,1:T(4,128)S(1)}, u32[]{:S(2)}, u32[]{:S(2)}) collective-permute-start(f32[16,1,4]{0,2,1:T(4,128)S(1)} %get-tuple-element.423), channel_id=1, source_target_pairs={{480,0},{0,32},{32,64},{64,96},{96,128},{128,160},{160,192},{192,2... | collective-permute-start | bytes 776 | tf_op jit(solution)/shard_map/while/body/eval_jaxpr/ppermute | solution.py:27
  200.8 15.5 %collective-permute-start.1 = (f32[16,1,4,128]{3,0,2,1:T(8,128)S(1)}, f32[16,1,4,128]{3,0,2,1:T(8,128)S(1)}, u32[]{:S(2)}, u32[]{:S(2)}) collective-permute-start(f32[16,1,4,128]{3,0,2,1:T(8,128)S(1)} %fusion.63), channel_id=1, source_target_pairs={{480,0},{0,32},{32,64},{64,96},{96,128},{128,160},{160,192},{192,2... | collective-permute-start | bytes 98312 | tf_op jit(solution)/shard_map/while/body/eval_jaxpr/ppermute | solution.py:27
  203.7 12.6 %collective-permute-start = (bf16[16,4,128]{2,1,0:T(4,128)(2,1)S(1)}, bf16[16,4,128]{2,1,0:T(4,128)(2,1)S(1)}, u32[]{:S(2)}, u32[]{:S(2)}) collective-permute-start(bf16[16,4,128]{2,1,0:T(4,128)(2,1)S(1)} %copy.132), channel_id=1, source_target_pairs={{480,0},{0,32},{32,64},{64,96},{96,128},{128,160},{160,192},{192,2... | collective-permute-start | bytes 49160 | tf_op jit(solution)/shard_map/while/body/eval_jaxpr/ppermute | solution.py:27
  219.7 14.3 %collective-permute-start.1 = (f32[16,1,4,128]{3,0,2,1:T(8,128)S(1)}, f32[16,1,4,128]{3,0,2,1:T(8,128)S(1)}, u32[]{:S(2)}, u32[]{:S(2)}) collective-permute-start(f32[16,1,4,128]{3,0,2,1:T(8,128)S(1)} %fusion.63), channel_id=1, source_target_pairs={{480,0},{0,32},{32,64},{64,96},{96,128},{128,160},{160,192},{192,2... | collective-permute-start | bytes 98312 | tf_op jit(solution)/shard_map/while/body/eval_jaxpr/ppermute | solution.py:27
  221.6 12.4 %collective-permute-start = (bf16[16,4,128]{2,1,0:T(4,128)(2,1)S(1)}, bf16[16,4,128]{2,1,0:T(4,128)(2,1)S(1)}, u32[]{:S(2)}, u32[]{:S(2)}) collective-permute-start(bf16[16,4,128]{2,1,0:T(4,128)(2,1)S(1)} %copy.132), channel_id=1, source_target_pairs={{480,0},{0,32},{32,64},{64,96},{96,128},{128,160},{160,192},{192,2... | collective-permute-start | bytes 49160 | tf_op jit(solution)/shard_map/while/body/eval_jaxpr/ppermute | solution.py:27
  224.4 7.1 %collective-permute-start.2 = (f32[16,1,4]{0,2,1:T(4,128)S(1)}, f32[16,1,4]{0,2,1:T(4,128)S(1)}, u32[]{:S(2)}, u32[]{:S(2)}) collective-permute-start(f32[16,1,4]{0,2,1:T(4,128)S(1)} %get-tuple-element.423), channel_id=1, source_target_pairs={{480,0},{0,32},{32,64},{64,96},{96,128},{128,160},{160,192},{192,2... | collective-permute-start | bytes 776 | tf_op jit(solution)/shard_map/while/body/eval_jaxpr/ppermute | solution.py:27
  237.4 13.5 %collective-permute-start.1 = (f32[16,1,4,128]{3,0,2,1:T(8,128)S(1)}, f32[16,1,4,128]{3,0,2,1:T(8,128)S(1)}, u32[]{:S(2)}, u32[]{:S(2)}) collective-permute-start(f32[16,1,4,128]{3,0,2,1:T(8,128)S(1)} %fusion.63), channel_id=1, source_target_pairs={{480,0},{0,32},{32,64},{64,96},{96,128},{128,160},{160,192},{192,2... | collective-permute-start | bytes 98312 | tf_op jit(solution)/shard_map/while/body/eval_jaxpr/ppermute | solution.py:27
  240.4 10.6 %collective-permute-start = (bf16[16,4,128]{2,1,0:T(4,128)(2,1)S(1)}, bf16[16,4,128]{2,1,0:T(4,128)(2,1)S(1)}, u32[]{:S(2)}, u32[]{:S(2)}) collective-permute-start(bf16[16,4,128]{2,1,0:T(4,128)(2,1)S(1)} %copy.132), channel_id=1, source_target_pairs={{480,0},{0,32},{32,64},{64,96},{96,128},{128,160},{160,192},{192,2... | collective-permute-start | bytes 49160 | tf_op jit(solution)/shard_map/while/body/eval_jaxpr/ppermute | solution.py:27
  244.2 6.7 %collective-permute-start.3 = (f32[16,1,4]{0,2,1:T(4,128)S(1)}, f32[16,1,4]{0,2,1:T(4,128)S(1)}, u32[]{:S(2)}, u32[]{:S(2)}) collective-permute-start(f32[16,1,4]{0,2,1:T(4,128)S(1)} %get-tuple-element.424), channel_id=1, source_target_pairs={{480,0},{0,32},{32,64},{64,96},{96,128},{128,160},{160,192},{192,2... | collective-permute-start | bytes 776 | tf_op jit(solution)/shard_map/while/body/eval_jaxpr/ppermute | solution.py:27
  254.4 12.6 %collective-permute-start.1 = (f32[16,1,4,128]{3,0,2,1:T(8,128)S(1)}, f32[16,1,4,128]{3,0,2,1:T(8,128)S(1)}, u32[]{:S(2)}, u32[]{:S(2)}) collective-permute-start(f32[16,1,4,128]{3,0,2,1:T(8,128)S(1)} %fusion.63), channel_id=1, source_target_pairs={{480,0},{0,32},{32,64},{64,96},{96,128},{128,160},{160,192},{192,2... | collective-permute-start | bytes 98312 | tf_op jit(solution)/shard_map/while/body/eval_jaxpr/ppermute | solution.py:27
  256.3 10.7 %collective-permute-start = (bf16[16,4,128]{2,1,0:T(4,128)(2,1)S(1)}, bf16[16,4,128]{2,1,0:T(4,128)(2,1)S(1)}, u32[]{:S(2)}, u32[]{:S(2)}) collective-permute-start(bf16[16,4,128]{2,1,0:T(4,128)(2,1)S(1)} %copy.132), channel_id=1, source_target_pairs={{480,0},{0,32},{32,64},{64,96},{96,128},{128,160},{160,192},{192,2... | collective-permute-start | bytes 49160 | tf_op jit(solution)/shard_map/while/body/eval_jaxpr/ppermute | solution.py:27
  258.2 7.1 %collective-permute-start.2 = (f32[16,1,4]{0,2,1:T(4,128)S(1)}, f32[16,1,4]{0,2,1:T(4,128)S(1)}, u32[]{:S(2)}, u32[]{:S(2)}) collective-permute-start(f32[16,1,4]{0,2,1:T(4,128)S(1)} %get-tuple-element.423), channel_id=1, source_target_pairs={{480,0},{0,32},{32,64},{64,96},{96,128},{128,160},{160,192},{192,2... | collective-permute-start | bytes 776 | tf_op jit(solution)/shard_map/while/body/eval_jaxpr/ppermute | solution.py:27
  270.4 18.2 %collective-permute-start.1 = (f32[16,1,4,128]{3,0,2,1:T(8,128)S(1)}, f32[16,1,4,128]{3,0,2,1:T(8,128)S(1)}, u32[]{:S(2)}, u32[]{:S(2)}) collective-permute-start(f32[16,1,4,128]{3,0,2,1:T(8,128)S(1)} %fusion.63), channel_id=1, source_target_pairs={{480,0},{0,32},{32,64},{64,96},{96,128},{128,160},{160,192},{192,2... | collective-permute-start | bytes 98312 | tf_op jit(solution)/shard_map/while/body/eval_jaxpr/ppermute | solution.py:27
  274.3 14.4 %collective-permute-start = (bf16[16,4,128]{2,1,0:T(4,128)(2,1)S(1)}, bf16[16,4,128]{2,1,0:T(4,128)(2,1)S(1)}, u32[]{:S(2)}, u32[]{:S(2)}) collective-permute-start(bf16[16,4,128]{2,1,0:T(4,128)(2,1)S(1)} %copy.132), channel_id=1, source_target_pairs={{480,0},{0,32},{32,64},{64,96},{96,128},{128,160},{160,192},{192,2... | collective-permute-start | bytes 49160 | tf_op jit(solution)/shard_map/while/body/eval_jaxpr/ppermute | solution.py:27
  278.1 8.9 %collective-permute-start.2 = (f32[16,1,4]{0,2,1:T(4,128)S(1)}, f32[16,1,4]{0,2,1:T(4,128)S(1)}, u32[]{:S(2)}, u32[]{:S(2)}) collective-permute-start(f32[16,1,4]{0,2,1:T(4,128)S(1)} %get-tuple-element.423), channel_id=1, source_target_pairs={{480,0},{0,32},{32,64},{64,96},{96,128},{128,160},{160,192},{192,2... | collective-permute-start | bytes 776 | tf_op jit(solution)/shard_map/while/body/eval_jaxpr/ppermute | solution.py:27
  292.1 16.4 %collective-permute-start.1 = (f32[16,1,4,128]{3,0,2,1:T(8,128)S(1)}, f32[16,1,4,128]{3,0,2,1:T(8,128)S(1)}, u32[]{:S(2)}, u32[]{:S(2)}) collective-permute-start(f32[16,1,4,128]{3,0,2,1:T(8,128)S(1)} %fusion.63), channel_id=1, source_target_pairs={{480,0},{0,32},{32,64},{64,96},{96,128},{128,160},{160,192},{192,2... | collective-permute-start | bytes 98312 | tf_op jit(solution)/shard_map/while/body/eval_jaxpr/ppermute | solution.py:27
  295.9 12.6 %collective-permute-start = (bf16[16,4,128]{2,1,0:T(4,128)(2,1)S(1)}, bf16[16,4,128]{2,1,0:T(4,128)(2,1)S(1)}, u32[]{:S(2)}, u32[]{:S(2)}) collective-permute-start(bf16[16,4,128]{2,1,0:T(4,128)(2,1)S(1)} %copy.132), channel_id=1, source_target_pairs={{480,0},{0,32},{32,64},{64,96},{96,128},{128,160},{160,192},{192,2... | collective-permute-start | bytes 49160 | tf_op jit(solution)/shard_map/while/body/eval_jaxpr/ppermute | solution.py:27
  298.9 7.1 %collective-permute-start.2 = (f32[16,1,4]{0,2,1:T(4,128)S(1)}, f32[16,1,4]{0,2,1:T(4,128)S(1)}, u32[]{:S(2)}, u32[]{:S(2)}) collective-permute-start(f32[16,1,4]{0,2,1:T(4,128)S(1)} %get-tuple-element.423), channel_id=1, source_target_pairs={{480,0},{0,32},{32,64},{64,96},{96,128},{128,160},{160,192},{192,2... | collective-permute-start | bytes 776 | tf_op jit(solution)/shard_map/while/body/eval_jaxpr/ppermute | solution.py:27
  311.9 14.3 %collective-permute-start.1 = (f32[16,1,4,128]{3,0,2,1:T(8,128)S(1)}, f32[16,1,4,128]{3,0,2,1:T(8,128)S(1)}, u32[]{:S(2)}, u32[]{:S(2)}) collective-permute-start(f32[16,1,4,128]{3,0,2,1:T(8,128)S(1)} %fusion.63), channel_id=1, source_target_pairs={{480,0},{0,32},{32,64},{64,96},{96,128},{128,160},{160,192},{192,2... | collective-permute-start | bytes 98312 | tf_op jit(solution)/shard_map/while/body/eval_jaxpr/ppermute | solution.py:27
  314.8 11.4 %collective-permute-start = (bf16[16,4,128]{2,1,0:T(4,128)(2,1)S(1)}, bf16[16,4,128]{2,1,0:T(4,128)(2,1)S(1)}, u32[]{:S(2)}, u32[]{:S(2)}) collective-permute-start(bf16[16,4,128]{2,1,0:T(4,128)(2,1)S(1)} %copy.132), channel_id=1, source_target_pairs={{480,0},{0,32},{32,64},{64,96},{96,128},{128,160},{160,192},{192,2... | collective-permute-start | bytes 49160 | tf_op jit(solution)/shard_map/while/body/eval_jaxpr/ppermute | solution.py:27
  316.8 6.9 %collective-permute-start.2 = (f32[16,1,4]{0,2,1:T(4,128)S(1)}, f32[16,1,4]{0,2,1:T(4,128)S(1)}, u32[]{:S(2)}, u32[]{:S(2)}) collective-permute-start(f32[16,1,4]{0,2,1:T(4,128)S(1)} %get-tuple-element.423), channel_id=1, source_target_pairs={{480,0},{0,32},{32,64},{64,96},{96,128},{128,160},{160,192},{192,2... | collective-permute-start | bytes 776 | tf_op jit(solution)/shard_map/while/body/eval_jaxpr/ppermute | solution.py:27
  329.7 14.5 %collective-permute-start.1 = (f32[16,1,4,128]{3,0,2,1:T(8,128)S(1)}, f32[16,1,4,128]{3,0,2,1:T(8,128)S(1)}, u32[]{:S(2)}, u32[]{:S(2)}) collective-permute-start(f32[16,1,4,128]{3,0,2,1:T(8,128)S(1)} %fusion.63), channel_id=1, source_target_pairs={{480,0},{0,32},{32,64},{64,96},{96,128},{128,160},{160,192},{192,2... | collective-permute-start | bytes 98312 | tf_op jit(solution)/shard_map/while/body/eval_jaxpr/ppermute | solution.py:27
  332.6 11.6 %collective-permute-start = (bf16[16,4,128]{2,1,0:T(4,128)(2,1)S(1)}, bf16[16,4,128]{2,1,0:T(4,128)(2,1)S(1)}, u32[]{:S(2)}, u32[]{:S(2)}) collective-permute-start(bf16[16,4,128]{2,1,0:T(4,128)(2,1)S(1)} %copy.132), channel_id=1, source_target_pairs={{480,0},{0,32},{32,64},{64,96},{96,128},{128,160},{160,192},{192,2... | collective-permute-start | bytes 49160 | tf_op jit(solution)/shard_map/while/body/eval_jaxpr/ppermute | solution.py:27
  (23 other events, 226.0 us)
where the time goes:
time: 348 us; the launch traced here: 345 us
  starting transfers between devices  211 us (61%)
  waiting for transfers between devices  50.6 us (15%)
  matrix products  45.5 us (13%)
  blocking collectives  15.7 us (5%)
  local copies, waits for them, and re-layouts  12.8 us (4%)
  other arithmetic  6.72 us (2%)
    ppermute x64, starting transfers between devices, from_behind(): return lax.ppermute(block, axis, route)  205 us
    ppermute x64, waiting for transfers between devices, from_behind(): return lax.ppermute(block, axis, route)  42 us
    dot_general x16, matrix products, attend_partially(): jnp.einsum('bkgd,pkd->bkgp', query_group, prompt_part[0], preferred_eleme...  19.9 us
    dot_general x16, matrix products, attend_partially(): jnp.einsum('bkgp,pkd->bkgd', prompt_weights.astype(jnp.bfloat16), prompt_...  19.2 us
    unnamed x1, blocking collectives  15.7 us
    ppermute x2, waiting for transfers between devices, swapped(): return lax.ppermute(block, axis, route)  8.56 us
    unnamed x18, local copies, waits for them, and re-layouts  7.4 us
  transfers between devices with their start and end apart: 66, of which 24 were waited for; matrix products, arithmetic and copies ran while one was open for 2% of the time, Pallas kernels for 0%

commit v1 on v0

v1 whole, which is shorter than its diff:
```python
import functools

import jax
import jax.numpy as jnp
from jax import lax
from jax.experimental import pallas as pl
from jax.experimental.pallas import tpu as pltpu
from jax.sharding import PartitionSpec as P

HEADS = 64
KVH = 8
HD = 128
FAMILY_DEVICES = 4
PENALTY_WEIGHT = 0.5
FAR_BELOW = -1e30
LOG2E = 1.4426950408889634
EXTRA = 16


def rows_by_head(count):
    row = lax.broadcasted_iota(jnp.int32, (128, 128), 0)
    col = lax.broadcasted_iota(jnp.int32, (128, 128), 1)
    per = 128 // count
    hit = (row // per == col % count) & (row % per == col // count)
    return jnp.where(hit, 1.0, 0.0).astype(jnp.bfloat16)


def attend_kernel(parents, lengths, q_ref, kv_ref, s0, s1, s2, s3, new_ref, out_ref, picked, ext):
    beams = 16
    z = lax.axis_index("ctx")
    place = lax.axis_index("beam") % FAMILY_DEVICES
    scale = HD**-0.5

    for b in range(beams):
        parent = parents[b]
        slot = lax.bitwise_xor((parent // beams) % FAMILY_DEVICES, place)
        local = parent % beams
        for k, held in enumerate((s0, s1, s2, s3)):

            @pl.when(slot == k)
            def _(held=held, local=local, b=b):
                for c in range(2):
                    picked[c, pl.ds(b * 32, 32)] = held[c, local]

    by_head = rows_by_head(KVH)
    ext[...] = jnp.zeros_like(ext)
    for c in range(2):
        for part in range(5):
            rows = picked[c, pl.ds(part * 128, 128)] if part < 4 else new_ref[c]
            moved = jnp.dot(by_head, rows, preferred_element_type=jnp.float32).astype(jnp.bfloat16)
            for g in range(KVH):
                ext[c, g, pl.ds(part * 16, 16)] = moved[g * 16 : (g + 1) * 16]

    row = lax.broadcasted_iota(jnp.int32, (128, 128), 0)
    col = lax.broadcasted_iota(jnp.int32, (128, 128), 1)
    row_beam = (row % 64) // 4
    live = jnp.zeros((128, 128), jnp.int32)
    for b in range(beams):
        live = jnp.where(row_beam == b, lengths[b], live)
    on_suffix = (col < 64) & (col // 4 == row_beam) & (z * 4 + col % 4 < live)
    on_new = (col >= 64) & (col - 64 == row_beam)
    bias_plain = jnp.where(on_suffix, 0.0, FAR_BELOW)
    bias_new = jnp.where(on_suffix | on_new, 0.0, FAR_BELOW)

    transposed = (((1,), (1,)), ((), ()))
    stats = jnp.zeros((128, 128), jnp.float32)
    for g in range(KVH):
        q = q_ref[2 * g : 2 * g + 2].reshape(128, HD)
        s = lax.dot_general(q, kv_ref[0, g], transposed, preferred_element_type=jnp.float32)
        e = lax.dot_general(q, ext[0, g], transposed, preferred_element_type=jnp.float32)
        e = e + jnp.where(z == 2 * g, bias_new, bias_plain)
        m = jnp.maximum(jnp.max(s, axis=1, keepdims=True), jnp.max(e, axis=1, keepdims=True))
        p = jnp.exp2((s - m) * (scale * LOG2E))
        pe = jnp.exp2((e - m) * (scale * LOG2E))
        total = jnp.sum(p, axis=1, keepdims=True) + jnp.sum(pe, axis=1, keepdims=True)
        o = jnp.dot(p.astype(jnp.bfloat16), kv_ref[1, g], preferred_element_type=jnp.float32)
        o = o + jnp.dot(pe.astype(jnp.bfloat16), ext[1, g], preferred_element_type=jnp.float32)
        o = (o / total).astype(jnp.bfloat16)
        out_ref[2 * g, 0:64] = o[0:64]
        out_ref[2 * g + 1, 0:64] = o[64:128]
        stats = jnp.where(col == g, m * scale + jnp.log(total), stats)
    flat = stats.T[0:KVH]
    high = flat.astype(jnp.bfloat16).astype(jnp.float32)
    middle = (flat - high).astype(jnp.bfloat16).astype(jnp.float32)
    low = flat - high - middle
    place_row = lax.broadcasted_iota(jnp.int32, (EXTRA, 128), 0)
    for g in range(KVH):
        block = jnp.where(place_row == 0, high[g : g + 1], 0.0)
        block = jnp.where(place_row == 1, middle[g : g + 1], block)
        block = jnp.where(place_row == 2, low[g : g + 1], block).astype(jnp.bfloat16)
        out_ref[2 * g, 64 : 64 + EXTRA] = block
        out_ref[2 * g + 1, 64 : 64 + EXTRA] = block


def combine_kernel(parts_ref, out_ref):
    z = lax.axis_index("ctx")
    extra = parts_ref[:, 64 : 64 + EXTRA].astype(jnp.float32)
    logs = extra[:, 0] + extra[:, 1] + extra[:, 2]
    weights = jnp.exp(logs - jnp.max(logs, axis=0, keepdims=True))
    weights = weights / jnp.sum(weights, axis=0, keepdims=True)
    weights = jnp.where(z % 2 == 1, pltpu.roll(weights, 64, 1), weights)
    by_row = weights.T[0:64]
    mixed = jnp.zeros((64, HD), jnp.float32)
    for source in range(16):
        mixed = mixed + by_row[:, source : source + 1] * parts_ref[source, 0:64].astype(jnp.float32)
    out_ref[...] = mixed.astype(jnp.bfloat16)


def body(queries, prompt_kv, suffix_kv, new_kv, parents, lengths, token_ids, group_ids):
    vmem = pl.BlockSpec(memory_space=pltpu.VMEM)
    smem = pl.BlockSpec(memory_space=pltpu.SMEM)

    own = queries.reshape(1, 64, HD)
    with jax.named_scope("queries_to_all"):
        everyone = lax.all_to_all(
            jnp.broadcast_to(own, (16, 64, HD)), "ctx", 0, 0, tiled=True
        )
    suffix = suffix_kv.reshape(2, 16, 32, HD)
    with jax.named_scope("suffix_family"):
        held = [suffix] + [
            lax.ppermute(suffix, "beam", [(i, i ^ k) for i in range(32)]) for k in (1, 2, 3)
        ]
    by_head = jnp.transpose(prompt_kv, (0, 2, 1, 3))

    parts = pl.pallas_call(
        attend_kernel,
        out_shape=jax.ShapeDtypeStruct((16, 64 + EXTRA, HD), jnp.bfloat16),
        in_specs=[smem, smem] + [vmem] * 7,
        out_specs=vmem,
        scratch_shapes=[
            pltpu.VMEM((2, 512, HD), jnp.bfloat16),
            pltpu.VMEM((2, KVH, 128, HD), jnp.bfloat16),
        ],
        compiler_params=pltpu.CompilerParams(vmem_limit_bytes=32 * 2**20),
        cost_estimate=pl.CostEstimate(
            flops=600_000_000, bytes_accessed=6_000_000, transcendentals=1_200_000
        ),
        name="attend",
    )(parents, lengths, everyone, by_head, *held, new_kv.reshape(2, 128, HD))

    with jax.named_scope("parts_home"):
        parts = lax.all_to_all(parts, "ctx", 0, 0, tiled=True)
    attended = pl.pallas_call(
        combine_kernel,
        out_shape=jax.ShapeDtypeStruct((64, HD), jnp.bfloat16),
        in_specs=[vmem],
        out_specs=vmem,
        name="combine",
    )(parts).reshape(16, 4, HD)

    all_tokens, all_groups = (
        lax.all_gather(token_ids, "beam", axis=0, tiled=True),
        lax.all_gather(group_ids, "beam", axis=0, tiled=True),
    )
    earlier = (all_groups[None, :] < group_ids[:, None]) & (
        all_tokens[None, :] == token_ids[:, None]
    )
    penalty = PENALTY_WEIGHT * jnp.sum(earlier.astype(jnp.float32), axis=1)
    return (attended, penalty)


def solution(mesh):
    in_specs = (
        P("beam", "ctx", None),
        P(None, "ctx", None, None),
        P(None, "beam", "ctx", None, None),
        P(None, "beam", None, None),
        P("beam"),
        P("beam"),
        P("beam"),
        P("beam"),
    )
    out_specs = (P("beam", "ctx", None), P("beam"))
    return jax.shard_map(body, mesh=mesh, in_specs=in_specs, out_specs=out_specs, check_vma=False)
```

time: 348 us -> 79.7 us (0.23)
  the two profiles are of different devices: /device:TPU:2 before, /device:TPU:12 now
where the time goes in v1:
time: 79.7 us; the launch traced here: 79.1 us
  starting transfers between devices  34.7 us (44%)
  blocking collectives  13.2 us (17%)
  local copies, waits for them, and re-layouts  11 us (14%)
  waiting for transfers between devices  10.8 us (14%)
  Pallas kernels  7.2 us (9%)
  between operations  1.4 us (2%)
    all_to_all x1, starting transfers between devices, body(): lax.all_to_all(jnp.broadcast_to(own, (16, 64, HD)), 'ctx', 0, 0, tiled=True)  15.2 us
    unnamed x1, blocking collectives  13.2 us
    all_to_all x1, starting transfers between devices, body(): parts = lax.all_to_all(parts, 'ctx', 0, 0, tiled=True)  11.8 us
    unnamed x22, local copies, waits for them, and re-layouts  9.57 us
    ppermute x3, starting transfers between devices, body(): lax.ppermute(suffix, 'beam', [(i, i ^ k) for i in range(32)])  7.72 us
    ppermute x3, waiting for transfers between devices, body(): lax.ppermute(suffix, 'beam', [(i, i ^ k) for i in range(32)])  5.46 us
    pallas_call x1, Pallas kernels, body(): pl.pallas_call(attend_kernel, out_shape=jax.ShapeDtypeStruct((16, 64 + EX...  5.21 us
    all_to_all x1, waiting for transfers between devices, body(): parts = lax.all_to_all(parts, 'ctx', 0, 0, tiled=True)  5.08 us
  transfers between devices with their start and end apart: 5, of which 4 were waited for; matrix products, arithmetic and copies ran while one was open for 9% of the time, Pallas kernels for 0%

profile of v1, /device:TPU:12, one launch (start us, length us, event | category | flops | bytes accessed | tf_op | source)
XLA Modules:
  0.0 79.1 jit_solution(15716339959284257488)
XLA Ops:
  0.6 1.5 %broadcast_in_dim.5 = bf16[16,64,128]{2,1,0:T(8,128)(2,1)} broadcast(bf16[64,128]{1,0:T(8,128)(2,1)} %bitcast.14), dimensions={1,2} | broadcast | bytes 278528 | tf_op jit(solution)/shard_map/queries_to_all/broadcast_in_dim | solution.py:116
  2.1 15.2 %all-to-all-start = ((bf16[16,64,128]{2,1,0:T(8,128)(2,1)}), bf16[16,64,128]{2,1,0:T(8,128)(2,1)S(1)}, u32[]{:S(2)}, u32[]{:S(2)}) async-start(bf16[16,64,128]{2,1,0:T(8,128)(2,1)} %broadcast_in_dim.5), calls=%async_computation | async-start | bytes 524288 | tf_op jit(solution)/shard_map/queries_to_all/all_to_all | solution.py:115
  17.3 0.0 copy-start.1
  17.3 0.0 copy-start.2
  17.3 0.0 copy-start.3
  17.3 0.0 copy-start.4
  17.3 2.1 %collective-permute-start = (bf16[2,16,32,128]{3,2,1,0:T(8,128)(2,1)}, bf16[2,16,32,128]{3,2,1,0:T(8,128)(2,1)S(1)}, u32[]{:S(2)}, u32[]{:S(2)}) collective-permute-start(bf16[2,16,32,128]{3,2,1,0:T(8,128)(2,1)} %bitcast.9), channel_id=1, source_target_pairs={{0,1},{1,0},{2,3},{3,2},{4,5},{5,4},{6,7},{7,6},{8,9},{9,8},{10,11... | collective-permute-start | bytes 786440 | tf_op jit(solution)/shard_map/suffix_family/ppermute | solution.py:121
  19.4 3.1 %collective-permute-start.1 = (bf16[2,16,32,128]{3,2,1,0:T(8,128)(2,1)}, bf16[2,16,32,128]{3,2,1,0:T(8,128)(2,1)S(1)}, u32[]{:S(2)}, u32[]{:S(2)}) collective-permute-start(bf16[2,16,32,128]{3,2,1,0:T(8,128)(2,1)} %bitcast.10), channel_id=1, source_target_pairs={{0,2},{1,3},{2,0},{3,1},{4,6},{5,7},{6,4},{7,5},{8,10},{9,11},{10,... | collective-permute-start | bytes 786440 | tf_op jit(solution)/shard_map/suffix_family/ppermute | solution.py:121
  22.5 2.6 %collective-permute-start.2 = (bf16[2,16,32,128]{3,2,1,0:T(8,128)(2,1)}, bf16[2,16,32,128]{3,2,1,0:T(8,128)(2,1)S(1)}, u32[]{:S(2)}, u32[]{:S(2)}) collective-permute-start(bf16[2,16,32,128]{3,2,1,0:T(8,128)(2,1)} %bitcast.11), channel_id=1, source_target_pairs={{0,3},{1,2},{2,1},{3,0},{4,7},{5,6},{6,5},{7,4},{8,11},{9,10},{10,... | collective-permute-start | bytes 786440 | tf_op jit(solution)/shard_map/suffix_family/ppermute | solution.py:121
  25.1 4.9 %copy.13 = bf16[2,1024,8,128]{3,1,2,0:T(8,128)(2,1)} copy(bf16[2,1024,8,128]{3,2,1,0:T(8,128)(2,1)} %param.9) | data formatting | bytes 8388608 | tf_op args[1]
  30.0 0.0 copy-start.7
  30.0 0.0 copy-start.6
  30.0 0.0 collective-permute-done.s1
  30.0 0.6 collective-permute-done.1.s2
  30.6 4.8 %collective-permute-done.2.s3 = bf16[2,16,32,128]{3,2,1,0:T(8,128)(2,1)S(1)} collective-permute-done((bf16[2,16,32,128]{3,2,1,0:T(8,128)(2,1)}, bf16[2,16,32,128]{3,2,1,0:T(8,128)(2,1)S(1)}, u32[]{:S(2)}, u32[]{:S(2)}) %collective-permute-start.2) | collective-permute-done | bytes 262176 | tf_op jit(solution)/shard_map/suffix_family/ppermute | solution.py:121
  35.4 0.2 all-to-all-done.q_ref
  35.7 0.0 copy-done.1
  35.7 0.0 copy-done.2
  35.7 0.0 copy-done.3
  35.7 0.0 copy-done.4
  35.7 0.0 copy-start
  35.7 2.2 %copy-done = bf16[2,1024,8,128]{3,1,2,0:T(8,128)(2,1)S(1)} copy-done((bf16[2,1024,8,128]{3,1,2,0:T(8,128)(2,1)S(1)}, bf16[2,1024,8,128]{3,1,2,0:T(8,128)(2,1)}, u32[]{:S(2)}) %copy-start) | copy-done | bytes 4194328
  37.9 5.2 %attend.1 = bf16[16,80,128]{2,1,0:T(8,128)(2,1)} custom-call(s32[16]{0:T(128)S(1)} %copy-done.3, s32[16]{0:T(128)S(1)} %copy-done.4, bf16[16,64,128]{2,1,0:T(8,128)(2,1)S(1)} %all-to-all-done.q_ref, bf16[2,8,1024,128]{3,2,1,0:T(8,128)(2,1)S(1)} %bitcast.8, bf16[2,16,32,128]{3,2,1,0:T(8,128)(2,1)S(1)} %bitcast.12, ...), custom_call_target="tpu_custom_call" | custom-call | flops 600000000 | bytes 6000000 | tf_op jit(solution)/shard_map/attend/pallas_call | solution.py:125
  43.1 11.8 %all-to-all-start.1 = ((bf16[16,80,128]{2,1,0:T(8,128)(2,1)}), bf16[16,80,128]{2,1,0:T(8,128)(2,1)S(1)}, u32[]{:S(2)}, u32[]{:S(2)}) async-start(bf16[16,80,128]{2,1,0:T(8,128)(2,1)} %attend.1), calls=%async_computation.1 | async-start | bytes 655360 | tf_op jit(solution)/shard_map/parts_home/all_to_all | solution.py:142
  54.9 1.3 %dynamic-slice = u32[1]{0:T(128)} dynamic-slice(u32[512]{0:T(512)} %constant.13, u32[]{:T(128)S(6)} %add), dynamic_slice_sizes={1} | dynamic-slice | bytes 12
  56.8 0.0 copy-done.7
  56.9 0.2 dynamic-update-slice
  57.1 0.0 copy-done.6
  57.1 0.2 dynamic-update-slice.1
  57.3 13.2 %all-reduce.2 = (s32[512]{0:T(512)S(1)}, s32[512]{0:T(512)S(1)}) all-reduce(s32[512]{0:T(512)S(1)} %dynamic-update-slice.1, s32[512]{0:T(512)S(1)} %dynamic-update-slice), channel_id=1, replica_groups=mesh['ctx'=16,'beam'=32] {'beam'}, use_global_device_ids=true, to_apply=%add.1 | all-reduce | flops 1024 | bytes 8192
  70.6 0.2 convert_reduce_fusion
  70.8 0.5 broadcast_multiply_fusion
  71.3 5.1 %all-to-all-done.1.parts_ref = bf16[16,80,128]{2,1,0:T(8,128)(2,1)S(1)} async-done(((bf16[16,80,128]{2,1,0:T(8,128)(2,1)}), bf16[16,80,128]{2,1,0:T(8,128)(2,1)S(1)}, u32[]{:S(2)}, u32[]{:S(2)}) %all-to-all-start.1) | async-done | bytes 327712 | tf_op jit(solution)/shard_map/parts_home/all_to_all | solution.py:142
  76.4 0.0 copy-start.5
  76.4 0.7 copy-done.5
  77.1 2.0 %combine.1 = bf16[64,128]{1,0:T(8,128)(2,1)} custom-call(bf16[16,80,128]{2,1,0:T(8,128)(2,1)} %copy-done.5), custom_call_target="tpu_custom_call" | custom-call | tf_op jit(solution)/shard_map/combine/pallas_call | solution.py:143
  (2 shorter events, 0.0 us)
Async XLA Ops:
  2.1 33.6 %all-to-all-start = ((bf16[16,64,128]{2,1,0:T(8,128)(2,1)}), bf16[16,64,128]{2,1,0:T(8,128)(2,1)S(1)}, u32[]{:S(2)}, u32[]{:S(2)}) async-start(bf16[16,64,128]{2,1,0:T(8,128)(2,1)} %broadcast_in_dim.5), calls=%async_computation | async-start | bytes 524288 | tf_op jit(solution)/shard_map/queries_to_all/all_to_all | solution.py:115
  17.3 18.4 %copy-start.1 = (bf16[2,16,4,8,128]{4,3,2,1,0:T(8,128)(2,1)S(1)}, bf16[2,16,4,8,128]{4,3,2,1,0:T(8,128)(2,1)}, u32[]{:S(2)}) copy-start(bf16[2,16,4,8,128]{4,3,2,1,0:T(8,128)(2,1)} %param.10) | copy-start | bytes 786436
  17.3 18.4 %copy-start.2 = (bf16[2,16,8,128]{3,2,1,0:T(8,128)(2,1)S(1)}, bf16[2,16,8,128]{3,2,1,0:T(8,128)(2,1)}, u32[]{:S(2)}) copy-start(bf16[2,16,8,128]{3,2,1,0:T(8,128)(2,1)} %param.11) | copy-start | bytes 196612
  17.3 18.3 %copy-start.3 = (s32[16]{0:T(128)S(1)}, s32[16]{0:T(128)}, u32[]{:S(2)}) copy-start(s32[16]{0:T(128)} %parents.1) | copy-start | bytes 196
  17.3 18.3 %copy-start.4 = (s32[16]{0:T(128)S(1)}, s32[16]{0:T(128)}, u32[]{:S(2)}) copy-start(s32[16]{0:T(128)} %lengths.1) | copy-start | bytes 196
  17.3 12.6 %collective-permute-start = (bf16[2,16,32,128]{3,2,1,0:T(8,128)(2,1)}, bf16[2,16,32,128]{3,2,1,0:T(8,128)(2,1)S(1)}, u32[]{:S(2)}, u32[]{:S(2)}) collective-permute-start(bf16[2,16,32,128]{3,2,1,0:T(8,128)(2,1)} %bitcast.9), channel_id=1, source_target_pairs={{0,1},{1,0},{2,3},{3,2},{4,5},{5,4},{6,7},{7,6},{8,9},{9,8},{10,11... | collective-permute-start | bytes 786440 | tf_op jit(solution)/shard_map/suffix_family/ppermute | solution.py:121
  19.4 11.2 %collective-permute-start.1 = (bf16[2,16,32,128]{3,2,1,0:T(8,128)(2,1)}, bf16[2,16,32,128]{3,2,1,0:T(8,128)(2,1)S(1)}, u32[]{:S(2)}, u32[]{:S(2)}) collective-permute-start(bf16[2,16,32,128]{3,2,1,0:T(8,128)(2,1)} %bitcast.10), channel_id=1, source_target_pairs={{0,2},{1,3},{2,0},{3,1},{4,6},{5,7},{6,4},{7,5},{8,10},{9,11},{10,... | collective-permute-start | bytes 786440 | tf_op jit(solution)/shard_map/suffix_family/ppermute | solution.py:121
  22.5 12.9 %collective-permute-start.2 = (bf16[2,16,32,128]{3,2,1,0:T(8,128)(2,1)}, bf16[2,16,32,128]{3,2,1,0:T(8,128)(2,1)S(1)}, u32[]{:S(2)}, u32[]{:S(2)}) collective-permute-start(bf16[2,16,32,128]{3,2,1,0:T(8,128)(2,1)} %bitcast.11), channel_id=1, source_target_pairs={{0,3},{1,2},{2,1},{3,0},{4,7},{5,6},{6,5},{7,4},{8,11},{9,10},{10,... | collective-permute-start | bytes 786440 | tf_op jit(solution)/shard_map/suffix_family/ppermute | solution.py:121
  30.0 26.9 %copy-start.7 = (s32[16]{0:T(128)S(1)}, s32[16]{0:T(128)}, u32[]{:S(2)}) copy-start(s32[16]{0:T(128)} %param.15) | copy-start | bytes 196
  30.0 27.1 %copy-start.6 = (s32[16]{0:T(128)S(1)}, s32[16]{0:T(128)}, u32[]{:S(2)}) copy-start(s32[16]{0:T(128)} %param.14) | copy-start | bytes 196
  35.7 2.2 %copy-start = (bf16[2,1024,8,128]{3,1,2,0:T(8,128)(2,1)S(1)}, bf16[2,1024,8,128]{3,1,2,0:T(8,128)(2,1)}, u32[]{:S(2)}) copy-start(bf16[2,1024,8,128]{3,1,2,0:T(8,128)(2,1)} %copy.13) | copy-start | bytes 12582916
  43.1 33.3 %all-to-all-start.1 = ((bf16[16,80,128]{2,1,0:T(8,128)(2,1)}), bf16[16,80,128]{2,1,0:T(8,128)(2,1)S(1)}, u32[]{:S(2)}, u32[]{:S(2)}) async-start(bf16[16,80,128]{2,1,0:T(8,128)(2,1)} %attend.1), calls=%async_computation.1 | async-start | bytes 655360 | tf_op jit(solution)/shard_map/parts_home/all_to_all | solution.py:142
  76.4 0.7 copy-start.5

commit v2 on v1

v2 whole, which is shorter than its diff:
```python
import functools

import jax
import jax.numpy as jnp
from jax import lax
from jax.experimental import pallas as pl
from jax.experimental.pallas import tpu as pltpu
from jax.sharding import PartitionSpec as P

HEADS = 64
KVH = 8
HD = 128
FAMILY_DEVICES = 4
PENALTY_WEIGHT = 0.5
FAR_BELOW = -1e30
LOG2E = 1.4426950408889634
EXTRA = 8


def rows_by_head(count):
    row = lax.broadcasted_iota(jnp.int32, (128, 128), 0)
    col = lax.broadcasted_iota(jnp.int32, (128, 128), 1)
    per = 128 // count
    hit = (row // per == col % count) & (row % per == col // count)
    return jnp.where(hit, 1.0, 0.0).astype(jnp.bfloat16)


def by_head_kernel(kv_ref, out_ref, natural, moved, in_sems, out_sems):
    step = 256
    chunks = [(c, pl.ds(first, step)) for c in range(2) for first in range(0, 1024, step)]
    loads = [
        pltpu.make_async_copy(kv_ref.at[c, rows], natural.at[c, rows], in_sems.at[n])
        for n, (c, rows) in enumerate(chunks)
    ]
    stores = [
        pltpu.make_async_copy(moved.at[c, :, rows], out_ref.at[c, :, rows], out_sems.at[n])
        for n, (c, rows) in enumerate(chunks)
    ]
    for load in loads:
        load.start()
    for (c, rows), load, store in zip(chunks, loads, stores):
        load.wait()
        for first in range(0, step, 64):
            part = pl.ds(rows.start + first, 64)
            moved[c, :, part] = jnp.swapaxes(natural[c, part], 0, 1)
        store.start()
    for store in stores:
        store.wait()


def token_rows_kernel(token_ids, group_ids, rows_a, rows_b):
    row = lax.broadcasted_iota(jnp.int32, (EXTRA, 128), 0)
    lane = lax.broadcasted_iota(jnp.int32, (EXTRA, 128), 1)
    for rows_ref, first_lane in ((rows_a, 0), (rows_b, 16)):
        tokens = jnp.zeros((EXTRA, 128), jnp.int32)
        groups = jnp.zeros((EXTRA, 128), jnp.int32)
        for b in range(16):
            tokens = jnp.where(lane == first_lane + b, token_ids[b], tokens)
            groups = jnp.where(lane == first_lane + b, group_ids[b], groups)
        digits = jnp.where(row == 3, tokens >> 16, 0)
        digits = jnp.where(row == 4, (tokens >> 8) & 255, digits)
        digits = jnp.where(row == 5, tokens & 255, digits)
        digits = jnp.where(row == 6, groups, digits)
        rows_ref[...] = digits.astype(jnp.float32).astype(jnp.bfloat16)


def attend_kernel(
    parents_ref, lengths_ref, q_ref, kv_ref, near, far, new_ref, tok_a, tok_b, out_ref,
    kv, picked, ext, new_rows, parents, lengths, sems, small_sems,
):
    beams = 16
    z = lax.axis_index("ctx")
    place = lax.axis_index("beam") % FAMILY_DEVICES
    scale = HD**-0.5

    loads = [
        pltpu.make_async_copy(kv_ref.at[c, g], kv.at[c, g], sems.at[c, g])
        for g in range(KVH)
        for c in range(2)
    ]
    small = [
        pltpu.make_async_copy(source, target, small_sems.at[n])
        for n, (source, target) in enumerate(
            ((parents_ref, parents), (lengths_ref, lengths), (new_ref, new_rows))
        )
    ]
    for load in small + loads:
        load.start()
    for load in small:
        load.wait()

    for b in range(beams):
        parent = parents[b]
        slot = lax.bitwise_xor((parent // beams) % FAMILY_DEVICES, place)
        local = parent % beams
        for k, held in enumerate((near, far)):

            @pl.when(slot % 2 == k)
            def _(held=held, local=local, slot=slot, b=b):
                for c in range(2):
                    picked[c, pl.ds(b * 32, 32)] = held[slot // 2, c, local]

    by_head = rows_by_head(KVH)
    ext[...] = jnp.zeros_like(ext)
    for c in range(2):
        for part in range(5):
            rows = picked[c, pl.ds(part * 128, 128)] if part < 4 else new_rows[c]
            moved = jnp.dot(by_head, rows, preferred_element_type=jnp.float32).astype(jnp.bfloat16)
            for g in range(KVH):
                ext[c, g, pl.ds(part * 16, 16)] = moved[g * 16 : (g + 1) * 16]

    row = lax.broadcasted_iota(jnp.int32, (128, 128), 0)
    col = lax.broadcasted_iota(jnp.int32, (128, 128), 1)
    row_beam = (row % 64) // 4
    live = jnp.zeros((128, 128), jnp.int32)
    for b in range(beams):
        live = jnp.where(row_beam == b, lengths[b], live)
    on_suffix = (col < 64) & (col // 4 == row_beam) & (z * 4 + col % 4 < live)
    on_new = (col >= 64) & (col - 64 == row_beam)
    bias_plain = jnp.where(on_suffix, 0.0, FAR_BELOW)
    bias_new = jnp.where(on_suffix | on_new, 0.0, FAR_BELOW)

    transposed = (((1,), (1,)), ((), ()))
    stats = jnp.zeros((128, 128), jnp.float32)
    for g in range(KVH):
        q = q_ref[2 * g : 2 * g + 2].reshape(128, HD)
        loads[2 * g].wait()
        s = lax.dot_general(q, kv[0, g], transposed, preferred_element_type=jnp.float32)
        e = lax.dot_general(q, ext[0, g], transposed, preferred_element_type=jnp.float32)
        e = e + jnp.where(z == 2 * g, bias_new, bias_plain)
        m = jnp.maximum(jnp.max(s, axis=1, keepdims=True), jnp.max(e, axis=1, keepdims=True))
        p = jnp.exp2((s - m) * (scale * LOG2E))
        pe = jnp.exp2((e - m) * (scale * LOG2E))
        total = jnp.sum(p, axis=1, keepdims=True) + jnp.sum(pe, axis=1, keepdims=True)
        loads[2 * g + 1].wait()
        o = jnp.dot(p.astype(jnp.bfloat16), kv[1, g], preferred_element_type=jnp.float32)
        o = o + jnp.dot(pe.astype(jnp.bfloat16), ext[1, g], preferred_element_type=jnp.float32)
        o = (o / total).astype(jnp.bfloat16)
        out_ref[2 * g, 0:64] = o[0:64]
        out_ref[2 * g + 1, 0:64] = o[64:128]
        stats = jnp.where(col == g, m * scale + jnp.log(total), stats)
    flat = stats.T[0:KVH]
    high = flat.astype(jnp.bfloat16).astype(jnp.float32)
    middle = (flat - high).astype(jnp.bfloat16).astype(jnp.float32)
    low = flat - high - middle
    place_row = lax.broadcasted_iota(jnp.int32, (EXTRA, 128), 0)
    tokens = tok_a[...].astype(jnp.float32) + tok_b[...].astype(jnp.float32)
    for g in range(KVH):
        block = jnp.where(place_row == 0, high[g : g + 1], tokens)
        block = jnp.where(place_row == 1, middle[g : g + 1], block)
        block = jnp.where(place_row == 2, low[g : g + 1], block).astype(jnp.bfloat16)
        out_ref[2 * g, 64 : 64 + EXTRA] = block
        out_ref[2 * g + 1, 64 : 64 + EXTRA] = block


def combine_kernel(token_ids, group_ids, parts_ref, out_ref, penalty_ref):
    z = lax.axis_index("ctx")
    extra = parts_ref[:, 64 : 64 + EXTRA].astype(jnp.float32)
    logs = extra[:, 0] + extra[:, 1] + extra[:, 2]
    weights = jnp.exp(logs - jnp.max(logs, axis=0, keepdims=True))
    weights = weights / jnp.sum(weights, axis=0, keepdims=True)
    weights = jnp.where(z % 2 == 1, pltpu.roll(weights, 64, 1), weights)
    by_row = weights.T[0:64]
    mixed = jnp.zeros((64, HD), jnp.float32)
    for source in range(16):
        mixed = mixed + by_row[:, source : source + 1] * parts_ref[source, 0:64].astype(jnp.float32)
    out_ref[...] = mixed.astype(jnp.bfloat16)

    all_tokens = extra[:, 3] * 65536.0 + extra[:, 4] * 256.0 + extra[:, 5]
    all_groups = extra[:, 6]
    used = lax.broadcasted_iota(jnp.int32, (16, 128), 1) < 32
    beam = lax.broadcasted_iota(jnp.int32, (16, 128), 0)
    counts = jnp.zeros((16, 128), jnp.float32)
    for b in range(16):
        token = token_ids[b].astype(jnp.float32)
        group = group_ids[b].astype(jnp.float32)
        same = used & (all_tokens == token) & (all_groups < group)
        count = jnp.sum(jnp.where(same, PENALTY_WEIGHT, 0.0), axis=0, keepdims=True)
        counts = jnp.where(beam == b, count, counts)
    penalty_ref[...] = jnp.sum(counts.T, axis=0, keepdims=True)


def within_plane(block, flip):
    pairs = [(z * 32 + b, z * 32 + (b ^ (2 * z) ^ flip)) for z in range(16) for b in range(32)]
    return lax.ppermute(block, ("ctx", "beam"), pairs)


def body(queries, prompt_kv, suffix_kv, new_kv, parents, lengths, token_ids, group_ids):
    vmem = pl.BlockSpec(memory_space=pltpu.VMEM)
    smem = pl.BlockSpec(memory_space=pltpu.SMEM)
    hbm = pl.BlockSpec(memory_space=pl.ANY)

    suffix = suffix_kv.reshape(1, 2, 16, 32, HD)
    with jax.named_scope("suffix_x"):
        across = lax.ppermute(suffix, "beam", [(i, i ^ 2) for i in range(32)])
    own = queries.reshape(1, 64, HD)
    with jax.named_scope("queries_to_all"):
        everyone = lax.all_to_all(
            jnp.broadcast_to(own, (16, 64, HD)), "ctx", 0, 0, tiled=True
        )
    rows_a, rows_b = pl.pallas_call(
        token_rows_kernel,
        out_shape=(jax.ShapeDtypeStruct((EXTRA, 128), jnp.bfloat16),) * 2,
        in_specs=[smem, smem],
        out_specs=(vmem, vmem),
        compiler_params=pltpu.CompilerParams(vmem_limit_bytes=2**20),
        name="token_rows",
    )(token_ids, group_ids)
    by_head = pl.pallas_call(
        by_head_kernel,
        out_shape=jax.ShapeDtypeStruct((12, KVH, 1024, HD), jnp.bfloat16),
        in_specs=[hbm],
        out_specs=hbm,
        scratch_shapes=[
            pltpu.VMEM((2, 1024, KVH, HD), jnp.bfloat16),
            pltpu.VMEM((2, KVH, 1024, HD), jnp.bfloat16),
            pltpu.SemaphoreType.DMA((8,)),
            pltpu.SemaphoreType.DMA((8,)),
        ],
        compiler_params=pltpu.CompilerParams(vmem_limit_bytes=57 * 2**20),
        cost_estimate=pl.CostEstimate(flops=0, bytes_accessed=8_000_000, transcendentals=0),
        name="prompt_by_head",
    )(prompt_kv)
    with jax.named_scope("tokens_plane"):
        tok_a = within_plane(rows_a, 0)
        tok_b = within_plane(rows_b, 1)
    with jax.named_scope("suffix_core"):
        across, by_head, *_ = lax.optimization_barrier((across, by_head, rows_a, rows_b))
        near = jnp.concatenate((suffix, across))
        far = lax.ppermute(near, "beam", [(i, i ^ 1) for i in range(32)])

    parts = pl.pallas_call(
        attend_kernel,
        out_shape=jax.ShapeDtypeStruct((16, 64 + EXTRA, HD), jnp.bfloat16),
        in_specs=[hbm, hbm, vmem, hbm, vmem, vmem, hbm, vmem, vmem],
        out_specs=vmem,
        scratch_shapes=[
            pltpu.VMEM((2, KVH, 1024, HD), jnp.bfloat16),
            pltpu.VMEM((2, 512, HD), jnp.bfloat16),
            pltpu.VMEM((2, KVH, 128, HD), jnp.bfloat16),
            pltpu.VMEM((2, 128, HD), jnp.bfloat16),
            pltpu.SMEM((16,), jnp.int32),
            pltpu.SMEM((16,), jnp.int32),
            pltpu.SemaphoreType.DMA((2, KVH)),
            pltpu.SemaphoreType.DMA((3,)),
        ],
        compiler_params=pltpu.CompilerParams(vmem_limit_bytes=40 * 2**20),
        cost_estimate=pl.CostEstimate(
            flops=600_000_000, bytes_accessed=6_000_000, transcendentals=1_200_000
        ),
        name="attend",
    )(parents, lengths, everyone, by_head, near, far, new_kv.reshape(2, 128, HD), tok_a, tok_b)

    with jax.named_scope("parts_home"):
        parts = lax.all_to_all(parts, "ctx", 0, 0, tiled=True)
    attended, penalty = pl.pallas_call(
        combine_kernel,
        out_shape=(
            jax.ShapeDtypeStruct((64, HD), jnp.bfloat16),
            jax.ShapeDtypeStruct((1, 16), jnp.float32),
        ),
        in_specs=[smem, smem, vmem],
        out_specs=(vmem, vmem),
        compiler_params=pltpu.CompilerParams(vmem_limit_bytes=4 * 2**20),
        name="combine",
    )(token_ids, group_ids, parts)
    return (attended.reshape(16, 4, HD), penalty.reshape(16))


def solution(mesh):
    in_specs = (
        P("beam", "ctx", None),
        P(None, "ctx", None, None),
        P(None, "beam", "ctx", None, None),
        P(None, "beam", None, None),
        P("beam"),
        P("beam"),
        P("beam"),
        P("beam"),
    )
    out_specs = (P("beam", "ctx", None), P("beam"))
    return jax.shard_map(body, mesh=mesh, in_specs=in_specs, out_specs=out_specs, check_vma=False)
```

time: 79.7 us -> 84.6 us (1.061)
  the two profiles are of different devices: /device:TPU:12 before, /device:TPU:32 now
where the time goes in v2:
time: 84.6 us; the launch traced here: 84.1 us
  blocking collectives  37.4 us (44%)
  starting transfers between devices  26.2 us (31%)
  Pallas kernels  13.2 us (16%)
  waiting for transfers between devices  4.84 us (6%)
  local copies, waits for them, and re-layouts  1.62 us (2%)
    all_to_all x1, blocking collectives, body(): parts = lax.all_to_all(parts, 'ctx', 0, 0, tiled=True)  37.4 us
    all_to_all x1, starting transfers between devices, body(): lax.all_to_all(jnp.broadcast_to(own, (16, 64, HD)), 'ctx', 0, 0, tiled=True)  15.2 us
    pallas_call x1, Pallas kernels, body(): pl.pallas_call(attend_kernel, out_shape=jax.ShapeDtypeStruct((16, 64 + EX...  7.34 us
    ppermute x2, starting transfers between devices, within_plane(): return lax.ppermute(block, ('ctx', 'beam'), pairs)  5.67 us
    ppermute x1, starting transfers between devices, body(): across = lax.ppermute(suffix, 'beam', [(i, i ^ 2) for i in range(32)])  3.39 us
    pallas_call x1, Pallas kernels, body(): pl.pallas_call(by_head_kernel, out_shape=jax.ShapeDtypeStruct((12, KVH, 1...  3.37 us
    ppermute x2, waiting for transfers between devices, within_plane(): return lax.ppermute(block, ('ctx', 'beam'), pairs)  2.62 us
    ppermute x1, waiting for transfers between devices, body(): across = lax.ppermute(suffix, 'beam', [(i, i ^ 2) for i in range(32)])  2.21 us
  transfers between devices with their start and end apart: 5, of which 2 were waited for; matrix products, arithmetic and copies ran while one was open for 0% of the time, Pallas kernels for 5%

profile of v2, /device:TPU:32, one launch (start us, length us, event | category | flops | bytes accessed | tf_op | source)
XLA Modules:
  0.0 84.1 jit_solution(16325563958632735524)
XLA Ops:
  0.6 0.0 copy-start.5
  0.6 0.0 copy-start.4
  0.7 0.0 copy-start.3
  0.7 0.0 copy-start.2
  0.7 0.0 copy-start.1
  0.7 0.0 copy-start
  0.7 1.6 %broadcast_in_dim.8 = bf16[16,64,128]{2,1,0:T(8,128)(2,1)} broadcast(bf16[64,128]{1,0:T(8,128)(2,1)} %bitcast.8), dimensions={1,2} | broadcast | bytes 278528 | tf_op jit(solution)/shard_map/queries_to_all/broadcast_in_dim | solution.py:199
  2.3 15.2 %all-to-all-start = ((bf16[16,64,128]{2,1,0:T(8,128)(2,1)}), bf16[16,64,128]{2,1,0:T(8,128)(2,1)S(1)}, u32[]{:S(2)}, u32[]{:S(2)}) async-start(bf16[16,64,128]{2,1,0:T(8,128)(2,1)} %broadcast_in_dim.8), calls=%async_computation | async-start | bytes 524288 | tf_op jit(solution)/shard_map/queries_to_all/all_to_all | solution.py:198
  17.5 3.4 %collective-permute-start = (bf16[1,2,16,32,128]{4,3,2,1,0:T(8,128)(2,1)}, bf16[1,2,16,32,128]{4,3,2,1,0:T(8,128)(2,1)S(1)}, u32[]{:S(2)}, u32[]{:S(2)}) collective-permute-start(bf16[1,2,16,32,128]{4,3,2,1,0:T(8,128)(2,1)} %bitcast.6), channel_id=1, source_target_pairs={{0,2},{1,3},{2,0},{3,1},{4,6},{5,7},{6,4},{7,5},{8,10},{9,11},{10,... | collective-permute-start | bytes 786440 | tf_op jit(solution)/shard_map/suffix_x/ppermute | solution.py:195
  20.9 3.4 %prompt_by_head.1.kv_ref = bf16[12,8,1024,128]{3,2,1,0:T(8,128)(2,1)} custom-call(bf16[2,1024,8,128]{3,2,1,0:T(8,128)(2,1)} %kv_ref.1), custom_call_target="tpu_custom_call" | custom-call | bytes 8000000 | tf_op jit(solution)/shard_map/prompt_by_head/pallas_call | solution.py:209
  24.3 0.0 copy-done.4
  24.3 0.0 copy-done.3
  24.3 0.6 token_rows.1
  24.9 2.2 %collective-permute-done = bf16[1,2,16,32,128]{4,3,2,1,0:T(8,128)(2,1)S(1)} collective-permute-done((bf16[1,2,16,32,128]{4,3,2,1,0:T(8,128)(2,1)}, bf16[1,2,16,32,128]{4,3,2,1,0:T(8,128)(2,1)S(1)}, u32[]{:S(2)}, u32[]{:S(2)}) %collective-permute-start) | collective-permute-done | bytes 262176 | tf_op jit(solution)/shard_map/suffix_x/ppermute | solution.py:195
  27.1 0.0 copy-done.5
  27.1 0.1 pad_maximum_fusion.near
  27.1 1.9 %collective-permute-start.1 = (bf16[2,2,16,32,128]{4,3,2,1,0:T(8,128)(2,1)S(1)}, bf16[2,2,16,32,128]{4,3,2,1,0:T(8,128)(2,1)S(1)}, u32[]{:S(2)}, u32[]{:S(2)}) collective-permute-start(bf16[2,2,16,32,128]{4,3,2,1,0:T(8,128)(2,1)S(1)} %pad_maximum_fusion.near), channel_id=1, source_target_pairs={{0,1},{1,0},{2,3},{3,2},{4,5},{5,4},{6,7},{7,6},{8,9},{9,8},{10,11... | collective-permute-start | bytes 1572872 | tf_op jit(solution)/shard_map/suffix_core/ppermute | solution.py:230
  29.1 3.4 %collective-permute-start.2 = (bf16[8,128]{1,0:T(8,128)(2,1)S(1)}, bf16[8,128]{1,0:T(8,128)(2,1)S(1)}, u32[]{:S(2)}, u32[]{:S(2)}) collective-permute-start(bf16[8,128]{1,0:T(8,128)(2,1)S(1)} %get-tuple-element.8), channel_id=1, source_target_pairs={{0,0},{1,1},{2,2},{3,3},{4,4},{5,5},{6,6},{7,7},{8,8},{9,9},{10,10... | collective-permute-start | bytes 6152 | tf_op jit(solution)/shard_map/tokens_plane/ppermute | solution.py:185
  32.5 2.3 %collective-permute-start.3 = (bf16[8,128]{1,0:T(8,128)(2,1)S(1)}, bf16[8,128]{1,0:T(8,128)(2,1)S(1)}, u32[]{:S(2)}, u32[]{:S(2)}) collective-permute-start(bf16[8,128]{1,0:T(8,128)(2,1)S(1)} %get-tuple-element.9), channel_id=1, source_target_pairs={{0,1},{1,0},{2,3},{3,2},{4,5},{5,4},{6,7},{7,6},{8,9},{9,8},{10,11... | collective-permute-start | bytes 6152 | tf_op jit(solution)/shard_map/tokens_plane/ppermute | solution.py:185
  34.7 0.0 collective-permute-done.2.tok_a
  34.8 2.6 %collective-permute-done.3.tok_b = bf16[8,128]{1,0:T(8,128)(2,1)S(1)} collective-permute-done((bf16[8,128]{1,0:T(8,128)(2,1)S(1)}, bf16[8,128]{1,0:T(8,128)(2,1)S(1)}, u32[]{:S(2)}, u32[]{:S(2)}) %collective-permute-start.3) | collective-permute-done | bytes 2080 | tf_op jit(solution)/shard_map/tokens_plane/ppermute | solution.py:185
  37.4 0.0 collective-permute-done.1.far
  37.4 0.0 all-to-all-done.q_ref
  37.4 0.0 copy-done.2
  37.4 0.0 copy-done.1
  37.4 0.0 copy-done
  37.4 7.3 %attend.1 = bf16[16,72,128]{2,1,0:T(8,128)(2,1)S(1)} custom-call(s32[16]{0:T(128)S(1)} %copy-done.1, s32[16]{0:T(128)S(1)} %copy-done.2, bf16[16,64,128]{2,1,0:T(8,128)(2,1)S(1)} %all-to-all-done.q_ref, bf16[12,8,1024,128]{3,2,1,0:T(8,128)(2,1)} %prompt_by_head.1.kv_ref, bf16[2,2,16,32,128]{4,3,2,1,0:T(8,128)(2,1)S(1)} %pad_maximum_fusion.near, ...), custom_call_target="tpu_custom_call" | custom-call | flops 600000000 | bytes 6000000 | tf_op jit(solution)/shard_map/attend/pallas_call | solution.py:232
  44.8 37.4 %all_to_all.10.parts_ref = bf16[16,72,128]{2,1,0:T(8,128)(2,1)S(1)} all-to-all(bf16[16,72,128]{2,1,0:T(8,128)(2,1)S(1)} %attend.1), channel_id=1, replica_groups=mesh['ctx'=16,'beam'=32] {'ctx'}, dimensions={0} | all-to-all | bytes 589824 | tf_op jit(solution)/shard_map/parts_home/all_to_all | solution.py:255
  82.1 2.0 %combine.1 = (bf16[64,128]{1,0:T(8,128)(2,1)}, f32[1,16]{1,0:T(1,128)}) custom-call(s32[16]{0:T(128)S(1)} %copy-done.3, s32[16]{0:T(128)S(1)} %copy-done.4, bf16[16,72,128]{2,1,0:T(8,128)(2,1)S(1)} %all_to_all.10.parts_ref), custom_call_target="tpu_custom_call" | custom-call | tf_op jit(solution)/shard_map/combine/pallas_call | solution.py:256
Async XLA Ops:
  0.6 26.4 %copy-start.5 = (bf16[2,16,4,8,128]{4,3,2,1,0:T(8,128)(2,1)S(1)}, bf16[2,16,4,8,128]{4,3,2,1,0:T(8,128)(2,1)}, u32[]{:S(2)}) copy-start(bf16[2,16,4,8,128]{4,3,2,1,0:T(8,128)(2,1)} %param.10) | copy-start | bytes 786436
  0.6 23.6 %copy-start.4 = (s32[16]{0:T(128)S(1)}, s32[16]{0:T(128)}, u32[]{:S(2)}) copy-start(s32[16]{0:T(128)} %group_ids.3) | copy-start | bytes 196
  0.7 23.6 %copy-start.3 = (s32[16]{0:T(128)S(1)}, s32[16]{0:T(128)}, u32[]{:S(2)}) copy-start(s32[16]{0:T(128)} %token_ids.3) | copy-start | bytes 196
  0.7 36.7 %copy-start.2 = (s32[16]{0:T(128)S(1)}, s32[16]{0:T(128)}, u32[]{:S(2)}) copy-start(s32[16]{0:T(128)} %lengths_ref.1) | copy-start | bytes 196
  0.7 36.7 %copy-start.1 = (s32[16]{0:T(128)S(1)}, s32[16]{0:T(128)}, u32[]{:S(2)}) copy-start(s32[16]{0:T(128)} %parents_ref.1) | copy-start | bytes 196
  0.7 36.7 %copy-start = (bf16[2,16,8,128]{3,2,1,0:T(8,128)(2,1)S(1)}, bf16[2,16,8,128]{3,2,1,0:T(8,128)(2,1)}, u32[]{:S(2)}) copy-start(bf16[2,16,8,128]{3,2,1,0:T(8,128)(2,1)} %param.11) | copy-start | bytes 196612
  2.3 35.1 %all-to-all-start = ((bf16[16,64,128]{2,1,0:T(8,128)(2,1)}), bf16[16,64,128]{2,1,0:T(8,128)(2,1)S(1)}, u32[]{:S(2)}, u32[]{:S(2)}) async-start(bf16[16,64,128]{2,1,0:T(8,128)(2,1)} %broadcast_in_dim.8), calls=%async_computation | async-start | bytes 524288 | tf_op jit(solution)/shard_map/queries_to_all/all_to_all | solution.py:198
  17.5 9.6 %collective-permute-start = (bf16[1,2,16,32,128]{4,3,2,1,0:T(8,128)(2,1)}, bf16[1,2,16,32,128]{4,3,2,1,0:T(8,128)(2,1)S(1)}, u32[]{:S(2)}, u32[]{:S(2)}) collective-permute-start(bf16[1,2,16,32,128]{4,3,2,1,0:T(8,128)(2,1)} %bitcast.6), channel_id=1, source_target_pairs={{0,2},{1,3},{2,0},{3,1},{4,6},{5,7},{6,4},{7,5},{8,10},{9,11},{10,... | collective-permute-start | bytes 786440 | tf_op jit(solution)/shard_map/suffix_x/ppermute | solution.py:195
  27.1 10.2 %collective-permute-start.1 = (bf16[2,2,16,32,128]{4,3,2,1,0:T(8,128)(2,1)S(1)}, bf16[2,2,16,32,128]{4,3,2,1,0:T(8,128)(2,1)S(1)}, u32[]{:S(2)}, u32[]{:S(2)}) collective-permute-start(bf16[2,2,16,32,128]{4,3,2,1,0:T(8,128)(2,1)S(1)} %pad_maximum_fusion.near), channel_id=1, source_target_pairs={{0,1},{1,0},{2,3},{3,2},{4,5},{5,4},{6,7},{7,6},{8,9},{9,8},{10,11... | collective-permute-start | bytes 1572872 | tf_op jit(solution)/shard_map/suffix_core/ppermute | solution.py:230
  29.1 5.7 %collective-permute-start.2 = (bf16[8,128]{1,0:T(8,128)(2,1)S(1)}, bf16[8,128]{1,0:T(8,128)(2,1)S(1)}, u32[]{:S(2)}, u32[]{:S(2)}) collective-permute-start(bf16[8,128]{1,0:T(8,128)(2,1)S(1)} %get-tuple-element.8), channel_id=1, source_target_pairs={{0,0},{1,1},{2,2},{3,3},{4,4},{5,5},{6,6},{7,7},{8,8},{9,9},{10,10... | collective-permute-start | bytes 6152 | tf_op jit(solution)/shard_map/tokens_plane/ppermute | solution.py:185
  32.5 4.9 %collective-permute-start.3 = (bf16[8,128]{1,0:T(8,128)(2,1)S(1)}, bf16[8,128]{1,0:T(8,128)(2,1)S(1)}, u32[]{:S(2)}, u32[]{:S(2)}) collective-permute-start(bf16[8,128]{1,0:T(8,128)(2,1)S(1)} %get-tuple-element.9), channel_id=1, source_target_pairs={{0,1},{1,0},{2,3},{3,2},{4,5},{5,4},{6,7},{7,6},{8,9},{9,8},{10,11... | collective-permute-start | bytes 6152 | tf_op jit(solution)/shard_map/tokens_plane/ppermute | solution.py:185

commit v3 on v1

v3 whole, which is shorter than its diff:
```python
import jax
import jax.numpy as jnp
from jax import lax
from jax.experimental import pallas as pl
from jax.experimental.pallas import tpu as pltpu
from jax.sharding import PartitionSpec as P

HEADS = 64
KVH = 8
HD = 128
FAMILY_DEVICES = 4
PENALTY_WEIGHT = 0.5
FAR_BELOW = -1e30
LOG2E = 1.4426950408889634
EXTRA = 8


def rows_by_head():
    row = lax.broadcasted_iota(jnp.int32, (128, 128), 0)
    col = lax.broadcasted_iota(jnp.int32, (128, 128), 1)
    hit = (row // 16 == col % KVH) & (row % 16 == col // KVH)
    return jnp.where(hit, 1.0, 0.0).astype(jnp.bfloat16)


def token_rows_kernel(scalars, rows_a, rows_b):
    row = lax.broadcasted_iota(jnp.int32, (EXTRA, 128), 0)
    lane = lax.broadcasted_iota(jnp.int32, (EXTRA, 128), 1)
    for rows_ref, first_lane in ((rows_a, 0), (rows_b, 16)):
        tokens = jnp.zeros((EXTRA, 128), jnp.int32)
        groups = jnp.zeros((EXTRA, 128), jnp.int32)
        for b in range(16):
            tokens = jnp.where(lane == first_lane + b, scalars[b], tokens)
            groups = jnp.where(lane == first_lane + b, scalars[16 + b], groups)
        digits = jnp.where(row == 3, tokens >> 16, 0)
        digits = jnp.where(row == 4, (tokens >> 8) & 255, digits)
        digits = jnp.where(row == 5, tokens & 255, digits)
        digits = jnp.where(row == 6, groups, digits)
        digits = jnp.concatenate((digits, jnp.zeros_like(digits)))
        rows_ref[...] = digits.astype(jnp.float32).astype(jnp.bfloat16)


def prepare_kernel(scalars, new_ref, new_rows_ref, bias_ref):
    z = lax.axis_index("ctx")
    by_head = rows_by_head()
    for c in range(2):
        moved = jnp.dot(by_head, new_ref[c], preferred_element_type=jnp.float32)
        new_rows_ref[c] = moved.astype(jnp.bfloat16)

    row = lax.broadcasted_iota(jnp.int32, (128, 128), 0)
    col = lax.broadcasted_iota(jnp.int32, (128, 128), 1)
    row_beam = (row % 64) // 4
    live = jnp.zeros((128, 128), jnp.int32)
    for b in range(16):
        live = jnp.where(row_beam == b, scalars[32 + b], live)
    on_suffix = (col < 64) & (col // 4 == row_beam) & (z * 4 + col % 4 < live)
    on_new = (col >= 64) & (col - 64 == row_beam)
    bias_ref[0] = jnp.where(on_suffix, 0.0, FAR_BELOW)
    bias_ref[1] = jnp.where(on_suffix | on_new, 0.0, FAR_BELOW)


def attend_kernel(
    scalars, q_ref, kv_ref, near, far, new_rows, bias_ref, out_ref,
    natural, kv, picked, ext, sems,
):
    beams = 16
    z = lax.axis_index("ctx")
    place = lax.axis_index("beam") % FAMILY_DEVICES
    scale = HD**-0.5

    step = 256
    chunks = [(c, pl.ds(first, step)) for c in range(2) for first in range(0, 1024, step)]
    loads = [
        pltpu.make_async_copy(kv_ref.at[c, rows], natural.at[c, rows], sems.at[n])
        for n, (c, rows) in enumerate(chunks)
    ]
    for load in loads:
        load.start()

    for b in range(beams):
        parent = scalars[48 + b]
        slot = lax.bitwise_xor((parent // beams) % FAMILY_DEVICES, place)
        local = parent % beams
        for k, held in enumerate((near, far)):

            @pl.when(slot % 2 == k)
            def _(held=held, local=local, slot=slot, b=b):
                for c in range(2):
                    first = pl.multiple_of((slot // 2 * 2 + c) * 512 + local * 32, 32)
                    picked[c, pl.ds(b * 32, 32)] = held[pl.ds(first, 32)]

    by_head = rows_by_head()
    for c in range(2):
        ext[c, :, 80:128] = jnp.zeros((KVH, 48, HD), jnp.bfloat16)
        for g in range(KVH):
            ext[c, g, 64:80] = new_rows[c, g * 16 : (g + 1) * 16]
        for part in range(4):
            rows = picked[c, pl.ds(part * 128, 128)]
            moved = jnp.dot(by_head, rows, preferred_element_type=jnp.float32).astype(jnp.bfloat16)
            for g in range(KVH):
                ext[c, g, pl.ds(part * 16, 16)] = moved[g * 16 : (g + 1) * 16]

    for (c, rows), load in zip(chunks, loads):
        load.wait()
        for first in range(rows.start, rows.start + step, 64):
            part = pl.ds(first, 64)
            kv[c, :, part] = jnp.swapaxes(natural[c, part], 0, 1)

    transposed = (((1,), (1,)), ((), ()))
    col = lax.broadcasted_iota(jnp.int32, (128, 128), 1)
    stats = jnp.zeros((128, 128), jnp.float32)
    for g in range(KVH):
        q = q_ref[2 * g : 2 * g + 2].reshape(128, HD)
        s = lax.dot_general(q, kv[0, g], transposed, preferred_element_type=jnp.float32)
        e = lax.dot_general(q, ext[0, g], transposed, preferred_element_type=jnp.float32)
        e = e + bias_ref[jnp.where(z == 2 * g, 1, 0)]
        m = jnp.maximum(jnp.max(s, axis=1, keepdims=True), jnp.max(e, axis=1, keepdims=True))
        p = jnp.exp2((s - m) * (scale * LOG2E))
        pe = jnp.exp2((e - m) * (scale * LOG2E))
        total = jnp.sum(p, axis=1, keepdims=True) + jnp.sum(pe, axis=1, keepdims=True)
        o = jnp.dot(p.astype(jnp.bfloat16), kv[1, g], preferred_element_type=jnp.float32)
        o = o + jnp.dot(pe.astype(jnp.bfloat16), ext[1, g], preferred_element_type=jnp.float32)
        o = (o / total).astype(jnp.bfloat16)
        out_ref[2 * g, 0:64] = o[0:64]
        out_ref[2 * g + 1, 0:64] = o[64:128]
        stats = jnp.where(col == g, m * scale + jnp.log(total), stats)
    flat = stats.T[0:KVH]
    high = flat.astype(jnp.bfloat16).astype(jnp.float32)
    middle = (flat - high).astype(jnp.bfloat16).astype(jnp.float32)
    low = flat - high - middle
    place_row = lax.broadcasted_iota(jnp.int32, (EXTRA, 128), 0)
    for g in range(KVH):
        block = jnp.where(place_row == 0, high[g : g + 1], 0.0)
        block = jnp.where(place_row == 1, middle[g : g + 1], block)
        block = jnp.where(place_row == 2, low[g : g + 1], block).astype(jnp.bfloat16)
        out_ref[2 * g, 64 : 64 + EXTRA] = block
        out_ref[2 * g + 1, 64 : 64 + EXTRA] = block


def insert_kernel(tokens_ref, parts_ref, out_ref):
    row = lax.broadcasted_iota(jnp.int32, (EXTRA, 128), 0)
    tokens = tokens_ref[0:EXTRA].astype(jnp.float32)
    for target in range(16):
        spare = parts_ref[target, 64 : 64 + EXTRA].astype(jnp.float32)
        out_ref[target, 64 : 64 + EXTRA] = jnp.where(row < 3, spare, tokens).astype(jnp.bfloat16)


def combine_kernel(scalars, parts_ref, out_ref, penalty_ref):
    z = lax.axis_index("ctx")
    extra = parts_ref[:, 64 : 64 + EXTRA].astype(jnp.float32)
    logs = extra[:, 0] + extra[:, 1] + extra[:, 2]
    weights = jnp.exp(logs - jnp.max(logs, axis=0, keepdims=True))
    weights = weights / jnp.sum(weights, axis=0, keepdims=True)
    weights = jnp.where(z % 2 == 1, pltpu.roll(weights, 64, 1), weights)
    by_row = weights.T[0:64]
    mixed = jnp.zeros((64, HD), jnp.float32)
    for source in range(16):
        mixed = mixed + by_row[:, source : source + 1] * parts_ref[source, 0:64].astype(jnp.float32)
    out_ref[...] = mixed.astype(jnp.bfloat16)

    all_tokens = extra[:, 3] * 65536.0 + extra[:, 4] * 256.0 + extra[:, 5]
    all_groups = extra[:, 6]
    used = lax.broadcasted_iota(jnp.int32, (16, 128), 1) < 32
    beam = lax.broadcasted_iota(jnp.int32, (16, 128), 0)
    counts = jnp.zeros((16, 128), jnp.float32)
    for b in range(16):
        token = scalars[b].astype(jnp.float32)
        group = scalars[16 + b].astype(jnp.float32)
        same = used & (all_tokens == token) & (all_groups < group)
        count = jnp.sum(jnp.where(same, PENALTY_WEIGHT, 0.0), axis=0, keepdims=True)
        counts = jnp.where(beam == b, count, counts)
    penalty_ref[...] = jnp.sum(counts.T, axis=0, keepdims=True)


def within_plane(block):
    pairs = [(z * 32 + b, z * 32 + (b ^ (2 * z))) for z in range(16) for b in range(32)]
    return lax.ppermute(block, ("ctx", "beam"), pairs)


def body(queries, prompt_kv, suffix_kv, new_kv, parents, lengths, token_ids, group_ids):
    vmem = pl.BlockSpec(memory_space=pltpu.VMEM)
    smem = pl.BlockSpec(memory_space=pltpu.SMEM)
    hbm = pl.BlockSpec(memory_space=pl.ANY)

    with jax.named_scope("queries_to_all"):
        sent = jnp.broadcast_to(queries.reshape(1, 64, HD), (16, 64, HD))
        everyone = lax.all_to_all(sent, "ctx", 0, 0, tiled=True)
    scalars = jnp.concatenate((token_ids, group_ids, lengths, parents))
    rows_a, rows_b = pl.pallas_call(
        token_rows_kernel,
        out_shape=(jax.ShapeDtypeStruct((2 * EXTRA, 128), jnp.bfloat16),) * 2,
        in_specs=[smem],
        out_specs=(vmem,) * 2,
        compiler_params=pltpu.CompilerParams(vmem_limit_bytes=2**20),
        name="token_rows",
    )(scalars)
    new_rows, bias = pl.pallas_call(
        prepare_kernel,
        out_shape=(
            jax.ShapeDtypeStruct((2, 128, HD), jnp.bfloat16),
            jax.ShapeDtypeStruct((2, 128, 128), jnp.float32),
        ),
        in_specs=[smem, vmem],
        out_specs=(vmem,) * 2,
        compiler_params=pltpu.CompilerParams(vmem_limit_bytes=4 * 2**20),
        name="prepare",
    )(scalars, new_kv.reshape(2, 128, HD))
    suffix = suffix_kv.reshape(1024, HD)
    with jax.named_scope("suffix_x"):
        across = lax.ppermute(suffix, "beam", [(i, i ^ 2) for i in range(32)])
    across, rows_b, new_rows, bias = lax.optimization_barrier((across, rows_b, new_rows, bias))
    with jax.named_scope("suffix_core"):
        near = jnp.concatenate((suffix, across, rows_b))
        far = lax.ppermute(near, "beam", [(i, i ^ 1) for i in range(32)])
    with jax.named_scope("tokens_plane"):
        plane = within_plane(rows_a + far[2048:])

    parts = pl.pallas_call(
        attend_kernel,
        out_shape=jax.ShapeDtypeStruct((16, 64 + EXTRA, HD), jnp.bfloat16),
        in_specs=[smem, vmem, hbm] + [vmem] * 4,
        out_specs=vmem,
        scratch_shapes=[
            pltpu.VMEM((2, 1024, KVH, HD), jnp.bfloat16),
            pltpu.VMEM((2, KVH, 1024, HD), jnp.bfloat16),
            pltpu.VMEM((2, 512, HD), jnp.bfloat16),
            pltpu.VMEM((2, KVH, 128, HD), jnp.bfloat16),
            pltpu.SemaphoreType.DMA((8,)),
        ],
        compiler_params=pltpu.CompilerParams(vmem_limit_bytes=51 * 2**20),
        cost_estimate=pl.CostEstimate(
            flops=600_000_000, bytes_accessed=6_000_000, transcendentals=1_200_000
        ),
        name="attend",
    )(scalars, everyone, prompt_kv, near, far, new_rows, bias)

    parts, plane = lax.optimization_barrier((parts, plane))
    parts = pl.pallas_call(
        insert_kernel,
        out_shape=jax.ShapeDtypeStruct(parts.shape, parts.dtype),
        in_specs=[vmem, vmem],
        out_specs=vmem,
        input_output_aliases={1: 0},
        compiler_params=pltpu.CompilerParams(vmem_limit_bytes=2 * 2**20),
        name="insert",
    )(plane, parts)
    with jax.named_scope("parts_home"):
        parts = lax.all_to_all(parts, "ctx", 0, 0, tiled=True)
    attended, penalty = pl.pallas_call(
        combine_kernel,
        out_shape=(
            jax.ShapeDtypeStruct((64, HD), jnp.bfloat16),
            jax.ShapeDtypeStruct((1, 16), jnp.float32),
        ),
        in_specs=[smem, vmem],
        out_specs=(vmem, vmem),
        compiler_params=pltpu.CompilerParams(vmem_limit_bytes=4 * 2**20),
        name="combine",
    )(scalars, parts)
    return (attended.reshape(16, 4, HD), penalty.reshape(16))


def solution(mesh):
    in_specs = (
        P("beam", "ctx", None),
        P(None, "ctx", None, None),
        P(None, "beam", "ctx", None, None),
        P(None, "beam", None, None),
        P("beam"),
        P("beam"),
        P("beam"),
        P("beam"),
    )
    out_specs = (P("beam", "ctx", None), P("beam"))
    return jax.shard_map(body, mesh=mesh, in_specs=in_specs, out_specs=out_specs, check_vma=False)
```

time: 79.7 us -> 72.4 us (0.908)
  the two profiles are of different devices: /device:TPU:12 before, /device:TPU:64 now
where the time goes in v3:
time: 72.4 us; the launch traced here: 71.9 us
  blocking collectives  25.3 us (35%)
  starting transfers between devices  24.8 us (34%)
  Pallas kernels  9.26 us (13%)
  waiting for transfers between devices  8.7 us (12%)
  local copies, waits for them, and re-layouts  2.31 us (3%)
  other arithmetic  0.82 us (1%)
    all_to_all x1, blocking collectives, body(): parts = lax.all_to_all(parts, 'ctx', 0, 0, tiled=True)  25.3 us
    all_to_all x1, starting transfers between devices, body(): everyone = lax.all_to_all(sent, 'ctx', 0, 0, tiled=True)  14.8 us
    all_to_all x1, waiting for transfers between devices, body(): everyone = lax.all_to_all(sent, 'ctx', 0, 0, tiled=True)  6.81 us
    pallas_call x1, Pallas kernels, body(): pl.pallas_call(attend_kernel, out_shape=jax.ShapeDtypeStruct((16, 64 + EX...  6.02 us
    ppermute x1, starting transfers between devices, within_plane(): return lax.ppermute(block, ('ctx', 'beam'), pairs)  4.63 us
    ppermute x1, starting transfers between devices, body(): across = lax.ppermute(suffix, 'beam', [(i, i ^ 2) for i in range(32)])  3.53 us
    pallas_call x1, Pallas kernels, body(): pl.pallas_call(combine_kernel, out_shape=(jax.ShapeDtypeStruct((64, HD),...  1.95 us
    ppermute x1, starting transfers between devices, body(): far = lax.ppermute(near, 'beam', [(i, i ^ 1) for i in range(32)])  1.92 us
  transfers between devices with their start and end apart: 4, of which 2 were waited for; matrix products, arithmetic and copies ran while one was open for 3% of the time, Pallas kernels for 10%

profile of v3, /device:TPU:64, one launch (start us, length us, event | category | flops | bytes accessed | tf_op | source)
XLA Modules:
  0.0 71.9 jit_solution(5850246291402972102)
XLA Ops:
  0.6 0.0 copy-start.1
  0.6 3.5 %collective-permute-start = (bf16[1024,128]{1,0:T(8,128)(2,1)}, bf16[1024,128]{1,0:T(8,128)(2,1)S(1)}, u32[]{:S(2)}, u32[]{:S(2)}) collective-permute-start(bf16[1024,128]{1,0:T(8,128)(2,1)} %bitcast.6), channel_id=1, source_target_pairs={{0,2},{1,3},{2,0},{3,1},{4,6},{5,7},{6,4},{7,5},{8,10},{9,11},{10,... | collective-permute-start | bytes 786440 | tf_op jit(solution)/shard_map/suffix_x/ppermute | solution.py:209
  4.2 1.5 %broadcast_in_dim.8 = bf16[16,64,128]{2,1,0:T(8,128)(2,1)} broadcast(bf16[64,128]{1,0:T(8,128)(2,1)} %bitcast.8), dimensions={1,2} | broadcast | bytes 278528 | tf_op jit(solution)/shard_map/queries_to_all/broadcast_in_dim | solution.py:185
  5.6 14.8 %all-to-all-start = ((bf16[16,64,128]{2,1,0:T(8,128)(2,1)}), bf16[16,64,128]{2,1,0:T(8,128)(2,1)S(1)}, u32[]{:S(2)}, u32[]{:S(2)}) async-start(bf16[16,64,128]{2,1,0:T(8,128)(2,1)} %broadcast_in_dim.8), calls=%async_computation | async-start | bytes 524288 | tf_op jit(solution)/shard_map/queries_to_all/all_to_all | solution.py:186
  20.4 0.8 %pad_add_fusion.scalars = s32[64]{0:T(128)S(1)} fusion(s32[16]{0:T(128)} %param.12, s32[16]{0:T(128)} %param.13, s32[16]{0:T(128)} %param.15, s32[16]{0:T(128)} %param.14), kind=kLoop, calls=%fused_computation.2 | loop fusion | flops 192 | bytes 512 | tf_op jit(solution)/shard_map/concatenate | solution.py:187
  21.2 0.6 token_rows.1
  21.8 0.0 copy-start
  21.8 0.8 %copy-done = bf16[2,16,8,128]{3,2,1,0:T(8,128)(2,1)S(1)} copy-done((bf16[2,16,8,128]{3,2,1,0:T(8,128)(2,1)S(1)}, bf16[2,16,8,128]{3,2,1,0:T(8,128)(2,1)}, u32[]{:S(2)}) %copy-start) | copy-done | bytes 65560
  22.6 0.7 prepare.1
  23.3 0.0 collective-permute-done
  23.3 0.0 copy-done.1
  23.4 1.9 %collective-permute-start.1 = (bf16[2064,128]{1,0:T(8,128)(2,1)S(1)}, bf16[2064,128]{1,0:T(8,128)(2,1)S(1)}, u32[]{:S(2)}, u32[]{:S(2)}) collective-permute-start(bf16[2064,128]{1,0:T(8,128)(2,1)S(1)} %pad_maximum_fusion.near), channel_id=1, source_target_pairs={{0,1},{1,0},{2,3},{3,2},{4,5},{5,4},{6,7},{7,6},{8,9},{9,8},{10,11... | collective-permute-start | bytes 1585160 | tf_op jit(solution)/shard_map/suffix_core/ppermute | solution.py:213
  25.3 1.9 %collective-permute-done.1.far = bf16[2064,128]{1,0:T(8,128)(2,1)S(1)} collective-permute-done((bf16[2064,128]{1,0:T(8,128)(2,1)S(1)}, bf16[2064,128]{1,0:T(8,128)(2,1)S(1)}, u32[]{:S(2)}, u32[]{:S(2)}) %collective-permute-start.1) | collective-permute-done | bytes 528416 | tf_op jit(solution)/shard_map/suffix_core/ppermute | solution.py:213
  27.2 4.6 %collective-permute-start.2 = (bf16[16,128]{1,0:T(8,128)(2,1)S(1)}, bf16[16,128]{1,0:T(8,128)(2,1)S(1)}, u32[]{:S(2)}, u32[]{:S(2)}) collective-permute-start(bf16[16,128]{1,0:T(8,128)(2,1)S(1)} %slice_add_fusion), channel_id=1, source_target_pairs={{0,0},{1,1},{2,2},{3,3},{4,4},{5,5},{6,6},{7,7},{8,8},{9,9},{10,10... | collective-permute-start | bytes 12296 | tf_op jit(solution)/shard_map/tokens_plane/ppermute | solution.py:176
  31.8 6.8 %all-to-all-done.q_ref = bf16[16,64,128]{2,1,0:T(8,128)(2,1)S(1)} async-done(((bf16[16,64,128]{2,1,0:T(8,128)(2,1)}), bf16[16,64,128]{2,1,0:T(8,128)(2,1)S(1)}, u32[]{:S(2)}, u32[]{:S(2)}) %all-to-all-start) | async-done | bytes 262176 | tf_op jit(solution)/shard_map/queries_to_all/all_to_all | solution.py:186
  38.6 6.0 %attend.1.parts_ref = bf16[16,72,128]{2,1,0:T(8,128)(2,1)S(1)} custom-call(s32[64]{0:T(128)S(1)} %pad_add_fusion.scalars, bf16[16,64,128]{2,1,0:T(8,128)(2,1)S(1)} %all-to-all-done.q_ref, bf16[2,1024,8,128]{3,2,1,0:T(8,128)(2,1)} %kv_ref.1, bf16[2064,128]{1,0:T(8,128)(2,1)S(1)} %pad_maximum_fusion.near, bf16[2064,128]{1,0:T(8,128)(2,1)S(1)} %collective-permute-done.1.far, ...), custom_call_target="tpu_custom_call" | custom-call | flops 600000000 | bytes 6000000 | tf_op jit(solution)/shard_map/attend/pallas_call | solution.py:217
  44.7 0.0 collective-permute-done.2.tokens_ref
  44.7 25.3 %all_to_all.10.parts_ref = bf16[16,72,128]{2,1,0:T(8,128)(2,1)S(1)} all-to-all(bf16[16,72,128]{2,1,0:T(8,128)(2,1)S(1)} %insert.1), channel_id=1, replica_groups=mesh['ctx'=16,'beam'=32] {'ctx'}, dimensions={0} | all-to-all | bytes 589824 | tf_op jit(solution)/shard_map/parts_home/all_to_all | solution.py:247
  70.0 1.9 %combine.1 = (bf16[64,128]{1,0:T(8,128)(2,1)}, f32[1,16]{1,0:T(1,128)}) custom-call(s32[64]{0:T(128)S(1)} %pad_add_fusion.scalars, bf16[16,72,128]{2,1,0:T(8,128)(2,1)S(1)} %all_to_all.10.parts_ref), custom_call_target="tpu_custom_call" | custom-call | tf_op jit(solution)/shard_map/combine/pallas_call | solution.py:248
  (3 shorter events, 0.1 us)
Async XLA Ops:
  0.6 22.7 %copy-start.1 = (bf16[2,16,4,8,128]{4,3,2,1,0:T(8,128)(2,1)S(1)}, bf16[2,16,4,8,128]{4,3,2,1,0:T(8,128)(2,1)}, u32[]{:S(2)}) copy-start(bf16[2,16,4,8,128]{4,3,2,1,0:T(8,128)(2,1)} %param.10) | copy-start | bytes 786436
  0.6 22.7 %collective-permute-start = (bf16[1024,128]{1,0:T(8,128)(2,1)}, bf16[1024,128]{1,0:T(8,128)(2,1)S(1)}, u32[]{:S(2)}, u32[]{:S(2)}) collective-permute-start(bf16[1024,128]{1,0:T(8,128)(2,1)} %bitcast.6), channel_id=1, source_target_pairs={{0,2},{1,3},{2,0},{3,1},{4,6},{5,7},{6,4},{7,5},{8,10},{9,11},{10,... | collective-permute-start | bytes 786440 | tf_op jit(solution)/shard_map/suffix_x/ppermute | solution.py:209
  5.6 33.0 %all-to-all-start = ((bf16[16,64,128]{2,1,0:T(8,128)(2,1)}), bf16[16,64,128]{2,1,0:T(8,128)(2,1)S(1)}, u32[]{:S(2)}, u32[]{:S(2)}) async-start(bf16[16,64,128]{2,1,0:T(8,128)(2,1)} %broadcast_in_dim.8), calls=%async_computation | async-start | bytes 524288 | tf_op jit(solution)/shard_map/queries_to_all/all_to_all | solution.py:186
  21.8 0.8 %copy-start = (bf16[2,16,8,128]{3,2,1,0:T(8,128)(2,1)S(1)}, bf16[2,16,8,128]{3,2,1,0:T(8,128)(2,1)}, u32[]{:S(2)}) copy-start(bf16[2,16,8,128]{3,2,1,0:T(8,128)(2,1)} %param.11) | copy-start | bytes 196612
  23.4 3.8 %collective-permute-start.1 = (bf16[2064,128]{1,0:T(8,128)(2,1)S(1)}, bf16[2064,128]{1,0:T(8,128)(2,1)S(1)}, u32[]{:S(2)}, u32[]{:S(2)}) collective-permute-start(bf16[2064,128]{1,0:T(8,128)(2,1)S(1)} %pad_maximum_fusion.near), channel_id=1, source_target_pairs={{0,1},{1,0},{2,3},{3,2},{4,5},{5,4},{6,7},{7,6},{8,9},{9,8},{10,11... | collective-permute-start | bytes 1585160 | tf_op jit(solution)/shard_map/suffix_core/ppermute | solution.py:213
  27.2 17.5 %collective-permute-start.2 = (bf16[16,128]{1,0:T(8,128)(2,1)S(1)}, bf16[16,128]{1,0:T(8,128)(2,1)S(1)}, u32[]{:S(2)}, u32[]{:S(2)}) collective-permute-start(bf16[16,128]{1,0:T(8,128)(2,1)S(1)} %slice_add_fusion), channel_id=1, source_target_pairs={{0,0},{1,1},{2,2},{3,3},{4,4},{5,5},{6,6},{7,7},{8,8},{9,9},{10,10... | collective-permute-start | bytes 12296 | tf_op jit(solution)/shard_map/tokens_plane/ppermute | solution.py:176

commit v4 on v3

--- a/solution.py
+++ b/solution.py
@@ -60,7 +60,7 @@
 
 def attend_kernel(
     scalars, q_ref, kv_ref, near, far, new_rows, bias_ref, out_ref,
-    natural, kv, picked, ext, sems,
+    natural, kv, picked, ext, weights, sems,
 ):
     beams = 16
     z = lax.axis_index("ctx")
@@ -99,16 +99,20 @@
             for g in range(KVH):
                 ext[c, g, pl.ds(part * 16, 16)] = moved[g * 16 : (g + 1) * 16]
 
-    for (c, rows), load in zip(chunks, loads):
-        load.wait()
+    def swap(n):
+        c, rows = chunks[n]
+        loads[n].wait()
         for first in range(rows.start, rows.start + step, 64):
             part = pl.ds(first, 64)
             kv[c, :, part] = jnp.swapaxes(natural[c, part], 0, 1)
 
+    for n in range(4):
+        swap(n)
+
     transposed = (((1,), (1,)), ((), ()))
     col = lax.broadcasted_iota(jnp.int32, (128, 128), 1)
     stats = jnp.zeros((128, 128), jnp.float32)
-    for g in range(KVH):
+    def weigh(g):
         q = q_ref[2 * g : 2 * g + 2].reshape(128, HD)
         s = lax.dot_general(q, kv[0, g], transposed, preferred_element_type=jnp.float32)
         e = lax.dot_general(q, ext[0, g], transposed, preferred_element_type=jnp.float32)
@@ -117,12 +121,31 @@
         p = jnp.exp2((s - m) * (scale * LOG2E))
         pe = jnp.exp2((e - m) * (scale * LOG2E))
         total = jnp.sum(p, axis=1, keepdims=True) + jnp.sum(pe, axis=1, keepdims=True)
-        o = jnp.dot(p.astype(jnp.bfloat16), kv[1, g], preferred_element_type=jnp.float32)
-        o = o + jnp.dot(pe.astype(jnp.bfloat16), ext[1, g], preferred_element_type=jnp.float32)
-        o = (o / total).astype(jnp.bfloat16)
+        weights[g, :, 0:1024] = p.astype(jnp.bfloat16)
+        weights[g, :, 1024:1152] = pe.astype(jnp.bfloat16)
+        return m * scale + jnp.log(total), 1.0 / total
+
+    def mix(g, inverse):
+        o = jnp.dot(weights[g, :, 0:1024], kv[1, g], preferred_element_type=jnp.float32)
+        o = o + jnp.dot(weights[g, :, 1024:1152], ext[1, g], preferred_element_type=jnp.float32)
+        o = (o * inverse).astype(jnp.bfloat16)
         out_ref[2 * g, 0:64] = o[0:64]
         out_ref[2 * g + 1, 0:64] = o[64:128]
-        stats = jnp.where(col == g, m * scale + jnp.log(total), stats)
+
+    logs, inverses = [], []
+    for g in range(KVH):
+        log, inverse = weigh(g)
+        logs.append(log)
+        inverses.append(inverse)
+        if g == 1:
+            for n in range(4, 8):
+                swap(n)
+        if g >= 2:
+            mix(g - 2, inverses[g - 2])
+    for g in range(6, KVH):
+        mix(g, inverses[g])
+    for g in range(KVH):
+        stats = jnp.where(col == g, logs[g], stats)
     flat = stats.T[0:KVH]
     high = flat.astype(jnp.bfloat16).astype(jnp.float32)
     middle = (flat - high).astype(jnp.bfloat16).astype(jnp.float32)
@@ -224,6 +247,7 @@
             pltpu.VMEM((2, KVH, 1024, HD), jnp.bfloat16),
             pltpu.VMEM((2, 512, HD), jnp.bfloat16),
             pltpu.VMEM((2, KVH, 128, HD), jnp.bfloat16),
+            pltpu.VMEM((KVH, 128, 1152), jnp.bfloat16),
             pltpu.SemaphoreType.DMA((8,)),
         ],
         compiler_params=pltpu.CompilerParams(vmem_limit_bytes=51 * 2**20),

time: 72.4 us -> 71.3 us (0.985)
  Pallas kernels: 9.26 us -> 8.21 us
    pallas_call x1, Pallas kernels: 6.02 us -> 4.97 us  [body(): pl.pallas_call(attend_kernel, out_shape=jax.ShapeDtypeStruct((16, 64 + EX...]
  transfers between devices with their start and end apart: 4 -> 4, of which waited for: 2 -> 2; matrix products, arithmetic and copies ran while one was open for 3% -> 3% of each run, Pallas kernels for 10% -> 9%
where the time goes in v4:
time: 71.3 us; the launch traced here: 70.9 us
  blocking collectives  25.3 us (35%)
  starting transfers between devices  24.8 us (35%)
  waiting for transfers between devices  8.7 us (12%)
  Pallas kernels  8.21 us (12%)
  local copies, waits for them, and re-layouts  2.31 us (3%)
  other arithmetic  0.82 us (1%)
  between operations  0.72 us (1%)
    all_to_all x1, blocking collectives, body(): parts = lax.all_to_all(parts, 'ctx', 0, 0, tiled=True)  25.3 us
    all_to_all x1, starting transfers between devices, body(): everyone = lax.all_to_all(sent, 'ctx', 0, 0, tiled=True)  14.8 us
    all_to_all x1, waiting for transfers between devices, body(): everyone = lax.all_to_all(sent, 'ctx', 0, 0, tiled=True)  6.81 us
    pallas_call x1, Pallas kernels, body(): pl.pallas_call(attend_kernel, out_shape=jax.ShapeDtypeStruct((16, 64 + EX...  4.97 us
    ppermute x1, starting transfers between devices, within_plane(): return lax.ppermute(block, ('ctx', 'beam'), pairs)  4.63 us
    ppermute x1, starting transfers between devices, body(): across = lax.ppermute(suffix, 'beam', [(i, i ^ 2) for i in range(32)])  3.53 us
    pallas_call x1, Pallas kernels, body(): pl.pallas_call(combine_kernel, out_shape=(jax.ShapeDtypeStruct((64, HD),...  1.95 us
    ppermute x1, starting transfers between devices, body(): far = lax.ppermute(near, 'beam', [(i, i ^ 1) for i in range(32)])  1.92 us
  transfers between devices with their start and end apart: 4, of which 2 were waited for; matrix products, arithmetic and copies ran while one was open for 3% of the time, Pallas kernels for 9%

profile of v4, /device:TPU:64, one launch (start us, length us, event | category | flops | bytes accessed | tf_op | source)
XLA Modules:
  0.0 70.9 jit_solution(14748501060030910333)
XLA Ops:
  0.6 0.0 copy-start.1
  0.6 3.5 %collective-permute-start = (bf16[1024,128]{1,0:T(8,128)(2,1)}, bf16[1024,128]{1,0:T(8,128)(2,1)S(1)}, u32[]{:S(2)}, u32[]{:S(2)}) collective-permute-start(bf16[1024,128]{1,0:T(8,128)(2,1)} %bitcast.6), channel_id=1, source_target_pairs={{0,2},{1,3},{2,0},{3,1},{4,6},{5,7},{6,4},{7,5},{8,10},{9,11},{10,... | collective-permute-start | bytes 786440 | tf_op jit(solution)/shard_map/suffix_x/ppermute | solution.py:232
  4.2 1.5 %broadcast_in_dim.8 = bf16[16,64,128]{2,1,0:T(8,128)(2,1)} broadcast(bf16[64,128]{1,0:T(8,128)(2,1)} %bitcast.8), dimensions={1,2} | broadcast | bytes 278528 | tf_op jit(solution)/shard_map/queries_to_all/broadcast_in_dim | solution.py:208
  5.6 14.8 %all-to-all-start = ((bf16[16,64,128]{2,1,0:T(8,128)(2,1)}), bf16[16,64,128]{2,1,0:T(8,128)(2,1)S(1)}, u32[]{:S(2)}, u32[]{:S(2)}) async-start(bf16[16,64,128]{2,1,0:T(8,128)(2,1)} %broadcast_in_dim.8), calls=%async_computation | async-start | bytes 524288 | tf_op jit(solution)/shard_map/queries_to_all/all_to_all | solution.py:209
  20.4 0.8 %pad_add_fusion.scalars = s32[64]{0:T(128)S(1)} fusion(s32[16]{0:T(128)} %param.12, s32[16]{0:T(128)} %param.13, s32[16]{0:T(128)} %param.15, s32[16]{0:T(128)} %param.14), kind=kLoop, calls=%fused_computation.2 | loop fusion | flops 192 | bytes 512 | tf_op jit(solution)/shard_map/concatenate | solution.py:210
  21.2 0.6 token_rows.1
  21.8 0.0 copy-start
  21.8 0.8 %copy-done = bf16[2,16,8,128]{3,2,1,0:T(8,128)(2,1)S(1)} copy-done((bf16[2,16,8,128]{3,2,1,0:T(8,128)(2,1)S(1)}, bf16[2,16,8,128]{3,2,1,0:T(8,128)(2,1)}, u32[]{:S(2)}) %copy-start) | copy-done | bytes 65560
  22.6 0.7 prepare.1
  23.3 0.0 collective-permute-done
  23.3 0.0 copy-done.1
  23.4 1.9 %collective-permute-start.1 = (bf16[2064,128]{1,0:T(8,128)(2,1)S(1)}, bf16[2064,128]{1,0:T(8,128)(2,1)S(1)}, u32[]{:S(2)}, u32[]{:S(2)}) collective-permute-start(bf16[2064,128]{1,0:T(8,128)(2,1)S(1)} %pad_maximum_fusion.near), channel_id=1, source_target_pairs={{0,1},{1,0},{2,3},{3,2},{4,5},{5,4},{6,7},{7,6},{8,9},{9,8},{10,11... | collective-permute-start | bytes 1585160 | tf_op jit(solution)/shard_map/suffix_core/ppermute | solution.py:236
  25.3 1.9 %collective-permute-done.1.far = bf16[2064,128]{1,0:T(8,128)(2,1)S(1)} collective-permute-done((bf16[2064,128]{1,0:T(8,128)(2,1)S(1)}, bf16[2064,128]{1,0:T(8,128)(2,1)S(1)}, u32[]{:S(2)}, u32[]{:S(2)}) %collective-permute-start.1) | collective-permute-done | bytes 528416 | tf_op jit(solution)/shard_map/suffix_core/ppermute | solution.py:236
  27.2 4.6 %collective-permute-start.2 = (bf16[16,128]{1,0:T(8,128)(2,1)S(1)}, bf16[16,128]{1,0:T(8,128)(2,1)S(1)}, u32[]{:S(2)}, u32[]{:S(2)}) collective-permute-start(bf16[16,128]{1,0:T(8,128)(2,1)S(1)} %slice_add_fusion), channel_id=1, source_target_pairs={{0,0},{1,1},{2,2},{3,3},{4,4},{5,5},{6,6},{7,7},{8,8},{9,9},{10,10... | collective-permute-start | bytes 12296 | tf_op jit(solution)/shard_map/tokens_plane/ppermute | solution.py:199
  31.8 6.8 %all-to-all-done.q_ref = bf16[16,64,128]{2,1,0:T(8,128)(2,1)S(1)} async-done(((bf16[16,64,128]{2,1,0:T(8,128)(2,1)}), bf16[16,64,128]{2,1,0:T(8,128)(2,1)S(1)}, u32[]{:S(2)}, u32[]{:S(2)}) %all-to-all-start) | async-done | bytes 262176 | tf_op jit(solution)/shard_map/queries_to_all/all_to_all | solution.py:209
  38.6 5.0 %attend.1.parts_ref = bf16[16,72,128]{2,1,0:T(8,128)(2,1)S(1)} custom-call(s32[64]{0:T(128)S(1)} %pad_add_fusion.scalars, bf16[16,64,128]{2,1,0:T(8,128)(2,1)S(1)} %all-to-all-done.q_ref, bf16[2,1024,8,128]{3,2,1,0:T(8,128)(2,1)} %kv_ref.1, bf16[2064,128]{1,0:T(8,128)(2,1)S(1)} %pad_maximum_fusion.near, bf16[2064,128]{1,0:T(8,128)(2,1)S(1)} %collective-permute-done.1.far, ...), custom_call_target="tpu_custom_call" | custom-call | flops 600000000 | bytes 6000000 | tf_op jit(solution)/shard_map/attend/pallas_call | solution.py:240
  43.6 0.0 collective-permute-done.2.tokens_ref
  43.6 25.3 %all_to_all.10.parts_ref = bf16[16,72,128]{2,1,0:T(8,128)(2,1)S(1)} all-to-all(bf16[16,72,128]{2,1,0:T(8,128)(2,1)S(1)} %insert.1), channel_id=1, replica_groups=mesh['ctx'=16,'beam'=32] {'ctx'}, dimensions={0} | all-to-all | bytes 589824 | tf_op jit(solution)/shard_map/parts_home/all_to_all | solution.py:271
  68.9 1.9 %combine.1 = (bf16[64,128]{1,0:T(8,128)(2,1)}, f32[1,16]{1,0:T(1,128)}) custom-call(s32[64]{0:T(128)S(1)} %pad_add_fusion.scalars, bf16[16,72,128]{2,1,0:T(8,128)(2,1)S(1)} %all_to_all.10.parts_ref), custom_call_target="tpu_custom_call" | custom-call | tf_op jit(solution)/shard_map/combine/pallas_call | solution.py:272
  (3 shorter events, 0.1 us)
Async XLA Ops:
  0.6 22.7 %copy-start.1 = (bf16[2,16,4,8,128]{4,3,2,1,0:T(8,128)(2,1)S(1)}, bf16[2,16,4,8,128]{4,3,2,1,0:T(8,128)(2,1)}, u32[]{:S(2)}) copy-start(bf16[2,16,4,8,128]{4,3,2,1,0:T(8,128)(2,1)} %param.10) | copy-start | bytes 786436
  0.6 22.7 %collective-permute-start = (bf16[1024,128]{1,0:T(8,128)(2,1)}, bf16[1024,128]{1,0:T(8,128)(2,1)S(1)}, u32[]{:S(2)}, u32[]{:S(2)}) collective-permute-start(bf16[1024,128]{1,0:T(8,128)(2,1)} %bitcast.6), channel_id=1, source_target_pairs={{0,2},{1,3},{2,0},{3,1},{4,6},{5,7},{6,4},{7,5},{8,10},{9,11},{10,... | collective-permute-start | bytes 786440 | tf_op jit(solution)/shard_map/suffix_x/ppermute | solution.py:232
  5.6 33.0 %all-to-all-start = ((bf16[16,64,128]{2,1,0:T(8,128)(2,1)}), bf16[16,64,128]{2,1,0:T(8,128)(2,1)S(1)}, u32[]{:S(2)}, u32[]{:S(2)}) async-start(bf16[16,64,128]{2,1,0:T(8,128)(2,1)} %broadcast_in_dim.8), calls=%async_computation | async-start | bytes 524288 | tf_op jit(solution)/shard_map/queries_to_all/all_to_all | solution.py:209
  21.8 0.8 %copy-start = (bf16[2,16,8,128]{3,2,1,0:T(8,128)(2,1)S(1)}, bf16[2,16,8,128]{3,2,1,0:T(8,128)(2,1)}, u32[]{:S(2)}) copy-start(bf16[2,16,8,128]{3,2,1,0:T(8,128)(2,1)} %param.11) | copy-start | bytes 196612
  23.4 3.8 %collective-permute-start.1 = (bf16[2064,128]{1,0:T(8,128)(2,1)S(1)}, bf16[2064,128]{1,0:T(8,128)(2,1)S(1)}, u32[]{:S(2)}, u32[]{:S(2)}) collective-permute-start(bf16[2064,128]{1,0:T(8,128)(2,1)S(1)} %pad_maximum_fusion.near), channel_id=1, source_target_pairs={{0,1},{1,0},{2,3},{3,2},{4,5},{5,4},{6,7},{7,6},{8,9},{9,8},{10,11... | collective-permute-start | bytes 1585160 | tf_op jit(solution)/shard_map/suffix_core/ppermute | solution.py:236
  27.2 16.4 %collective-permute-start.2 = (bf16[16,128]{1,0:T(8,128)(2,1)S(1)}, bf16[16,128]{1,0:T(8,128)(2,1)S(1)}, u32[]{:S(2)}, u32[]{:S(2)}) collective-permute-start(bf16[16,128]{1,0:T(8,128)(2,1)S(1)} %slice_add_fusion), channel_id=1, source_target_pairs={{0,0},{1,1},{2,2},{3,3},{4,4},{5,5},{6,6},{7,7},{8,8},{9,9},{10,10... | collective-permute-start | bytes 12296 | tf_op jit(solution)/shard_map/tokens_plane/ppermute | solution.py:199

commit v5 on v4

--- a/solution.py
+++ b/solution.py
@@ -39,12 +39,44 @@
         rows_ref[...] = digits.astype(jnp.float32).astype(jnp.bfloat16)
 
 
-def prepare_kernel(scalars, new_ref, new_rows_ref, bias_ref):
+def attend_kernel(
+    scalars, q_ref, kv_ref, near, far, new_ref, out_ref,
+    natural, kv, picked, ext, weights, bias_ref, sems,
+):
+    beams = 16
     z = lax.axis_index("ctx")
+    place = lax.axis_index("beam") % FAMILY_DEVICES
+    scale = HD**-0.5
+
+    step = 256
+    chunks = [(c, pl.ds(first, step)) for c in range(2) for first in range(0, 1024, step)]
+    loads = [
+        pltpu.make_async_copy(kv_ref.at[c, rows], natural.at[c, rows], sems.at[n])
+        for n, (c, rows) in enumerate(chunks)
+    ]
+    for load in loads:
+        load.start()
+
+    for b in range(beams):
+        parent = scalars[48 + b]
+        slot = lax.bitwise_xor((parent // beams) % FAMILY_DEVICES, place)
+        local = parent % beams
+        for k, held in enumerate((near, far)):
+
+            @pl.when(slot % 2 == k)
+            def _(held=held, local=local, slot=slot, b=b):
+                for c in range(2):
+                    first = pl.multiple_of((slot // 2 * 2 + c) * 512 + local * 32, 32)
+                    picked[c, pl.ds(b * 32, 32)] = held[pl.ds(first, 32)]
+
     by_head = rows_by_head()
     for c in range(2):
-        moved = jnp.dot(by_head, new_ref[c], preferred_element_type=jnp.float32)
-        new_rows_ref[c] = moved.astype(jnp.bfloat16)
+        ext[c, :, 80:128] = jnp.zeros((KVH, 48, HD), jnp.bfloat16)
+        for part in range(5):
+            rows = picked[c, pl.ds(part * 128, 128)] if part < 4 else new_ref[c]
+            moved = jnp.dot(by_head, rows, preferred_element_type=jnp.float32).astype(jnp.bfloat16)
+            for g in range(KVH):
+                ext[c, g, pl.ds(part * 16, 16)] = moved[g * 16 : (g + 1) * 16]
 
     row = lax.broadcasted_iota(jnp.int32, (128, 128), 0)
     col = lax.broadcasted_iota(jnp.int32, (128, 128), 1)
@@ -57,48 +89,6 @@
     bias_ref[0] = jnp.where(on_suffix, 0.0, FAR_BELOW)
     bias_ref[1] = jnp.where(on_suffix | on_new, 0.0, FAR_BELOW)
 
-
-def attend_kernel(
-    scalars, q_ref, kv_ref, near, far, new_rows, bias_ref, out_ref,
-    natural, kv, picked, ext, weights, sems,
-):
-    beams = 16
-    z = lax.axis_index("ctx")
-    place = lax.axis_index("beam") % FAMILY_DEVICES
-    scale = HD**-0.5
-
-    step = 256
-    chunks = [(c, pl.ds(first, step)) for c in range(2) for first in range(0, 1024, step)]
-    loads = [
-        pltpu.make_async_copy(kv_ref.at[c, rows], natural.at[c, rows], sems.at[n])
-        for n, (c, rows) in enumerate(chunks)
-    ]
-    for load in loads:
-        load.start()
-
-    for b in range(beams):
-        parent = scalars[48 + b]
-        slot = lax.bitwise_xor((parent // beams) % FAMILY_DEVICES, place)
-        local = parent % beams
-        for k, held in enumerate((near, far)):
-
-            @pl.when(slot % 2 == k)
-            def _(held=held, local=local, slot=slot, b=b):
-                for c in range(2):
-                    first = pl.multiple_of((slot // 2 * 2 + c) * 512 + local * 32, 32)
-                    picked[c, pl.ds(b * 32, 32)] = held[pl.ds(first, 32)]
-
-    by_head = rows_by_head()
-    for c in range(2):
-        ext[c, :, 80:128] = jnp.zeros((KVH, 48, HD), jnp.bfloat16)
-        for g in range(KVH):
-            ext[c, g, 64:80] = new_rows[c, g * 16 : (g + 1) * 16]
-        for part in range(4):
-            rows = picked[c, pl.ds(part * 128, 128)]
-            moved = jnp.dot(by_head, rows, preferred_element_type=jnp.float32).astype(jnp.bfloat16)
-            for g in range(KVH):
-                ext[c, g, pl.ds(part * 16, 16)] = moved[g * 16 : (g + 1) * 16]
-
     def swap(n):
         c, rows = chunks[n]
         loads[n].wait()
@@ -110,7 +100,6 @@
         swap(n)
 
     transposed = (((1,), (1,)), ((), ()))
-    col = lax.broadcasted_iota(jnp.int32, (128, 128), 1)
     stats = jnp.zeros((128, 128), jnp.float32)
     def weigh(g):
         q = q_ref[2 * g : 2 * g + 2].reshape(128, HD)
@@ -216,21 +205,10 @@
         compiler_params=pltpu.CompilerParams(vmem_limit_bytes=2**20),
         name="token_rows",
     )(scalars)
-    new_rows, bias = pl.pallas_call(
-        prepare_kernel,
-        out_shape=(
-            jax.ShapeDtypeStruct((2, 128, HD), jnp.bfloat16),
-            jax.ShapeDtypeStruct((2, 128, 128), jnp.float32),
-        ),
-        in_specs=[smem, vmem],
-        out_specs=(vmem,) * 2,
-        compiler_params=pltpu.CompilerParams(vmem_limit_bytes=4 * 2**20),
-        name="prepare",
-    )(scalars, new_kv.reshape(2, 128, HD))
     suffix = suffix_kv.reshape(1024, HD)
     with jax.named_scope("suffix_x"):
         across = lax.ppermute(suffix, "beam", [(i, i ^ 2) for i in range(32)])
-    across, rows_b, new_rows, bias = lax.optimization_barrier((across, rows_b, new_rows, bias))
+    across, rows_b = lax.optimization_barrier((across, rows_b))
     with jax.named_scope("suffix_core"):
         near = jnp.concatenate((suffix, across, rows_b))
         far = lax.ppermute(near, "beam", [(i, i ^ 1) for i in range(32)])
@@ -240,7 +218,7 @@
     parts = pl.pallas_call(
         attend_kernel,
         out_shape=jax.ShapeDtypeStruct((16, 64 + EXTRA, HD), jnp.bfloat16),
-        in_specs=[smem, vmem, hbm] + [vmem] * 4,
+        in_specs=[smem, vmem, hbm] + [vmem] * 3,
         out_specs=vmem,
         scratch_shapes=[
             pltpu.VMEM((2, 1024, KVH, HD), jnp.bfloat16),
@@ -248,6 +226,7 @@
             pltpu.VMEM((2, 512, HD), jnp.bfloat16),
             pltpu.VMEM((2, KVH, 128, HD), jnp.bfloat16),
             pltpu.VMEM((KVH, 128, 1152), jnp.bfloat16),
+            pltpu.VMEM((2, 128, 128), jnp.float32),
             pltpu.SemaphoreType.DMA((8,)),
         ],
         compiler_params=pltpu.CompilerParams(vmem_limit_bytes=51 * 2**20),
@@ -255,7 +234,7 @@
             flops=600_000_000, bytes_accessed=6_000_000, transcendentals=1_200_000
         ),
         name="attend",
-    )(scalars, everyone, prompt_kv, near, far, new_rows, bias)
+    )(scalars, everyone, prompt_kv, near, far, new_kv.reshape(2, 128, HD))
 
     parts, plane = lax.optimization_barrier((parts, plane))
     parts = pl.pallas_call(

time: 71.3 us -> 71.1 us (level)
  the two profiles are of different devices: /device:TPU:64 before, /device:TPU:8 now
where the time goes in v5:
time: 71.1 us; the launch traced here: 70.7 us
  blocking collectives  24.6 us (35%)
  starting transfers between devices  21.3 us (30%)
  waiting for transfers between devices  13.3 us (19%)
  Pallas kernels  7.49 us (11%)
  other arithmetic  1.77 us (2%)
  local copies, waits for them, and re-layouts  1.47 us (2%)
    all_to_all x1, blocking collectives, body(): parts = lax.all_to_all(parts, 'ctx', 0, 0, tiled=True)  24.6 us
    all_to_all x1, starting transfers between devices, body(): everyone = lax.all_to_all(sent, 'ctx', 0, 0, tiled=True)  15.2 us
    all_to_all x1, waiting for transfers between devices, body(): everyone = lax.all_to_all(sent, 'ctx', 0, 0, tiled=True)  11.4 us
    pallas_call x1, Pallas kernels, body(): pl.pallas_call(attend_kernel, out_shape=jax.ShapeDtypeStruct((16, 64 + EX...  4.95 us
    ppermute x1, starting transfers between devices, body(): across = lax.ppermute(suffix, 'beam', [(i, i ^ 2) for i in range(32)])  3.53 us
    pallas_call x1, Pallas kernels, body(): pl.pallas_call(combine_kernel, out_shape=(jax.ShapeDtypeStruct((64, HD),...  1.95 us
    ppermute x1, starting transfers between devices, body(): far = lax.ppermute(near, 'beam', [(i, i ^ 1) for i in range(32)])  1.92 us
    ppermute x1, waiting for transfers between devices, body(): far = lax.ppermute(near, 'beam', [(i, i ^ 1) for i in range(32)])  1.88 us
  transfers between devices with their start and end apart: 4, of which 2 were waited for; matrix products, arithmetic and copies ran while one was open for 5% of the time, Pallas kernels for 8%

profile of v5, /device:TPU:8, one launch (start us, length us, event | category | flops | bytes accessed | tf_op | source)
XLA Modules:
  0.0 70.7 jit_solution(15154177003931584801)
XLA Ops:
  0.6 0.0 copy-start
  0.6 3.5 %collective-permute-start = (bf16[1024,128]{1,0:T(8,128)(2,1)}, bf16[1024,128]{1,0:T(8,128)(2,1)S(1)}, u32[]{:S(2)}, u32[]{:S(2)}) collective-permute-start(bf16[1024,128]{1,0:T(8,128)(2,1)} %bitcast.6), channel_id=1, source_target_pairs={{0,2},{1,3},{2,0},{3,1},{4,6},{5,7},{6,4},{7,5},{8,10},{9,11},{10,... | collective-permute-start | bytes 786440 | tf_op jit(solution)/shard_map/suffix_x/ppermute | solution.py:210
  4.2 1.5 %broadcast_in_dim.8 = bf16[16,64,128]{2,1,0:T(8,128)(2,1)} broadcast(bf16[64,128]{1,0:T(8,128)(2,1)} %bitcast.8), dimensions={1,2} | broadcast | bytes 278528 | tf_op jit(solution)/shard_map/queries_to_all/broadcast_in_dim | solution.py:197
  5.6 15.2 %all-to-all-start = ((bf16[16,64,128]{2,1,0:T(8,128)(2,1)}), bf16[16,64,128]{2,1,0:T(8,128)(2,1)S(1)}, u32[]{:S(2)}, u32[]{:S(2)}) async-start(bf16[16,64,128]{2,1,0:T(8,128)(2,1)} %broadcast_in_dim.8), calls=%async_computation | async-start | bytes 524288 | tf_op jit(solution)/shard_map/queries_to_all/all_to_all | solution.py:198
  20.9 0.8 %pad_add_fusion.scalars = s32[64]{0:T(128)S(1)} fusion(s32[16]{0:T(128)} %param.12, s32[16]{0:T(128)} %param.13, s32[16]{0:T(128)} %param.15, s32[16]{0:T(128)} %param.14), kind=kLoop, calls=%fused_computation.2 | loop fusion | flops 192 | bytes 512 | tf_op jit(solution)/shard_map/concatenate | solution.py:199
  21.6 0.6 token_rows.1
  22.2 0.0 collective-permute-done
  22.2 1.0 %pad_maximum_fusion.near = bf16[2064,128]{1,0:T(8,128)(2,1)S(1)} fusion(bf16[16,128]{1,0:T(8,128)(2,1)S(1)} %get-tuple-element.12, bf16[1024,128]{1,0:T(8,128)(2,1)S(1)} %collective-permute-done, bf16[1024,128]{1,0:T(8,128)(2,1)} %bitcast.7), kind=kLoop, calls=%fused_computation | loop fusion | flops 1585152 | bytes 1056768 | tf_op jit(solution)/shard_map/suffix_core/concatenate | solution.py:213
  23.2 1.9 %collective-permute-start.1 = (bf16[2064,128]{1,0:T(8,128)(2,1)S(1)}, bf16[2064,128]{1,0:T(8,128)(2,1)S(1)}, u32[]{:S(2)}, u32[]{:S(2)}) collective-permute-start(bf16[2064,128]{1,0:T(8,128)(2,1)S(1)} %pad_maximum_fusion.near), channel_id=1, source_target_pairs={{0,1},{1,0},{2,3},{3,2},{4,5},{5,4},{6,7},{7,6},{8,9},{9,8},{10,11... | collective-permute-start | bytes 1585160 | tf_op jit(solution)/shard_map/suffix_core/ppermute | solution.py:214
  25.1 1.9 %collective-permute-done.1.far = bf16[2064,128]{1,0:T(8,128)(2,1)S(1)} collective-permute-done((bf16[2064,128]{1,0:T(8,128)(2,1)S(1)}, bf16[2064,128]{1,0:T(8,128)(2,1)S(1)}, u32[]{:S(2)}, u32[]{:S(2)}) %collective-permute-start.1) | collective-permute-done | bytes 528416 | tf_op jit(solution)/shard_map/suffix_core/ppermute | solution.py:214
  27.0 0.7 collective-permute-start.2
  27.7 11.4 %all-to-all-done.q_ref = bf16[16,64,128]{2,1,0:T(8,128)(2,1)S(1)} async-done(((bf16[16,64,128]{2,1,0:T(8,128)(2,1)}), bf16[16,64,128]{2,1,0:T(8,128)(2,1)S(1)}, u32[]{:S(2)}, u32[]{:S(2)}) %all-to-all-start) | async-done | bytes 262176 | tf_op jit(solution)/shard_map/queries_to_all/all_to_all | solution.py:198
  39.1 0.0 copy-done
  39.1 5.0 %attend.1.parts_ref = bf16[16,72,128]{2,1,0:T(8,128)(2,1)S(1)} custom-call(s32[64]{0:T(128)S(1)} %pad_add_fusion.scalars, bf16[16,64,128]{2,1,0:T(8,128)(2,1)S(1)} %all-to-all-done.q_ref, bf16[2,1024,8,128]{3,2,1,0:T(8,128)(2,1)} %kv_ref.1, bf16[2064,128]{1,0:T(8,128)(2,1)S(1)} %pad_maximum_fusion.near, bf16[2064,128]{1,0:T(8,128)(2,1)S(1)} %collective-permute-done.1.far, ...), custom_call_target="tpu_custom_call" | custom-call | flops 600000000 | bytes 6000000 | tf_op jit(solution)/shard_map/attend/pallas_call | solution.py:218
  44.1 0.0 collective-permute-done.2.tokens_ref
  44.1 24.6 %all_to_all.10.parts_ref = bf16[16,72,128]{2,1,0:T(8,128)(2,1)S(1)} all-to-all(bf16[16,72,128]{2,1,0:T(8,128)(2,1)S(1)} %insert.1), channel_id=1, replica_groups=mesh['ctx'=16,'beam'=32] {'ctx'}, dimensions={0} | all-to-all | bytes 589824 | tf_op jit(solution)/shard_map/parts_home/all_to_all | solution.py:250
  68.7 1.9 %combine.1 = (bf16[64,128]{1,0:T(8,128)(2,1)}, f32[1,16]{1,0:T(1,128)}) custom-call(s32[64]{0:T(128)S(1)} %pad_add_fusion.scalars, bf16[16,72,128]{2,1,0:T(8,128)(2,1)S(1)} %all_to_all.10.parts_ref), custom_call_target="tpu_custom_call" | custom-call | tf_op jit(solution)/shard_map/combine/pallas_call | solution.py:251
  (2 shorter events, 0.0 us)
Async XLA Ops:
  0.6 38.5 %copy-start = (bf16[2,16,8,128]{3,2,1,0:T(8,128)(2,1)S(1)}, bf16[2,16,8,128]{3,2,1,0:T(8,128)(2,1)}, u32[]{:S(2)}) copy-start(bf16[2,16,8,128]{3,2,1,0:T(8,128)(2,1)} %param.11) | copy-start | bytes 196612
  0.6 21.6 %collective-permute-start = (bf16[1024,128]{1,0:T(8,128)(2,1)}, bf16[1024,128]{1,0:T(8,128)(2,1)S(1)}, u32[]{:S(2)}, u32[]{:S(2)}) collective-permute-start(bf16[1024,128]{1,0:T(8,128)(2,1)} %bitcast.6), channel_id=1, source_target_pairs={{0,2},{1,3},{2,0},{3,1},{4,6},{5,7},{6,4},{7,5},{8,10},{9,11},{10,... | collective-permute-start | bytes 786440 | tf_op jit(solution)/shard_map/suffix_x/ppermute | solution.py:210
  5.6 33.5 %all-to-all-start = ((bf16[16,64,128]{2,1,0:T(8,128)(2,1)}), bf16[16,64,128]{2,1,0:T(8,128)(2,1)S(1)}, u32[]{:S(2)}, u32[]{:S(2)}) async-start(bf16[16,64,128]{2,1,0:T(8,128)(2,1)} %broadcast_in_dim.8), calls=%async_computation | async-start | bytes 524288 | tf_op jit(solution)/shard_map/queries_to_all/all_to_all | solution.py:198
  23.2 3.8 %collective-permute-start.1 = (bf16[2064,128]{1,0:T(8,128)(2,1)S(1)}, bf16[2064,128]{1,0:T(8,128)(2,1)S(1)}, u32[]{:S(2)}, u32[]{:S(2)}) collective-permute-start(bf16[2064,128]{1,0:T(8,128)(2,1)S(1)} %pad_maximum_fusion.near), channel_id=1, source_target_pairs={{0,1},{1,0},{2,3},{3,2},{4,5},{5,4},{6,7},{7,6},{8,9},{9,8},{10,11... | collective-permute-start | bytes 1585160 | tf_op jit(solution)/shard_map/suffix_core/ppermute | solution.py:214
  27.0 17.1 %collective-permute-start.2 = (bf16[16,128]{1,0:T(8,128)(2,1)S(1)}, bf16[16,128]{1,0:T(8,128)(2,1)S(1)}, u32[]{:S(2)}, u32[]{:S(2)}) collective-permute-start(bf16[16,128]{1,0:T(8,128)(2,1)S(1)} %slice_add_fusion), channel_id=1, source_target_pairs={{0,0},{1,1},{2,2},{3,3},{4,4},{5,5},{6,6},{7,7},{8,8},{9,9},{10,10... | collective-permute-start | bytes 12296 | tf_op jit(solution)/shard_map/tokens_plane/ppermute | solution.py:188

commit v6 on v5

--- a/solution.py
+++ b/solution.py
@@ -22,25 +22,23 @@
     return jnp.where(hit, 1.0, 0.0).astype(jnp.bfloat16)
 
 
-def token_rows_kernel(scalars, rows_a, rows_b):
-    row = lax.broadcasted_iota(jnp.int32, (EXTRA, 128), 0)
-    lane = lax.broadcasted_iota(jnp.int32, (EXTRA, 128), 1)
-    for rows_ref, first_lane in ((rows_a, 0), (rows_b, 16)):
-        tokens = jnp.zeros((EXTRA, 128), jnp.int32)
-        groups = jnp.zeros((EXTRA, 128), jnp.int32)
-        for b in range(16):
-            tokens = jnp.where(lane == first_lane + b, scalars[b], tokens)
-            groups = jnp.where(lane == first_lane + b, scalars[16 + b], groups)
-        digits = jnp.where(row == 3, tokens >> 16, 0)
-        digits = jnp.where(row == 4, (tokens >> 8) & 255, digits)
-        digits = jnp.where(row == 5, tokens & 255, digits)
-        digits = jnp.where(row == 6, groups, digits)
-        digits = jnp.concatenate((digits, jnp.zeros_like(digits)))
-        rows_ref[...] = digits.astype(jnp.float32).astype(jnp.bfloat16)
+def token_rows_kernel(scalars, rows_ref):
+    row = lax.broadcasted_iota(jnp.int32, (2 * EXTRA, 128), 0)
+    lane = lax.broadcasted_iota(jnp.int32, (2 * EXTRA, 128), 1)
+    tokens = jnp.zeros((2 * EXTRA, 128), jnp.int32)
+    groups = jnp.zeros((2 * EXTRA, 128), jnp.int32)
+    for b in range(16):
+        tokens = jnp.where(lane == b, scalars[b], tokens)
+        groups = jnp.where(lane == b, scalars[16 + b], groups)
+    digits = jnp.where(row == 3, tokens >> 16, 0)
+    digits = jnp.where(row == 4, (tokens >> 8) & 255, digits)
+    digits = jnp.where(row == 5, tokens & 255, digits)
+    digits = jnp.where(row == 6, groups, digits)
+    rows_ref[...] = digits.astype(jnp.float32).astype(jnp.bfloat16)
 
 
 def attend_kernel(
-    scalars, q_ref, kv_ref, near, far, new_ref, out_ref,
+    scalars, q_ref, kv_ref, near, far, new_ref, tok_ref, out_ref,
     natural, kv, picked, ext, weights, bias_ref, sems,
 ):
     beams = 16
@@ -140,20 +138,15 @@
     middle = (flat - high).astype(jnp.bfloat16).astype(jnp.float32)
     low = flat - high - middle
     place_row = lax.broadcasted_iota(jnp.int32, (EXTRA, 128), 0)
+    tokens = tok_ref[...].astype(jnp.float32)
+    tokens = tokens + pltpu.roll(far[2048:2064].astype(jnp.float32), 16, 1)
+    tokens = tokens[0:EXTRA]
     for g in range(KVH):
-        block = jnp.where(place_row == 0, high[g : g + 1], 0.0)
+        block = jnp.where(place_row == 0, high[g : g + 1], tokens)
         block = jnp.where(place_row == 1, middle[g : g + 1], block)
         block = jnp.where(place_row == 2, low[g : g + 1], block).astype(jnp.bfloat16)
         out_ref[2 * g, 64 : 64 + EXTRA] = block
         out_ref[2 * g + 1, 64 : 64 + EXTRA] = block
-
-
-def insert_kernel(tokens_ref, parts_ref, out_ref):
-    row = lax.broadcasted_iota(jnp.int32, (EXTRA, 128), 0)
-    tokens = tokens_ref[0:EXTRA].astype(jnp.float32)
-    for target in range(16):
-        spare = parts_ref[target, 64 : 64 + EXTRA].astype(jnp.float32)
-        out_ref[target, 64 : 64 + EXTRA] = jnp.where(row < 3, spare, tokens).astype(jnp.bfloat16)
 
 
 def combine_kernel(scalars, parts_ref, out_ref, penalty_ref):
@@ -183,8 +176,11 @@
     penalty_ref[...] = jnp.sum(counts.T, axis=0, keepdims=True)
 
 
+TOKENS_FROM = (10, 9, 11, 6, 15, 7, 5, 12, 0, 1, 3, 4, 13, 8, 2, 14)
+
+
 def within_plane(block):
-    pairs = [(z * 32 + b, z * 32 + (b ^ (2 * z))) for z in range(16) for b in range(32)]
+    pairs = [(z * 32 + b, z * 32 + (b ^ (2 * TOKENS_FROM[z]))) for z in range(16) for b in range(32)]
     return lax.ppermute(block, ("ctx", "beam"), pairs)
 
 
@@ -197,28 +193,31 @@
         sent = jnp.broadcast_to(queries.reshape(1, 64, HD), (16, 64, HD))
         everyone = lax.all_to_all(sent, "ctx", 0, 0, tiled=True)
     scalars = jnp.concatenate((token_ids, group_ids, lengths, parents))
-    rows_a, rows_b = pl.pallas_call(
+    rows = pl.pallas_call(
         token_rows_kernel,
-        out_shape=(jax.ShapeDtypeStruct((2 * EXTRA, 128), jnp.bfloat16),) * 2,
+        out_shape=jax.ShapeDtypeStruct((2 * EXTRA, 128), jnp.bfloat16),
         in_specs=[smem],
-        out_specs=(vmem,) * 2,
+        out_specs=vmem,
         compiler_params=pltpu.CompilerParams(vmem_limit_bytes=2**20),
+        cost_estimate=pl.CostEstimate(
+            flops=30_000_000_000, bytes_accessed=1_000_000, transcendentals=0
+        ),
         name="token_rows",
     )(scalars)
     suffix = suffix_kv.reshape(1024, HD)
     with jax.named_scope("suffix_x"):
         across = lax.ppermute(suffix, "beam", [(i, i ^ 2) for i in range(32)])
-    across, rows_b = lax.optimization_barrier((across, rows_b))
+    with jax.named_scope("tokens_plane"):
+        tokens = within_plane(rows)
+    across, tokens = lax.optimization_barrier((across, tokens))
     with jax.named_scope("suffix_core"):
-        near = jnp.concatenate((suffix, across, rows_b))
+        near = jnp.concatenate((suffix, across, tokens))
         far = lax.ppermute(near, "beam", [(i, i ^ 1) for i in range(32)])
-    with jax.named_scope("tokens_plane"):
-        plane = within_plane(rows_a + far[2048:])
 
     parts = pl.pallas_call(
         attend_kernel,
         out_shape=jax.ShapeDtypeStruct((16, 64 + EXTRA, HD), jnp.bfloat16),
-        in_specs=[smem, vmem, hbm] + [vmem] * 3,
+        in_specs=[smem, vmem, hbm] + [vmem] * 4,
         out_specs=vmem,
         scratch_shapes=[
             pltpu.VMEM((2, 1024, KVH, HD), jnp.bfloat16),
@@ -234,18 +233,8 @@
             flops=600_000_000, bytes_accessed=6_000_000, transcendentals=1_200_000
         ),
         name="attend",
-    )(scalars, everyone, prompt_kv, near, far, new_kv.reshape(2, 128, HD))
-
-    parts, plane = lax.optimization_barrier((parts, plane))
-    parts = pl.pallas_call(
-        insert_kernel,
-        out_shape=jax.ShapeDtypeStruct(parts.shape, parts.dtype),
-        in_specs=[vmem, vmem],
-        out_specs=vmem,
-        input_output_aliases={1: 0},
-        compiler_params=pltpu.CompilerParams(vmem_limit_bytes=2 * 2**20),
-        name="insert",
-    )(plane, parts)
+    )(scalars, everyone, prompt_kv, near, far, new_kv.reshape(2, 128, HD), tokens)
+
     with jax.named_scope("parts_home"):
         parts = lax.all_to_all(parts, "ctx", 0, 0, tiled=True)
     attended, penalty = pl.pallas_call(

time: 71.1 us -> 70 us (0.985)
  waiting for transfers between devices: 13.3 us -> 5.1 us
  starting transfers between devices: 21.3 us -> 27 us
  blocking collectives: 24.6 us -> 27 us
  other arithmetic: 1.77 us -> 0.82 us
    all_to_all x1, waiting for transfers between devices: 11.4 us -> 0.19 us  [body(): everyone = lax.all_to_all(sent, 'ctx', 0, 0, tiled=True)]
    ppermute x1, starting transfers between devices: 0.65 us -> 6.5 us  [within_plane(): return lax.ppermute(block, ('ctx', 'beam'), pairs)]
    ppermute x1, waiting for transfers between devices: 0.01 us -> 3.03 us  [within_plane(): return lax.ppermute(block, ('ctx', 'beam'), pairs)]
    all_to_all x1, blocking collectives: 24.6 us -> 27 us  [body(): parts = lax.all_to_all(parts, 'ctx', 0, 0, tiled=True)]
    concatenate x1, other arithmetic: 0.99 us -> 0.04 us  [body(): near = jnp.concatenate((suffix, across, tokens))]
  transfers between devices with their start and end apart: 4 -> 4, of which waited for: 2 -> 3; matrix products, arithmetic and copies ran while one was open for 5% -> 1% of each run, Pallas kernels for 8% -> 1%
where the time goes in v6:
time: 70 us; the launch traced here: 69.6 us
  starting transfers between devices  27 us (39%)
  blocking collectives  27 us (39%)
  Pallas kernels  7.45 us (11%)
  waiting for transfers between devices  5.1 us (7%)
  local copies, waits for them, and re-layouts  1.48 us (2%)
  other arithmetic  0.82 us (1%)
    all_to_all x1, blocking collectives, body(): parts = lax.all_to_all(parts, 'ctx', 0, 0, tiled=True)  27 us
    all_to_all x1, starting transfers between devices, body(): everyone = lax.all_to_all(sent, 'ctx', 0, 0, tiled=True)  15.2 us
    ppermute x1, starting transfers between devices, within_plane(): return lax.ppermute(block, ('ctx', 'beam'), pairs)  6.5 us
    pallas_call x1, Pallas kernels, body(): pl.pallas_call(attend_kernel, out_shape=jax.ShapeDtypeStruct((16, 64 + EX...  4.94 us
    ppermute x1, starting transfers between devices, body(): across = lax.ppermute(suffix, 'beam', [(i, i ^ 2) for i in range(32)])  3.4 us
    ppermute x1, waiting for transfers between devices, within_plane(): return lax.ppermute(block, ('ctx', 'beam'), pairs)  3.03 us
    pallas_call x1, Pallas kernels, body(): pl.pallas_call(combine_kernel, out_shape=(jax.ShapeDtypeStruct((64, HD),...  1.95 us
    ppermute x1, starting transfers between devices, body(): far = lax.ppermute(near, 'beam', [(i, i ^ 1) for i in range(32)])  1.92 us
  transfers between devices with their start and end apart: 4, of which 3 were waited for; matrix products, arithmetic and copies ran while one was open for 1% of the time, Pallas kernels for 1%

profile of v6, /device:TPU:8, one launch (start us, length us, event | category | flops | bytes accessed | tf_op | source)
XLA Modules:
  0.0 69.6 jit_solution(6062914328358631373)
XLA Ops:
  0.6 1.5 %broadcast_in_dim.8 = bf16[16,64,128]{2,1,0:T(8,128)(2,1)} broadcast(bf16[64,128]{1,0:T(8,128)(2,1)} %bitcast.8), dimensions={1,2} | broadcast | bytes 278528 | tf_op jit(solution)/shard_map/queries_to_all/broadcast_in_dim | solution.py:193
  2.1 15.2 %all-to-all-start = ((bf16[16,64,128]{2,1,0:T(8,128)(2,1)}), bf16[16,64,128]{2,1,0:T(8,128)(2,1)S(1)}, u32[]{:S(2)}, u32[]{:S(2)}) async-start(bf16[16,64,128]{2,1,0:T(8,128)(2,1)} %broadcast_in_dim.8), calls=%async_computation | async-start | bytes 524288 | tf_op jit(solution)/shard_map/queries_to_all/all_to_all | solution.py:194
  17.3 3.4 %collective-permute-start = (bf16[1024,128]{1,0:T(8,128)(2,1)}, bf16[1024,128]{1,0:T(8,128)(2,1)S(1)}, u32[]{:S(2)}, u32[]{:S(2)}) collective-permute-start(bf16[1024,128]{1,0:T(8,128)(2,1)} %bitcast.6), channel_id=1, source_target_pairs={{0,2},{1,3},{2,0},{3,1},{4,6},{5,7},{6,4},{7,5},{8,10},{9,11},{10,... | collective-permute-start | bytes 786440 | tf_op jit(solution)/shard_map/suffix_x/ppermute | solution.py:209
  20.7 0.8 %pad_add_fusion.scalars = s32[64]{0:T(128)S(1)} fusion(s32[16]{0:T(128)} %param.12, s32[16]{0:T(128)} %param.13, s32[16]{0:T(128)} %param.15, s32[16]{0:T(128)} %param.14), kind=kLoop, calls=%fused_computation.1 | loop fusion | flops 192 | bytes 512 | tf_op jit(solution)/shard_map/concatenate | solution.py:195
  21.5 0.0 copy-start.1
  21.5 0.6 token_rows.1
  22.1 0.0 copy-start
  22.1 6.5 %collective-permute-start.1 = (bf16[16,128]{1,0:T(8,128)(2,1)S(1)}, bf16[16,128]{1,0:T(8,128)(2,1)S(1)}, u32[]{:S(2)}, u32[]{:S(2)}) collective-permute-start(bf16[16,128]{1,0:T(8,128)(2,1)S(1)} %token_rows.1), channel_id=1, source_target_pairs={{0,20},{1,21},{2,22},{3,23},{4,16},{5,17},{6,18},{7,19},{8,28},{9,... | collective-permute-start | bytes 12296 | tf_op jit(solution)/shard_map/tokens_plane/ppermute | solution.py:184
  28.6 3.0 %collective-permute-done.1.tok_ref = bf16[16,128]{1,0:T(8,128)(2,1)S(1)} collective-permute-done((bf16[16,128]{1,0:T(8,128)(2,1)S(1)}, bf16[16,128]{1,0:T(8,128)(2,1)S(1)}, u32[]{:S(2)}, u32[]{:S(2)}) %collective-permute-start.1) | collective-permute-done | bytes 4128 | tf_op jit(solution)/shard_map/tokens_plane/ppermute | solution.py:184
  31.6 0.0 collective-permute-done
  31.6 0.0 copy-done.1
  31.7 1.9 %collective-permute-start.2 = (bf16[2064,128]{1,0:T(8,128)(2,1)S(1)}, bf16[2064,128]{1,0:T(8,128)(2,1)S(1)}, u32[]{:S(2)}, u32[]{:S(2)}) collective-permute-start(bf16[2064,128]{1,0:T(8,128)(2,1)S(1)} %pad_maximum_fusion.near), channel_id=1, source_target_pairs={{0,1},{1,0},{2,3},{3,2},{4,5},{5,4},{6,7},{7,6},{8,9},{9,8},{10,11... | collective-permute-start | bytes 1585160 | tf_op jit(solution)/shard_map/suffix_core/ppermute | solution.py:215
  33.6 1.9 %collective-permute-done.2.far = bf16[2064,128]{1,0:T(8,128)(2,1)S(1)} collective-permute-done((bf16[2064,128]{1,0:T(8,128)(2,1)S(1)}, bf16[2064,128]{1,0:T(8,128)(2,1)S(1)}, u32[]{:S(2)}, u32[]{:S(2)}) %collective-permute-start.2) | collective-permute-done | bytes 528416 | tf_op jit(solution)/shard_map/suffix_core/ppermute | solution.py:215
  35.5 0.2 all-to-all-done.q_ref
  35.7 0.0 copy-done
  35.7 4.9 %attend.1 = bf16[16,72,128]{2,1,0:T(8,128)(2,1)S(1)} custom-call(s32[64]{0:T(128)S(1)} %pad_add_fusion.scalars, bf16[16,64,128]{2,1,0:T(8,128)(2,1)S(1)} %all-to-all-done.q_ref, bf16[2,1024,8,128]{3,2,1,0:T(8,128)(2,1)} %kv_ref.1, bf16[2064,128]{1,0:T(8,128)(2,1)S(1)} %pad_maximum_fusion.near, bf16[2064,128]{1,0:T(8,128)(2,1)S(1)} %collective-permute-done.2.far, ...), custom_call_target="tpu_custom_call" | custom-call | flops 600000000 | bytes 6000000 | tf_op jit(solution)/shard_map/attend/pallas_call | solution.py:217
  40.6 27.0 %all_to_all.10.parts_ref = bf16[16,72,128]{2,1,0:T(8,128)(2,1)S(1)} all-to-all(bf16[16,72,128]{2,1,0:T(8,128)(2,1)S(1)} %attend.1), channel_id=1, replica_groups=mesh['ctx'=16,'beam'=32] {'ctx'}, dimensions={0} | all-to-all | bytes 589824 | tf_op jit(solution)/shard_map/parts_home/all_to_all | solution.py:239
  67.6 1.9 %combine.1 = (bf16[64,128]{1,0:T(8,128)(2,1)}, f32[1,16]{1,0:T(1,128)}) custom-call(s32[64]{0:T(128)S(1)} %pad_add_fusion.scalars, bf16[16,72,128]{2,1,0:T(8,128)(2,1)S(1)} %all_to_all.10.parts_ref), custom_call_target="tpu_custom_call" | custom-call | tf_op jit(solution)/shard_map/combine/pallas_call | solution.py:240
  (1 shorter events, 0.0 us)
Async XLA Ops:
  2.1 33.6 %all-to-all-start = ((bf16[16,64,128]{2,1,0:T(8,128)(2,1)}), bf16[16,64,128]{2,1,0:T(8,128)(2,1)S(1)}, u32[]{:S(2)}, u32[]{:S(2)}) async-start(bf16[16,64,128]{2,1,0:T(8,128)(2,1)} %broadcast_in_dim.8), calls=%async_computation | async-start | bytes 524288 | tf_op jit(solution)/shard_map/queries_to_all/all_to_all | solution.py:194
  17.3 14.3 %collective-permute-start = (bf16[1024,128]{1,0:T(8,128)(2,1)}, bf16[1024,128]{1,0:T(8,128)(2,1)S(1)}, u32[]{:S(2)}, u32[]{:S(2)}) collective-permute-start(bf16[1024,128]{1,0:T(8,128)(2,1)} %bitcast.6), channel_id=1, source_target_pairs={{0,2},{1,3},{2,0},{3,1},{4,6},{5,7},{6,4},{7,5},{8,10},{9,11},{10,... | collective-permute-start | bytes 786440 | tf_op jit(solution)/shard_map/suffix_x/ppermute | solution.py:209
  21.5 10.1 %copy-start.1 = (bf16[2,16,4,8,128]{4,3,2,1,0:T(8,128)(2,1)S(1)}, bf16[2,16,4,8,128]{4,3,2,1,0:T(8,128)(2,1)}, u32[]{:S(2)}) copy-start(bf16[2,16,4,8,128]{4,3,2,1,0:T(8,128)(2,1)} %param.10) | copy-start | bytes 786436
  22.1 13.6 %copy-start = (bf16[2,16,8,128]{3,2,1,0:T(8,128)(2,1)S(1)}, bf16[2,16,8,128]{3,2,1,0:T(8,128)(2,1)}, u32[]{:S(2)}) copy-start(bf16[2,16,8,128]{3,2,1,0:T(8,128)(2,1)} %param.11) | copy-start | bytes 196612
  22.1 9.5 %collective-permute-start.1 = (bf16[16,128]{1,0:T(8,128)(2,1)S(1)}, bf16[16,128]{1,0:T(8,128)(2,1)S(1)}, u32[]{:S(2)}, u32[]{:S(2)}) collective-permute-start(bf16[16,128]{1,0:T(8,128)(2,1)S(1)} %token_rows.1), channel_id=1, source_target_pairs={{0,20},{1,21},{2,22},{3,23},{4,16},{5,17},{6,18},{7,19},{8,28},{9,... | collective-permute-start | bytes 12296 | tf_op jit(solution)/shard_map/tokens_plane/ppermute | solution.py:184
  31.7 3.8 %collective-permute-start.2 = (bf16[2064,128]{1,0:T(8,128)(2,1)S(1)}, bf16[2064,128]{1,0:T(8,128)(2,1)S(1)}, u32[]{:S(2)}, u32[]{:S(2)}) collective-permute-start(bf16[2064,128]{1,0:T(8,128)(2,1)S(1)} %pad_maximum_fusion.near), channel_id=1, source_target_pairs={{0,1},{1,0},{2,3},{3,2},{4,5},{5,4},{6,7},{7,6},{8,9},{9,8},{10,11... | collective-permute-start | bytes 1585160 | tf_op jit(solution)/shard_map/suffix_core/ppermute | solution.py:215

commit v7 on v6

--- a/solution.py
+++ b/solution.py
@@ -154,7 +154,7 @@
     extra = parts_ref[:, 64 : 64 + EXTRA].astype(jnp.float32)
     logs = extra[:, 0] + extra[:, 1] + extra[:, 2]
     weights = jnp.exp(logs - jnp.max(logs, axis=0, keepdims=True))
-    weights = weights / jnp.sum(weights, axis=0, keepdims=True)
+    weights = weights * (1.0 / jnp.sum(weights, axis=0, keepdims=True))
     weights = jnp.where(z % 2 == 1, pltpu.roll(weights, 64, 1), weights)
     by_row = weights.T[0:64]
     mixed = jnp.zeros((64, HD), jnp.float32)
@@ -165,15 +165,16 @@
     all_tokens = extra[:, 3] * 65536.0 + extra[:, 4] * 256.0 + extra[:, 5]
     all_groups = extra[:, 6]
     used = lax.broadcasted_iota(jnp.int32, (16, 128), 1) < 32
-    beam = lax.broadcasted_iota(jnp.int32, (16, 128), 0)
-    counts = jnp.zeros((16, 128), jnp.float32)
+    all_groups = jnp.where(used, all_groups, 1e9)
+    lane = lax.broadcasted_iota(jnp.int32, (1, 128), 1)
+    counts = jnp.zeros((1, 128), jnp.float32)
     for b in range(16):
         token = scalars[b].astype(jnp.float32)
         group = scalars[16 + b].astype(jnp.float32)
-        same = used & (all_tokens == token) & (all_groups < group)
-        count = jnp.sum(jnp.where(same, PENALTY_WEIGHT, 0.0), axis=0, keepdims=True)
-        counts = jnp.where(beam == b, count, counts)
-    penalty_ref[...] = jnp.sum(counts.T, axis=0, keepdims=True)
+        same = (all_tokens == token) & (all_groups < group)
+        count = jnp.sum(jnp.where(same, PENALTY_WEIGHT, 0.0))
+        counts = jnp.where(lane == b, count, counts)
+    penalty_ref[...] = counts[:, 0:16]
 
 
 TOKENS_FROM = (10, 9, 11, 6, 15, 7, 5, 12, 0, 1, 3, 4, 13, 8, 2, 14)

time: 70 us -> 69.8 us (level)
  no operation moved by 1% of the time
where the time goes in v7:
time: 69.8 us; the launch traced here: 69.3 us
  starting transfers between devices  27 us (39%)
  blocking collectives  27 us (39%)
  Pallas kernels  7.24 us (10%)
  waiting for transfers between devices  5.1 us (7%)
  local copies, waits for them, and re-layouts  1.48 us (2%)
  other arithmetic  0.82 us (1%)
    all_to_all x1, blocking collectives, body(): parts = lax.all_to_all(parts, 'ctx', 0, 0, tiled=True)  27 us
    all_to_all x1, starting transfers between devices, body(): everyone = lax.all_to_all(sent, 'ctx', 0, 0, tiled=True)  15.2 us
    ppermute x1, starting transfers between devices, within_plane(): return lax.ppermute(block, ('ctx', 'beam'), pairs)  6.5 us
    pallas_call x1, Pallas kernels, body(): pl.pallas_call(attend_kernel, out_shape=jax.ShapeDtypeStruct((16, 64 + EX...  4.94 us
    ppermute x1, starting transfers between devices, body(): across = lax.ppermute(suffix, 'beam', [(i, i ^ 2) for i in range(32)])  3.4 us
    ppermute x1, waiting for transfers between devices, within_plane(): return lax.ppermute(block, ('ctx', 'beam'), pairs)  3.03 us
    ppermute x1, starting transfers between devices, body(): far = lax.ppermute(near, 'beam', [(i, i ^ 1) for i in range(32)])  1.92 us
    ppermute x1, waiting for transfers between devices, body(): far = lax.ppermute(near, 'beam', [(i, i ^ 1) for i in range(32)])  1.88 us
  transfers between devices with their start and end apart: 4, of which 3 were waited for; matrix products, arithmetic and copies ran while one was open for 1% of the time, Pallas kernels for 1%

profile of v7, /device:TPU:8, one launch (start us, length us, event | category | flops | bytes accessed | tf_op | source)
XLA Modules:
  0.0 69.3 jit_solution(5462094103176306224)
XLA Ops:
  0.6 1.5 %broadcast_in_dim.8 = bf16[16,64,128]{2,1,0:T(8,128)(2,1)} broadcast(bf16[64,128]{1,0:T(8,128)(2,1)} %bitcast.8), dimensions={1,2} | broadcast | bytes 278528 | tf_op jit(solution)/shard_map/queries_to_all/broadcast_in_dim | solution.py:194
  2.1 15.2 %all-to-all-start = ((bf16[16,64,128]{2,1,0:T(8,128)(2,1)}), bf16[16,64,128]{2,1,0:T(8,128)(2,1)S(1)}, u32[]{:S(2)}, u32[]{:S(2)}) async-start(bf16[16,64,128]{2,1,0:T(8,128)(2,1)} %broadcast_in_dim.8), calls=%async_computation | async-start | bytes 524288 | tf_op jit(solution)/shard_map/queries_to_all/all_to_all | solution.py:195
  17.3 3.4 %collective-permute-start = (bf16[1024,128]{1,0:T(8,128)(2,1)}, bf16[1024,128]{1,0:T(8,128)(2,1)S(1)}, u32[]{:S(2)}, u32[]{:S(2)}) collective-permute-start(bf16[1024,128]{1,0:T(8,128)(2,1)} %bitcast.6), channel_id=1, source_target_pairs={{0,2},{1,3},{2,0},{3,1},{4,6},{5,7},{6,4},{7,5},{8,10},{9,11},{10,... | collective-permute-start | bytes 786440 | tf_op jit(solution)/shard_map/suffix_x/ppermute | solution.py:210
  20.7 0.8 %pad_add_fusion.scalars = s32[64]{0:T(128)S(1)} fusion(s32[16]{0:T(128)} %param.12, s32[16]{0:T(128)} %param.13, s32[16]{0:T(128)} %param.15, s32[16]{0:T(128)} %param.14), kind=kLoop, calls=%fused_computation.1 | loop fusion | flops 192 | bytes 512 | tf_op jit(solution)/shard_map/concatenate | solution.py:196
  21.5 0.0 copy-start.1
  21.5 0.6 token_rows.1
  22.1 0.0 copy-start
  22.1 6.5 %collective-permute-start.1 = (bf16[16,128]{1,0:T(8,128)(2,1)S(1)}, bf16[16,128]{1,0:T(8,128)(2,1)S(1)}, u32[]{:S(2)}, u32[]{:S(2)}) collective-permute-start(bf16[16,128]{1,0:T(8,128)(2,1)S(1)} %token_rows.1), channel_id=1, source_target_pairs={{0,20},{1,21},{2,22},{3,23},{4,16},{5,17},{6,18},{7,19},{8,28},{9,... | collective-permute-start | bytes 12296 | tf_op jit(solution)/shard_map/tokens_plane/ppermute | solution.py:185
  28.6 3.0 %collective-permute-done.1.tok_ref = bf16[16,128]{1,0:T(8,128)(2,1)S(1)} collective-permute-done((bf16[16,128]{1,0:T(8,128)(2,1)S(1)}, bf16[16,128]{1,0:T(8,128)(2,1)S(1)}, u32[]{:S(2)}, u32[]{:S(2)}) %collective-permute-start.1) | collective-permute-done | bytes 4128 | tf_op jit(solution)/shard_map/tokens_plane/ppermute | solution.py:185
  31.6 0.0 collective-permute-done
  31.6 0.0 copy-done.1
  31.7 1.9 %collective-permute-start.2 = (bf16[2064,128]{1,0:T(8,128)(2,1)S(1)}, bf16[2064,128]{1,0:T(8,128)(2,1)S(1)}, u32[]{:S(2)}, u32[]{:S(2)}) collective-permute-start(bf16[2064,128]{1,0:T(8,128)(2,1)S(1)} %pad_maximum_fusion.near), channel_id=1, source_target_pairs={{0,1},{1,0},{2,3},{3,2},{4,5},{5,4},{6,7},{7,6},{8,9},{9,8},{10,11... | collective-permute-start | bytes 1585160 | tf_op jit(solution)/shard_map/suffix_core/ppermute | solution.py:216
  33.6 1.9 %collective-permute-done.2.far = bf16[2064,128]{1,0:T(8,128)(2,1)S(1)} collective-permute-done((bf16[2064,128]{1,0:T(8,128)(2,1)S(1)}, bf16[2064,128]{1,0:T(8,128)(2,1)S(1)}, u32[]{:S(2)}, u32[]{:S(2)}) %collective-permute-start.2) | collective-permute-done | bytes 528416 | tf_op jit(solution)/shard_map/suffix_core/ppermute | solution.py:216
  35.5 0.2 all-to-all-done.q_ref
  35.7 0.0 copy-done
  35.7 4.9 %attend.1 = bf16[16,72,128]{2,1,0:T(8,128)(2,1)S(1)} custom-call(s32[64]{0:T(128)S(1)} %pad_add_fusion.scalars, bf16[16,64,128]{2,1,0:T(8,128)(2,1)S(1)} %all-to-all-done.q_ref, bf16[2,1024,8,128]{3,2,1,0:T(8,128)(2,1)} %kv_ref.1, bf16[2064,128]{1,0:T(8,128)(2,1)S(1)} %pad_maximum_fusion.near, bf16[2064,128]{1,0:T(8,128)(2,1)S(1)} %collective-permute-done.2.far, ...), custom_call_target="tpu_custom_call" | custom-call | flops 600000000 | bytes 6000000 | tf_op jit(solution)/shard_map/attend/pallas_call | solution.py:218
  40.6 27.0 %all_to_all.10.parts_ref = bf16[16,72,128]{2,1,0:T(8,128)(2,1)S(1)} all-to-all(bf16[16,72,128]{2,1,0:T(8,128)(2,1)S(1)} %attend.1), channel_id=1, replica_groups=mesh['ctx'=16,'beam'=32] {'ctx'}, dimensions={0} | all-to-all | bytes 589824 | tf_op jit(solution)/shard_map/parts_home/all_to_all | solution.py:240
  67.6 1.7 %combine.1 = (bf16[64,128]{1,0:T(8,128)(2,1)}, f32[1,16]{1,0:T(1,128)}) custom-call(s32[64]{0:T(128)S(1)} %pad_add_fusion.scalars, bf16[16,72,128]{2,1,0:T(8,128)(2,1)S(1)} %all_to_all.10.parts_ref), custom_call_target="tpu_custom_call" | custom-call | tf_op jit(solution)/shard_map/combine/pallas_call | solution.py:241
  (1 shorter events, 0.0 us)
Async XLA Ops:
  2.1 33.6 %all-to-all-start = ((bf16[16,64,128]{2,1,0:T(8,128)(2,1)}), bf16[16,64,128]{2,1,0:T(8,128)(2,1)S(1)}, u32[]{:S(2)}, u32[]{:S(2)}) async-start(bf16[16,64,128]{2,1,0:T(8,128)(2,1)} %broadcast_in_dim.8), calls=%async_computation | async-start | bytes 524288 | tf_op jit(solution)/shard_map/queries_to_all/all_to_all | solution.py:195
  17.3 14.3 %collective-permute-start = (bf16[1024,128]{1,0:T(8,128)(2,1)}, bf16[1024,128]{1,0:T(8,128)(2,1)S(1)}, u32[]{:S(2)}, u32[]{:S(2)}) collective-permute-start(bf16[1024,128]{1,0:T(8,128)(2,1)} %bitcast.6), channel_id=1, source_target_pairs={{0,2},{1,3},{2,0},{3,1},{4,6},{5,7},{6,4},{7,5},{8,10},{9,11},{10,... | collective-permute-start | bytes 786440 | tf_op jit(solution)/shard_map/suffix_x/ppermute | solution.py:210
  21.5 10.1 %copy-start.1 = (bf16[2,16,4,8,128]{4,3,2,1,0:T(8,128)(2,1)S(1)}, bf16[2,16,4,8,128]{4,3,2,1,0:T(8,128)(2,1)}, u32[]{:S(2)}) copy-start(bf16[2,16,4,8,128]{4,3,2,1,0:T(8,128)(2,1)} %param.10) | copy-start | bytes 786436
  22.1 13.6 %copy-start = (bf16[2,16,8,128]{3,2,1,0:T(8,128)(2,1)S(1)}, bf16[2,16,8,128]{3,2,1,0:T(8,128)(2,1)}, u32[]{:S(2)}) copy-start(bf16[2,16,8,128]{3,2,1,0:T(8,128)(2,1)} %param.11) | copy-start | bytes 196612
  22.1 9.5 %collective-permute-start.1 = (bf16[16,128]{1,0:T(8,128)(2,1)S(1)}, bf16[16,128]{1,0:T(8,128)(2,1)S(1)}, u32[]{:S(2)}, u32[]{:S(2)}) collective-permute-start(bf16[16,128]{1,0:T(8,128)(2,1)S(1)} %token_rows.1), channel_id=1, source_target_pairs={{0,20},{1,21},{2,22},{3,23},{4,16},{5,17},{6,18},{7,19},{8,28},{9,... | collective-permute-start | bytes 12296 | tf_op jit(solution)/shard_map/tokens_plane/ppermute | solution.py:185
  31.7 3.8 %collective-permute-start.2 = (bf16[2064,128]{1,0:T(8,128)(2,1)S(1)}, bf16[2064,128]{1,0:T(8,128)(2,1)S(1)}, u32[]{:S(2)}, u32[]{:S(2)}) collective-permute-start(bf16[2064,128]{1,0:T(8,128)(2,1)S(1)} %pad_maximum_fusion.near), channel_id=1, source_target_pairs={{0,1},{1,0},{2,3},{3,2},{4,5},{5,4},{6,7},{7,6},{8,9},{9,8},{10,11... | collective-permute-start | bytes 1585160 | tf_op jit(solution)/shard_map/suffix_core/ppermute | solution.py:216

commit v8 on v7

--- a/solution.py
+++ b/solution.py
@@ -157,9 +157,14 @@
     weights = weights * (1.0 / jnp.sum(weights, axis=0, keepdims=True))
     weights = jnp.where(z % 2 == 1, pltpu.roll(weights, 64, 1), weights)
     by_row = weights.T[0:64]
-    mixed = jnp.zeros((64, HD), jnp.float32)
-    for source in range(16):
-        mixed = mixed + by_row[:, source : source + 1] * parts_ref[source, 0:64].astype(jnp.float32)
+    halves = []
+    for first in (0, 8):
+        half = jnp.zeros((64, HD), jnp.float32)
+        for source in range(first, first + 8):
+            part = parts_ref[source, 0:64].astype(jnp.float32)
+            half = half + by_row[:, source : source + 1] * part
+        halves.append(half)
+    mixed = halves[0] + halves[1]
     out_ref[...] = mixed.astype(jnp.bfloat16)
 
     all_tokens = extra[:, 3] * 65536.0 + extra[:, 4] * 256.0 + extra[:, 5]

time: 69.8 us -> 69.8 us (level)
  no operation moved by 1% of the time
where the time goes in v8:
time: 69.8 us; the launch traced here: 69.4 us
  starting transfers between devices  27 us (39%)
  blocking collectives  27 us (39%)
  Pallas kernels  7.24 us (10%)
  waiting for transfers between devices  5.1 us (7%)
  local copies, waits for them, and re-layouts  1.48 us (2%)
  other arithmetic  0.82 us (1%)
    all_to_all x1, blocking collectives, body(): parts = lax.all_to_all(parts, 'ctx', 0, 0, tiled=True)  27 us
    all_to_all x1, starting transfers between devices, body(): everyone = lax.all_to_all(sent, 'ctx', 0, 0, tiled=True)  15.2 us
    ppermute x1, starting transfers between devices, within_plane(): return lax.ppermute(block, ('ctx', 'beam'), pairs)  6.5 us
    pallas_call x1, Pallas kernels, body(): pl.pallas_call(attend_kernel, out_shape=jax.ShapeDtypeStruct((16, 64 + EX...  4.94 us
    ppermute x1, starting transfers between devices, body(): across = lax.ppermute(suffix, 'beam', [(i, i ^ 2) for i in range(32)])  3.4 us
    ppermute x1, waiting for transfers between devices, within_plane(): return lax.ppermute(block, ('ctx', 'beam'), pairs)  3.03 us
    ppermute x1, starting transfers between devices, body(): far = lax.ppermute(near, 'beam', [(i, i ^ 1) for i in range(32)])  1.92 us
    ppermute x1, waiting for transfers between devices, body(): far = lax.ppermute(near, 'beam', [(i, i ^ 1) for i in range(32)])  1.88 us
  transfers between devices with their start and end apart: 4, of which 3 were waited for; matrix products, arithmetic and copies ran while one was open for 1% of the time, Pallas kernels for 1%

profile of v8, /device:TPU:8, one launch (start us, length us, event | category | flops | bytes accessed | tf_op | source)
XLA Modules:
  0.0 69.4 jit_solution(1460553797268523782)
XLA Ops:
  0.6 1.5 %broadcast_in_dim.8 = bf16[16,64,128]{2,1,0:T(8,128)(2,1)} broadcast(bf16[64,128]{1,0:T(8,128)(2,1)} %bitcast.8), dimensions={1,2} | broadcast | bytes 278528 | tf_op jit(solution)/shard_map/queries_to_all/broadcast_in_dim | solution.py:199
  2.1 15.2 %all-to-all-start = ((bf16[16,64,128]{2,1,0:T(8,128)(2,1)}), bf16[16,64,128]{2,1,0:T(8,128)(2,1)S(1)}, u32[]{:S(2)}, u32[]{:S(2)}) async-start(bf16[16,64,128]{2,1,0:T(8,128)(2,1)} %broadcast_in_dim.8), calls=%async_computation | async-start | bytes 524288 | tf_op jit(solution)/shard_map/queries_to_all/all_to_all | solution.py:200
  17.3 3.4 %collective-permute-start = (bf16[1024,128]{1,0:T(8,128)(2,1)}, bf16[1024,128]{1,0:T(8,128)(2,1)S(1)}, u32[]{:S(2)}, u32[]{:S(2)}) collective-permute-start(bf16[1024,128]{1,0:T(8,128)(2,1)} %bitcast.6), channel_id=1, source_target_pairs={{0,2},{1,3},{2,0},{3,1},{4,6},{5,7},{6,4},{7,5},{8,10},{9,11},{10,... | collective-permute-start | bytes 786440 | tf_op jit(solution)/shard_map/suffix_x/ppermute | solution.py:215
  20.7 0.8 %pad_add_fusion.scalars = s32[64]{0:T(128)S(1)} fusion(s32[16]{0:T(128)} %param.12, s32[16]{0:T(128)} %param.13, s32[16]{0:T(128)} %param.15, s32[16]{0:T(128)} %param.14), kind=kLoop, calls=%fused_computation.1 | loop fusion | flops 192 | bytes 512 | tf_op jit(solution)/shard_map/concatenate | solution.py:201
  21.5 0.0 copy-start.1
  21.5 0.6 token_rows.1
  22.1 0.0 copy-start
  22.1 6.5 %collective-permute-start.1 = (bf16[16,128]{1,0:T(8,128)(2,1)S(1)}, bf16[16,128]{1,0:T(8,128)(2,1)S(1)}, u32[]{:S(2)}, u32[]{:S(2)}) collective-permute-start(bf16[16,128]{1,0:T(8,128)(2,1)S(1)} %token_rows.1), channel_id=1, source_target_pairs={{0,20},{1,21},{2,22},{3,23},{4,16},{5,17},{6,18},{7,19},{8,28},{9,... | collective-permute-start | bytes 12296 | tf_op jit(solution)/shard_map/tokens_plane/ppermute | solution.py:190
  28.6 3.0 %collective-permute-done.1.tok_ref = bf16[16,128]{1,0:T(8,128)(2,1)S(1)} collective-permute-done((bf16[16,128]{1,0:T(8,128)(2,1)S(1)}, bf16[16,128]{1,0:T(8,128)(2,1)S(1)}, u32[]{:S(2)}, u32[]{:S(2)}) %collective-permute-start.1) | collective-permute-done | bytes 4128 | tf_op jit(solution)/shard_map/tokens_plane/ppermute | solution.py:190
  31.6 0.0 collective-permute-done
  31.6 0.0 copy-done.1
  31.7 1.9 %collective-permute-start.2 = (bf16[2064,128]{1,0:T(8,128)(2,1)S(1)}, bf16[2064,128]{1,0:T(8,128)(2,1)S(1)}, u32[]{:S(2)}, u32[]{:S(2)}) collective-permute-start(bf16[2064,128]{1,0:T(8,128)(2,1)S(1)} %pad_maximum_fusion.near), channel_id=1, source_target_pairs={{0,1},{1,0},{2,3},{3,2},{4,5},{5,4},{6,7},{7,6},{8,9},{9,8},{10,11... | collective-permute-start | bytes 1585160 | tf_op jit(solution)/shard_map/suffix_core/ppermute | solution.py:221
  33.6 1.9 %collective-permute-done.2.far = bf16[2064,128]{1,0:T(8,128)(2,1)S(1)} collective-permute-done((bf16[2064,128]{1,0:T(8,128)(2,1)S(1)}, bf16[2064,128]{1,0:T(8,128)(2,1)S(1)}, u32[]{:S(2)}, u32[]{:S(2)}) %collective-permute-start.2) | collective-permute-done | bytes 528416 | tf_op jit(solution)/shard_map/suffix_core/ppermute | solution.py:221
  35.5 0.2 all-to-all-done.q_ref
  35.7 0.0 copy-done
  35.7 4.9 %attend.1 = bf16[16,72,128]{2,1,0:T(8,128)(2,1)S(1)} custom-call(s32[64]{0:T(128)S(1)} %pad_add_fusion.scalars, bf16[16,64,128]{2,1,0:T(8,128)(2,1)S(1)} %all-to-all-done.q_ref, bf16[2,1024,8,128]{3,2,1,0:T(8,128)(2,1)} %kv_ref.1, bf16[2064,128]{1,0:T(8,128)(2,1)S(1)} %pad_maximum_fusion.near, bf16[2064,128]{1,0:T(8,128)(2,1)S(1)} %collective-permute-done.2.far, ...), custom_call_target="tpu_custom_call" | custom-call | flops 600000000 | bytes 6000000 | tf_op jit(solution)/shard_map/attend/pallas_call | solution.py:223
  40.6 27.0 %all_to_all.10.parts_ref = bf16[16,72,128]{2,1,0:T(8,128)(2,1)S(1)} all-to-all(bf16[16,72,128]{2,1,0:T(8,128)(2,1)S(1)} %attend.1), channel_id=1, replica_groups=mesh['ctx'=16,'beam'=32] {'ctx'}, dimensions={0} | all-to-all | bytes 589824 | tf_op jit(solution)/shard_map/parts_home/all_to_all | solution.py:245
  67.6 1.7 %combine.1 = (bf16[64,128]{1,0:T(8,128)(2,1)}, f32[1,16]{1,0:T(1,128)}) custom-call(s32[64]{0:T(128)S(1)} %pad_add_fusion.scalars, bf16[16,72,128]{2,1,0:T(8,128)(2,1)S(1)} %all_to_all.10.parts_ref), custom_call_target="tpu_custom_call" | custom-call | tf_op jit(solution)/shard_map/combine/pallas_call | solution.py:246
  (1 shorter events, 0.0 us)
Async XLA Ops:
  2.1 33.6 %all-to-all-start = ((bf16[16,64,128]{2,1,0:T(8,128)(2,1)}), bf16[16,64,128]{2,1,0:T(8,128)(2,1)S(1)}, u32[]{:S(2)}, u32[]{:S(2)}) async-start(bf16[16,64,128]{2,1,0:T(8,128)(2,1)} %broadcast_in_dim.8), calls=%async_computation | async-start | bytes 524288 | tf_op jit(solution)/shard_map/queries_to_all/all_to_all | solution.py:200
  17.3 14.3 %collective-permute-start = (bf16[1024,128]{1,0:T(8,128)(2,1)}, bf16[1024,128]{1,0:T(8,128)(2,1)S(1)}, u32[]{:S(2)}, u32[]{:S(2)}) collective-permute-start(bf16[1024,128]{1,0:T(8,128)(2,1)} %bitcast.6), channel_id=1, source_target_pairs={{0,2},{1,3},{2,0},{3,1},{4,6},{5,7},{6,4},{7,5},{8,10},{9,11},{10,... | collective-permute-start | bytes 786440 | tf_op jit(solution)/shard_map/suffix_x/ppermute | solution.py:215
  21.5 10.1 %copy-start.1 = (bf16[2,16,4,8,128]{4,3,2,1,0:T(8,128)(2,1)S(1)}, bf16[2,16,4,8,128]{4,3,2,1,0:T(8,128)(2,1)}, u32[]{:S(2)}) copy-start(bf16[2,16,4,8,128]{4,3,2,1,0:T(8,128)(2,1)} %param.10) | copy-start | bytes 786436
  22.1 13.6 %copy-start = (bf16[2,16,8,128]{3,2,1,0:T(8,128)(2,1)S(1)}, bf16[2,16,8,128]{3,2,1,0:T(8,128)(2,1)}, u32[]{:S(2)}) copy-start(bf16[2,16,8,128]{3,2,1,0:T(8,128)(2,1)} %param.11) | copy-start | bytes 196612
  22.1 9.5 %collective-permute-start.1 = (bf16[16,128]{1,0:T(8,128)(2,1)S(1)}, bf16[16,128]{1,0:T(8,128)(2,1)S(1)}, u32[]{:S(2)}, u32[]{:S(2)}) collective-permute-start(bf16[16,128]{1,0:T(8,128)(2,1)S(1)} %token_rows.1), channel_id=1, source_target_pairs={{0,20},{1,21},{2,22},{3,23},{4,16},{5,17},{6,18},{7,19},{8,28},{9,... | collective-permute-start | bytes 12296 | tf_op jit(solution)/shard_map/tokens_plane/ppermute | solution.py:190
  31.7 3.8 %collective-permute-start.2 = (bf16[2064,128]{1,0:T(8,128)(2,1)S(1)}, bf16[2064,128]{1,0:T(8,128)(2,1)S(1)}, u32[]{:S(2)}, u32[]{:S(2)}) collective-permute-start(bf16[2064,128]{1,0:T(8,128)(2,1)S(1)} %pad_maximum_fusion.near), channel_id=1, source_target_pairs={{0,1},{1,0},{2,3},{3,2},{4,5},{5,4},{6,7},{7,6},{8,9},{9,8},{10,11... | collective-permute-start | bytes 1585160 | tf_op jit(solution)/shard_map/suffix_core/ppermute | solution.py:221
